TPU v7x, 128 devices: a whole 4x4x4 slice. The times are simulated.
128 devices in a mesh: dp: 8 (over x, z_hi), tensor: 16 (over y, z_lo, core).
Axes of the slice: x: 4, y: 4, z: 4 (z_hi: 2, z_lo: 2; z = z_hi * 2 + z_lo), core: 2. Of those that a mesh axis runs over, the one named last changes fastest.
Arguments:
- tokens: bfloat16 [16384, 1024], P(('dp', 'tensor')), may hold values from -6 to 6
- w_qkv: bfloat16 [1024, 16, 192], P(None, 'tensor'), may hold values from -0.25 to 0.25
- b_qkv: bfloat16 [16, 192], P('tensor'), may hold values from -2 to 2
- w_out: bfloat16 [16, 64, 1024], P('tensor'), may hold values from -0.75 to 0.75
- w_up: bfloat16 [1024, 4096], P(None, 'tensor'), may hold values from -0.1875 to 0.1875
- b_up: bfloat16 [4096], P('tensor'), may hold values from -3 to 3
- w_down: bfloat16 [4096, 1024], P('tensor'), may hold values from -0.09375 to 0.09375
- out_bias: bfloat16 [1024], replicated, may hold values from -2 to 2
- ln1_gain: bfloat16 [1024], replicated, may hold values from 0.5 to 1.5
- ln1_shift: bfloat16 [1024], replicated, may hold values from -2 to 2
- ln2_gain: bfloat16 [1024], replicated, may hold values from 0.5 to 1.5
- ln2_shift: bfloat16 [1024], replicated, may hold values from -2 to 2
- cotangent: bfloat16 [16384, 1024], P(('dp', 'tensor')), may hold values from -6 to 6
Outputs:
- layer_out: bfloat16 [16384, 1024], P(('dp', 'tensor'))
- input_grad: bfloat16 [16384, 1024], P(('dp', 'tensor'))
- grad_w_qkv: float32 [1024, 16, 192], P(None, 'tensor')
- grad_b_qkv: float32 [16, 192], P('tensor')
- grad_w_out: float32 [16, 64, 1024], P('tensor')
- grad_w_up: float32 [1024, 4096], P(None, 'tensor')
- grad_b_up: float32 [4096], P('tensor')
- grad_w_down: float32 [4096, 1024], P('tensor')
- grad_out_bias: float32 [1024], replicated
- grad_ln1_gain: float32 [1024], replicated
- grad_ln1_shift: float32 [1024], replicated
- grad_ln2_gain: float32 [1024], replicated
- grad_ln2_shift: float32 [1024], replicated
All inputs are finite; a program needn't handle non-finite values.
Results may differ from a plain program's by a relative error of at most 0.019.
The roundings to bfloat16 on the way count: a program that leaves them out, or rounds other values in their place, can miss the bound.
Values may be sent and summed in bfloat16 or wider, within the bound.
No kernel may reach another device: no remote copies, remote signals or barrier semaphores. Data moves between devices by JAX's collectives and lax.ppermute only.
A program may use at most 128 MiB of HBM per device.

v0:
```python
from functools import partial

import jax
import jax.numpy as jnp
from jax import lax
from jax.sharding import PartitionSpec as P

ROT = 16
LEN = 2048


EPS = 1e-05


def together(arrays, axis):
    ends = [0]
    for a in arrays:
        ends.append(ends[-1] + a.size)
    running = lax.psum(jnp.concatenate([a.ravel() for a in arrays]), axis)
    return tuple((running[b:e].reshape(a.shape) for a, b, e in zip(arrays, ends, ends[1:])))


def normalize(values):
    center = values - jnp.mean(values, axis=-1, keepdims=True)
    inverse = lax.rsqrt(jnp.mean(center * center, axis=-1, keepdims=True) + EPS)
    return (center * inverse, inverse)


def norm_back(scaled, normalized, inverse):
    centered = scaled - jnp.mean(scaled, axis=-1, keepdims=True)
    return inverse * (centered - normalized * jnp.mean(scaled * normalized, axis=-1, keepdims=True))


def rotary_tables(length, rotary):
    places = jnp.arange(length, dtype=jnp.float32)
    inverse = 10000.0 ** (-2.0 * jnp.arange(rotary // 2, dtype=jnp.float32) / rotary)
    angles = places[:, None] * inverse[None, :]
    return (jnp.cos(angles)[:, None, :], jnp.sin(angles)[:, None, :])


def rotate(values, cosine, sine, rotary):
    half = rotary // 2
    first = values[..., :half]
    second = values[..., half:rotary]
    return jnp.concatenate(
        [first * cosine - second * sine, second * cosine + first * sine, values[..., rotary:]],
        axis=-1,
    )


def block_scores(query_rows, keys_all, start, scale):
    block = query_rows.shape[0]
    scores = (
        jnp.einsum("bhe,the->hbt", query_rows, keys_all, preferred_element_type=jnp.float32) * scale
    )
    places = start + jnp.arange(block, dtype=jnp.int32)
    key_places = jnp.arange(keys_all.shape[0], dtype=jnp.int32)
    return jnp.where(places[:, None] >= key_places[None, :], scores, -1e30)


def attend_forward(queries, keys_all, values_all, scale):
    length = queries.shape[0]
    block = min(512, length)
    count = length // block

    def one_block(index):
        start = index * block
        query_rows = lax.dynamic_slice_in_dim(queries, start, block, 0)
        scores = block_scores(query_rows, keys_all, start, scale)
        top = jnp.max(scores, axis=-1, keepdims=True)
        expo = jnp.exp(scores - top)
        mass = jnp.sum(expo, axis=-1, keepdims=True)
        weights = (expo / mass).astype(jnp.bfloat16)
        context = jnp.einsum(
            "hbt,the->bhe", weights, values_all, preferred_element_type=jnp.float32
        )
        return (context.astype(jnp.bfloat16), (top + jnp.log(mass))[..., 0])

    contexts, log_mass = lax.map(one_block, jnp.arange(count, dtype=jnp.int32))
    return (contexts.reshape(length, queries.shape[1], queries.shape[2]), log_mass)


def attend_backward(queries, keys_all, values_all, grad_context, log_mass, scale):
    length = queries.shape[0]
    block = min(512, length)
    count = length // block

    def one_block(carry, index):
        grad_keys, grad_values = carry
        start = index * block
        query_rows = lax.dynamic_slice_in_dim(queries, start, block, 0)
        grad_rows = lax.dynamic_slice_in_dim(grad_context, start, block, 0)
        scores = block_scores(query_rows, keys_all, start, scale)
        weights = jnp.exp(scores - log_mass[index][..., None])
        grad_values = grad_values + jnp.einsum(
            "hbt,bhe->the",
            weights.astype(jnp.bfloat16),
            grad_rows,
            preferred_element_type=jnp.float32,
        )
        grad_weights = jnp.einsum(
            "bhe,the->hbt", grad_rows, values_all, preferred_element_type=jnp.float32
        )
        inner = jnp.sum(weights * grad_weights, axis=-1, keepdims=True)
        grad_scores = (weights * (grad_weights - inner)).astype(jnp.bfloat16)
        grad_query = (
            jnp.einsum("hbt,the->bhe", grad_scores, keys_all, preferred_element_type=jnp.float32)
            * scale
        )
        grad_keys = (
            grad_keys
            + jnp.einsum(
                "hbt,bhe->the", grad_scores, query_rows, preferred_element_type=jnp.float32
            )
            * scale
        )
        return ((grad_keys, grad_values), grad_query)

    empty = jnp.zeros(keys_all.shape, jnp.float32)
    (grad_keys, grad_values), grad_queries = lax.scan(
        one_block, (empty, empty), jnp.arange(count, dtype=jnp.int32)
    )
    return (grad_queries.reshape(queries.shape), grad_keys, grad_values)


def per_device(
    tokens,
    w_qkv,
    b_qkv,
    w_out,
    w_up,
    b_up,
    w_down,
    out_bias,
    ln1_gain,
    ln1_shift,
    ln2_gain,
    ln2_shift,
    cotangent,
):
    local_rows = tokens.astype(jnp.float32)
    share = local_rows.shape[0]
    gain_one = ln1_gain.astype(jnp.float32)
    gain_two = ln2_gain.astype(jnp.float32)
    shift_one = ln1_shift.astype(jnp.float32)
    shift_two = ln2_shift.astype(jnp.float32)
    rows_all = lax.all_gather(tokens, "tensor", axis=0, tiled=True).astype(jnp.float32)
    normalized_all, inverse_all = normalize(rows_all)
    first_all = (normalized_all * gain_one + shift_one).astype(jnp.bfloat16)
    second_all = (normalized_all * gain_two + shift_two).astype(jnp.bfloat16)
    offset = lax.axis_index("tensor") * share
    normalized = lax.dynamic_slice_in_dim(normalized_all, offset, share, 0)
    inverse = lax.dynamic_slice_in_dim(inverse_all, offset, share, 0)
    token_count = first_all.shape[0]
    sequences = token_count // LEN
    heads_here = w_qkv.shape[1]
    head_size = w_qkv.shape[2] // 3
    scale = head_size ** (-0.5)
    cosine, sine = rotary_tables(LEN, ROT)
    projected = jnp.einsum(
        "td,dhe->the", first_all, w_qkv, preferred_element_type=jnp.float32
    ) + b_qkv.astype(jnp.float32)
    projected = projected.reshape(sequences, LEN, heads_here, 3 * head_size)
    queries = rotate(projected[..., :head_size], cosine, sine, ROT).astype(jnp.bfloat16)
    keys_bf = rotate(projected[..., head_size : 2 * head_size], cosine, sine, ROT).astype(
        jnp.bfloat16
    )
    values_bf = projected[..., 2 * head_size :].astype(jnp.bfloat16)

    def forward_sequence(group):
        return attend_forward(group[0], group[1], group[2], scale)

    contexts, log_mass = lax.map(forward_sequence, (queries, keys_bf, values_bf))
    context_flat = contexts.reshape(token_count, heads_here * head_size)
    hidden = jnp.dot(second_all, w_up, preferred_element_type=jnp.float32) + b_up.astype(
        jnp.float32
    )
    activated = jax.nn.gelu(hidden, approximate=False).astype(jnp.bfloat16)
    out_flat = w_out.reshape(heads_here * head_size, w_out.shape[2])
    branch_total = lax.psum_scatter(
        (
            jnp.dot(context_flat, out_flat, preferred_element_type=jnp.float32)
            + jnp.dot(activated, w_down, preferred_element_type=jnp.float32)
        ).astype(jnp.bfloat16),
        "tensor",
        scatter_dimension=0,
        tiled=True,
    ).astype(jnp.float32)
    layer_out = (local_rows + branch_total + out_bias.astype(jnp.float32)).astype(jnp.bfloat16)
    grad_all = lax.all_gather(cotangent, "tensor", axis=0, tiled=True)
    grad_active = jnp.einsum("td,fd->tf", grad_all, w_down, preferred_element_type=jnp.float32)
    grad_w_down = jnp.einsum("tf,td->fd", activated, grad_all, preferred_element_type=jnp.float32)
    gelu_value, gelu_pull = jax.vjp(partial(jax.nn.gelu, approximate=False), hidden)
    grad_hidden = gelu_pull(grad_active)[0].astype(jnp.bfloat16)
    grad_b_up = jnp.sum(grad_hidden.astype(jnp.float32), axis=0)
    grad_w_up = jnp.einsum("td,tf->df", second_all, grad_hidden, preferred_element_type=jnp.float32)
    grad_second = jnp.einsum("tf,df->td", grad_hidden, w_up, preferred_element_type=jnp.float32)
    context_heads = contexts.reshape(token_count, heads_here, head_size)
    grad_context = jnp.einsum(
        "td,hed->the", grad_all, w_out, preferred_element_type=jnp.float32
    ).astype(jnp.bfloat16)
    grad_w_out = jnp.einsum(
        "the,td->hed", context_heads, grad_all, preferred_element_type=jnp.float32
    )
    grad_context = grad_context.reshape(sequences, LEN, heads_here, head_size)

    def backward_sequence(group):
        return attend_backward(group[0], group[1], group[2], group[3], group[4], scale)

    grad_queries, grad_keys, grad_values = lax.map(
        backward_sequence, (queries, keys_bf, values_bf, grad_context, log_mass)
    )
    grad_projected = jnp.concatenate(
        [
            rotate(grad_queries, cosine, -sine, ROT),
            rotate(grad_keys, cosine, -sine, ROT),
            grad_values,
        ],
        axis=-1,
    )
    grad_projected = grad_projected.astype(jnp.bfloat16).reshape(
        token_count, heads_here, 3 * head_size
    )
    grad_b_qkv = jnp.sum(grad_projected.astype(jnp.float32), axis=0)
    grad_w_qkv = jnp.einsum(
        "td,the->dhe", first_all, grad_projected, preferred_element_type=jnp.float32
    )
    grad_first = jnp.einsum(
        "the,dhe->td", grad_projected, w_qkv, preferred_element_type=jnp.float32
    )
    grad_rows = cotangent.astype(jnp.float32)
    partial_sums = (
        jnp.sum(grad_rows, axis=0),
        jnp.sum(grad_first * normalized_all, axis=0),
        jnp.sum(grad_first, axis=0),
        jnp.sum(grad_second * normalized_all, axis=0),
        jnp.sum(grad_second, axis=0),
    )
    weighted = grad_first * gain_one + grad_second * gain_two
    local_weighted = lax.psum_scatter(
        weighted.astype(jnp.bfloat16), "tensor", scatter_dimension=0, tiled=True
    ).astype(jnp.float32)
    input_grad = (grad_rows + norm_back(local_weighted, normalized, inverse)).astype(jnp.bfloat16)
    small_sums = together(
        (partial_sums[0], partial_sums[1], partial_sums[2], partial_sums[3], partial_sums[4]),
        ("dp", "tensor"),
    )
    large_sums = (
        lax.psum(grad_w_qkv.astype(jnp.bfloat16), "dp").astype(jnp.float32),
        lax.psum(grad_b_qkv.astype(jnp.bfloat16), "dp").astype(jnp.float32),
        lax.psum(grad_w_out.astype(jnp.bfloat16), "dp").astype(jnp.float32),
        lax.psum(grad_w_up.astype(jnp.bfloat16), "dp").astype(jnp.float32),
        lax.psum(grad_b_up.astype(jnp.bfloat16), "dp").astype(jnp.float32),
        lax.psum(grad_w_down.astype(jnp.bfloat16), "dp").astype(jnp.float32),
    )
    return (
        layer_out,
        input_grad,
        large_sums[0],
        large_sums[1],
        large_sums[2],
        large_sums[3],
        large_sums[4],
        large_sums[5],
        small_sums[0],
        small_sums[1],
        small_sums[2],
        small_sums[3],
        small_sums[4],
    )


def solution(mesh):
    placed = (
        P(("dp", "tensor"), None),
        P(None, "tensor", None),
        P("tensor", None),
        P("tensor", None, None),
        P(None, "tensor"),
        P("tensor"),
        P("tensor", None),
        P(),
        P(),
        P(),
        P(),
        P(),
        P(("dp", "tensor"), None),
    )
    return jax.shard_map(
        per_device,
        mesh=mesh,
        in_specs=placed,
        out_specs=(
            P(("dp", "tensor"), None),
            P(("dp", "tensor"), None),
            P(None, "tensor", None),
            P("tensor", None),
            P("tensor", None, None),
            P(None, "tensor"),
            P("tensor"),
            P("tensor", None),
            P(),
            P(),
            P(),
            P(),
            P(),
        ),
        check_vma=False,
    )
```

profile of v0, /device:TPU:0, one launch (start us, length us, event | category | flops | bytes accessed | tf_op | source)
XLA Modules:
  0.0 413.6 jit_solution(2769586262432596271)
XLA Ops:
  13.4 36.2 %all-gather.3.cloned.1.call-done = bf16[2048,1024]{1,0:T(8,128)(2,1)} async-done(((bf16[128,1024]{1,0:T(8,128)(2,1)}), bf16[2048,1024]{1,0:T(8,128)(2,1)}) %all-gather.3.cloned.1.call-update) | async-done | bytes 4194320 | tf_op jit(solution)/shard_map/all_gather | solution.py:147
  49.7 3.0 convert_reduce_fusion
  54.5 3.7 add_convert_fusion.2
  60.7 16.3 %while.47 = (s32[]{:T(128)}, bf16[4,512,1,64]{1,3,2,0:T(8,128)(2,1)S(1)}, f32[4,1,512]{2,1,0:T(1,128)S(1)}, s32[4]{0:T(128)S(1)}, bf16[2048,1,64]{0,2,1:T(8,128)...) while((s32[]{:T(128)}, ...), condition=%wide.region_5.6_spmd, body=%wide.region_2.5_spmd.sunk | while | flops 277905408 | bytes 13263039 | solution.py:79
  77.7 11.3 %all-gather.5.cloned.1.call-done = bf16[2048,1024]{1,0:T(8,128)(2,1)} async-done(((bf16[128,1024]{1,0:T(8,128)(2,1)}), bf16[2048,1024]{1,0:T(8,128)(2,1)}) %all-gather.5.cloned.1.call-update) | async-done | bytes 4194320 | tf_op jit(solution)/shard_map/all_gather | solution.py:190
  89.0 3.6 fusion.35
  92.6 46.9 %while.48 = (s32[]{:T(128)}, f32[2048,1,64]{0,2,1:T(8,128)S(1)}, f32[2048,1,64]{0,2,1:T(8,128)S(1)}, f32[4,512,1,64]{1,0,3,2:T(4,128)}, s32[4]{0:T(128)S(1)}, /*...) while((s32[]{:T(128)}, f32[2048,1,64]{0,2,1:T(8,128)S(1)}, ...), condition=%wide.region_9.10_spmd.clone, body=%wide.region_7.9_spmd.clone.sunk | while | flops 682262528 | bytes 35272980 | solution.py:120
  100.7 3.6 dynamic_update_slice.33
  112.4 3.6 dynamic_update_slice.33
  124.1 3.6 dynamic_update_slice.33
  135.8 3.6 dynamic_update_slice.33
  147.4 4.3 %fusion.42 = bf16[1024,1,192]{0,2,1:T(8,128)(2,1)} fusion(bf16[2048,192]{0,1:T(8,128)(2,1)S(1)} %bitcast_dynamic-update-slice_fusion, bf16[2048,1024]{1,0:T(8,128)(2,1)} %copy-done.3), kind=kOutput, calls=%fused_computation.83 | convolution fusion | flops 805502976 | bytes 5373952 | tf_op jit(solution)/shard_map/td,the->dhe/dot_general | solution.py:225
  154.0 6.3 %fusion.63 = (bf16[256]{0:T(256)(128)(2,1)}, bf16[2048,256]{1,0:T(8,128)(2,1)S(1)}, f32[2048,256]{1,0:T(8,128)S(1)}) fusion(f32[2048,256]{1,0:T(8,128)S(1)} %convolution_add_fusion, bf16[2048,1024]{1,0:T(8,128)(2,1)S(1)} %copy-done.4, bf16[256,1024]{1,0:T(8,128)(2,1)S(1)} %copy-done.11), kind=kOutput, calls=%fused_computation.151 | convolution fusion | flops 1112014592 | bytes 9961984 | tf_op jit(solution)/shard_map/td,fd->tf/dot_general | solution.py:191
  160.4 2.1 convolution_convert_fusion.2
  164.6 2.1 convolution_convert_fusion.1
  166.7 2.6 fusion.48
  169.4 7.3 %fusion.61 = (f32[1024]{0:T(1024)}, f32[1024]{0:T(1024)}, bf16[2048,1024]{1,0:T(8,128)(2,1)}, f32[1024]{0:T(1024)}, f32[1024]{0:T(1024)}, /*index=5*/f32[2048,1024]{1,0:T(8,128)}) fusion(f32[2048]{0:T(1024)S(1)} %add_rsqrt_fusion, f32[2048]{0:T(1024)S(1)} %broadcast_multiply_fusion, bf16[2048,1024]{1,0:T(8,128)(2,1)S(1)} %copy-done.2, ...), kind=kOutput, calls=%fused_computation.149 | convolution fusion | flops 1101000704 | bytes 26779648 | tf_op jit(solution)/shard_map/tf,df->td/dot_general | solution.py:197
  178.1 3.4 add_convert_fusion.1
  182.8 24.0 %all-reduce = (bf16[1,192]{1,0:T(2,128)(2,1)S(1)}, bf16[256]{0:T(256)(128)(2,1)S(1)}) all-reduce(bf16[1,192]{1,0:T(2,128)(2,1)S(1)} %reduce_sum.130, bf16[256]{0:T(256)(128)(2,1)S(1)} %copy-done.27), channel_id=1, replica_groups=mesh['dp'=8,'tensor'=16] {'dp'}, use_global_device_ids=true, to_apply=%region_15.16 | all-reduce | flops 448 | bytes 1792 | tf_op jit(solution)/shard_map/psum | solution.py:250
  208.0 57.7 %all-reduce.4.cloned.1.call-done = (bf16[1024,1,192]{0,2,1:T(8,128)(2,1)}, bf16[1,64,1024]{2,1,0:T(8,128)(2,1)}, bf16[1024,256]{1,0:T(8,128)(2,1)}, bf16[256,1024]{1,0:T(8,128)(2,1)}) async-done(((bf16[1024,1,192]{0,2,1:T(8,128)(2,1)}, bf16[1,64,1024]{2,1,0:T(8,128)(2,1)}, bf16[1024,256]{1,0:T(8,128)(2,1)}, bf16[256,1024]{1,0:T(8,128)(2,1)}), (bf16[1024,1,192]{0,2,1:T(8,128)(2,1)}, ...) | async-done | bytes 1572880 | tf_op jit(solution)/shard_map/psum | solution.py:249
  269.4 2.1 convert_element_type.187
  272.6 62.1 %reduce-scatter.5.cloned.1.call-done = bf16[128,1024]{1,0:T(8,128)(2,1)} async-done(((bf16[2048,1024]{1,0:T(8,128)(2,1)}), bf16[128,1024]{1,0:T(8,128)(2,1)}) %reduce-scatter.5.cloned.1.call-update) | async-done | bytes 262160 | tf_op jit(solution)/shard_map/reduce_scatter | solution.py:240
  336.0 2.0 convert_reduce_fusion.2
  338.1 66.5 %psum.55 = f32[5120]{0:T(1024)S(1)} all-reduce(f32[5120]{0:T(1024)S(1)} %constant_dynamic-update-slice_fusion.10), channel_id=1, replica_groups=mesh['dp'=8,'tensor'=16] {'dp','tensor'}, use_global_device_ids=true, to_apply=%region_26.27 | all-reduce | flops 5120 | bytes 40960 | tf_op jit(solution)/shard_map/psum | solution.py:19
  (201 shorter events, 71.0 us)
Async XLA Ops:
  7.2 144.5 %copy-start = (bf16[1024,256]{1,0:T(8,128)(2,1)S(1)}, bf16[1024,256]{1,0:T(8,128)(2,1)}, u32[]{:S(2)}) copy-start(bf16[1024,256]{1,0:T(8,128)(2,1)} %param.21) | copy-start | bytes 1572868
  7.2 42.5 %all-gather.3.cloned.1.call-start = ((), (), s32[]{:S(2)}) async-start(), calls=%async_computation.2 | async-start | bytes 4456448 | tf_op jit(solution)/shard_map/all_gather | solution.py:147
  7.9 81.1 %all-gather.5.cloned.1.call-start = ((), (), s32[]{:S(2)}) async-start(), calls=%async_computation.4 | async-start | bytes 4456448 | tf_op jit(solution)/shard_map/all_gather | solution.py:190
  8.7 257.0 %all-reduce.4.cloned.1.call-start = ((), (), s32[]{:S(2)}) async-start(), calls=%async_computation.6 | async-start | bytes 3145728 | tf_op jit(solution)/shard_map/psum | solution.py:249
  8.7 136.0 %copy-start.20 = (f32[8]{0:T(128)}, f32[8]{0:T(128)S(1)}, u32[]{:S(2)}) copy-start(f32[8]{0:T(128)S(1)} %multiply_power_fusion) | copy-start | bytes 100
  11.4 43.1 %copy-start.16 = (f32[1024]{0:T(1024)}, f32[1024]{0:T(1024)S(1)}, u32[]{:S(2)}) copy-start(f32[1024]{0:T(1024)S(1)} %convert_element_type.161) | copy-start | bytes 12292
  12.1 42.4 %copy-start.18 = (f32[1024]{0:T(1024)}, f32[1024]{0:T(1024)S(1)}, u32[]{:S(2)}) copy-start(f32[1024]{0:T(1024)S(1)} %convert_element_type.164) | copy-start | bytes 12292
  49.6 3.4 copy-start.1
  54.5 3.8 copy-start.7
  60.7 28.3 %copy-start.13 = (bf16[1,64,1024]{2,1,0:T(8,128)(2,1)S(1)}, bf16[1,64,1024]{2,1,0:T(8,128)(2,1)}, u32[]{:S(2)}) copy-start(bf16[1,64,1024]{2,1,0:T(8,128)(2,1)} %param.20) | copy-start | bytes 393220
  147.4 4.3 %copy-start.6 = (bf16[2048,192]{0,1:T(8,128)(2,1)}, bf16[2048,192]{0,1:T(8,128)(2,1)S(1)}, u32[]{:S(2)}) copy-start(bf16[2048,192]{0,1:T(8,128)(2,1)S(1)} %bitcast_dynamic-update-slice_fusion) | copy-start | bytes 2359300
  147.4 4.3 %copy-start.5 = (bf16[2048,1024]{1,0:T(8,128)(2,1)S(1)}, bf16[2048,1024]{1,0:T(8,128)(2,1)}, u32[]{:S(2)}) copy-start(bf16[2048,1024]{1,0:T(8,128)(2,1)} %get-tuple-element.270) | copy-start | bytes 12582916
  147.4 4.3 %copy-start.26 = (f32[256]{0:T(256)S(1)}, f32[256]{0:T(256)}, u32[]{:S(2)}) copy-start(f32[256]{0:T(256)} %convert_element_type.167) | copy-start | bytes 3076
  166.6 2.7 copy-start.17
  166.7 168.1 %reduce-scatter.5.cloned.1.call-start = ((), (), s32[]{:S(2)}) async-start(), calls=%async_computation.5 | async-start | bytes 4456448 | tf_op jit(solution)/shard_map/reduce_scatter | solution.py:240
  166.7 2.7 copy-start.29
  176.7 228.6 %reduce-scatter.3.cloned.1.call-start = ((), (), s32[]{:S(2)}) async-start(), calls=%async_computation.3 | async-start | bytes 4456448 | tf_op jit(solution)/shard_map/reduce_scatter | solution.py:180
  265.7 5.8 %copy-start.14 = (bf16[256,1024]{1,0:T(8,128)(2,1)S(1)}, bf16[256,1024]{1,0:T(8,128)(2,1)}, u32[]{:S(2)}) copy-start(bf16[256,1024]{1,0:T(8,128)(2,1)} %get-tuple-element.250) | copy-start | bytes 1572868
  269.4 66.7 %copy-start.8 = (bf16[128,1024]{1,0:T(8,128)(2,1)S(1)}, bf16[128,1024]{1,0:T(8,128)(2,1)}, u32[]{:S(2)}) copy-start(bf16[128,1024]{1,0:T(8,128)(2,1)} %param.29) | copy-start | bytes 786436
  271.5 66.6 %copy-start.24 = (f32[1024]{0:T(1024)S(1)}, f32[1024]{0:T(1024)}, u32[]{:S(2)}) copy-start(f32[1024]{0:T(1024)} %get-tuple-element.267) | copy-start | bytes 12292
  271.5 66.6 %copy-start.23 = (f32[1024]{0:T(1024)S(1)}, f32[1024]{0:T(1024)}, u32[]{:S(2)}) copy-start(f32[1024]{0:T(1024)} %get-tuple-element.268) | copy-start | bytes 12292
  271.5 66.6 %copy-start.22 = (f32[1024]{0:T(1024)S(1)}, f32[1024]{0:T(1024)}, u32[]{:S(2)}) copy-start(f32[1024]{0:T(1024)} %get-tuple-element.206) | copy-start | bytes 12292
  271.5 66.6 %copy-start.21 = (f32[1024]{0:T(1024)S(1)}, f32[1024]{0:T(1024)}, u32[]{:S(2)}) copy-start(f32[1024]{0:T(1024)} %get-tuple-element.205) | copy-start | bytes 12292
  271.5 133.8 %copy-start.9 = (bf16[128,1024]{1,0:T(8,128)(2,1)S(1)}, bf16[128,1024]{1,0:T(8,128)(2,1)}, u32[]{:S(2)}) copy-start(bf16[128,1024]{1,0:T(8,128)(2,1)} %param.17) | copy-start | bytes 786436
  (11 other events, 19.1 us)
Sparse Core Ops, SparseCore 0:
  9.7 39.8 all-gather.2
  51.4 37.5 all-gather.4
  166.8 98.9 all-reduce.3
  268.0 66.7 reduce-scatter.4
  337.0 66.0 reduce-scatter.2
where the time goes:
time: 415 us; the launch traced here: 414 us
  waiting for transfers between devices  169 us (41%)
  blocking collectives  90.6 us (22%)
  matrix products  62.7 us (15%)
  other arithmetic  35.9 us (9%)
  local copies, waits for them, and re-layouts  27.8 us (7%)
  between operations  14.3 us (3%)
  loops' own time  13.4 us (3%)
    psum x1, blocking collectives, together(): running = lax.psum(jnp.concatenate([a.ravel() for a in arrays]), axis)  66.5 us
    reduce_scatter x1, waiting for transfers between devices, per_device(): lax.psum_scatter(weighted.astype(jnp.bfloat16), 'tensor', scatter_dimensi...  62.1 us
    psum x1, waiting for transfers between devices, per_device(): lax.psum(grad_w_qkv.astype(jnp.bfloat16), 'dp').astype(jnp.float32)  57.7 us
    all_gather x1, waiting for transfers between devices, per_device(): lax.all_gather(tokens, 'tensor', axis=0, tiled=True).astype(jnp.float32)  36.2 us
    psum x1, blocking collectives, per_device(): lax.psum(grad_b_qkv.astype(jnp.bfloat16), 'dp').astype(jnp.float32)  24 us
    dynamic_update_slice x8, local copies, waits for them, and re-layouts, attend_backward(): lax.scan(one_block, (empty, empty), jnp.arange(count, dtype=jnp.int32))  15.1 us
    all_gather x1, waiting for transfers between devices, per_device(): grad_all = lax.all_gather(cotangent, 'tensor', axis=0, tiled=True)  11.3 us
    dot_general x8, matrix products, block_scores(): jnp.einsum('bhe,the->hbt', query_rows, keys_all, preferred_element_type=j...  10.8 us
  transfers between devices with their start and end apart: 5, of which 4 were waited for; matrix products, arithmetic and copies ran while one was open for 13% of the time, Pallas kernels for 0%

commit v1 on v0

--- a/solution.py
+++ b/solution.py
@@ -12,12 +12,58 @@
 EPS = 1e-05
 
 
-def together(arrays, axis):
-    ends = [0]
-    for a in arrays:
-        ends.append(ends[-1] + a.size)
-    running = lax.psum(jnp.concatenate([a.ravel() for a in arrays]), axis)
-    return tuple((running[b:e].reshape(a.shape) for a, b, e in zip(arrays, ends, ends[1:])))
+SAME_CORE = [[c + 2 * i for i in range(8)] for c in range(2)]
+SAME_Z = [[c + 2 * i for i in range(4)] for c in range(2)]
+PAIR = [(i, i ^ 1) for i in range(16)]
+Z_PAIR = [(i, i ^ 1) for i in range(8)]
+
+
+def swap_core(value):
+    return lax.ppermute(value, "tensor", PAIR)
+
+
+def trade_chips(blocks):
+    return lax.all_to_all(blocks, "tensor", 0, 0, axis_index_groups=SAME_CORE, tiled=True)
+
+
+def trade_x(blocks):
+    return lax.all_to_all(blocks, "dp", 0, 0, axis_index_groups=SAME_Z, tiled=True)
+
+
+def gather_rows(block):
+    mine = trade_chips(jnp.broadcast_to(block[None], (8,) + block.shape))
+    other = swap_core(mine)
+    first_core = lax.axis_index("tensor") % 2 == 0
+    even = jnp.where(first_core, mine, other)
+    odd = jnp.where(first_core, other, mine)
+    return jnp.stack([even, odd], axis=1).reshape(16 * block.shape[0], block.shape[1])
+
+
+def scatter_rows(partial):
+    core = lax.axis_index("tensor") % 2
+    split = partial.reshape(8, 2, partial.shape[0] // 16, partial.shape[1])
+    send = lax.dynamic_index_in_dim(split, 1 - core, 1, keepdims=False)
+    keep = lax.dynamic_index_in_dim(split, core, 1, keepdims=False)
+    other = swap_core(send)
+    both = (keep.astype(jnp.float32) + other.astype(jnp.float32)).astype(jnp.bfloat16)
+    return jnp.sum(trade_chips(both).astype(jnp.float32), axis=0)
+
+
+def sum_dp(chunks):
+    mine = jnp.sum(trade_x(chunks).astype(jnp.float32), axis=0)
+    low = mine.astype(jnp.bfloat16)
+    other = lax.ppermute(low, "dp", Z_PAIR)
+    both = (low.astype(jnp.float32) + other.astype(jnp.float32)).astype(jnp.bfloat16)
+    return trade_x(jnp.broadcast_to(both[None], chunks.shape)).astype(jnp.float32)
+
+
+def sum_all(rows):
+    chips = jnp.sum(trade_chips(jnp.broadcast_to(rows[None], (8,) + rows.shape)), axis=0)
+    pair = chips + swap_core(chips)
+    return jnp.sum(
+        lax.all_to_all(jnp.broadcast_to(pair[None], (8,) + rows.shape), "dp", 0, 0, tiled=True),
+        axis=0,
+    )
 
 
 def normalize(values):
@@ -144,7 +190,7 @@
     gain_two = ln2_gain.astype(jnp.float32)
     shift_one = ln1_shift.astype(jnp.float32)
     shift_two = ln2_shift.astype(jnp.float32)
-    rows_all = lax.all_gather(tokens, "tensor", axis=0, tiled=True).astype(jnp.float32)
+    rows_all = gather_rows(tokens).astype(jnp.float32)
     normalized_all, inverse_all = normalize(rows_all)
     first_all = (normalized_all * gain_one + shift_one).astype(jnp.bfloat16)
     second_all = (normalized_all * gain_two + shift_two).astype(jnp.bfloat16)
@@ -177,17 +223,14 @@
     )
     activated = jax.nn.gelu(hidden, approximate=False).astype(jnp.bfloat16)
     out_flat = w_out.reshape(heads_here * head_size, w_out.shape[2])
-    branch_total = lax.psum_scatter(
+    branch_total = scatter_rows(
         (
             jnp.dot(context_flat, out_flat, preferred_element_type=jnp.float32)
             + jnp.dot(activated, w_down, preferred_element_type=jnp.float32)
-        ).astype(jnp.bfloat16),
-        "tensor",
-        scatter_dimension=0,
-        tiled=True,
-    ).astype(jnp.float32)
+        ).astype(jnp.bfloat16)
+    )
     layer_out = (local_rows + branch_total + out_bias.astype(jnp.float32)).astype(jnp.bfloat16)
-    grad_all = lax.all_gather(cotangent, "tensor", axis=0, tiled=True)
+    grad_all = gather_rows(cotangent)
     grad_active = jnp.einsum("td,fd->tf", grad_all, w_down, preferred_element_type=jnp.float32)
     grad_w_down = jnp.einsum("tf,td->fd", activated, grad_all, preferred_element_type=jnp.float32)
     gelu_value, gelu_pull = jax.vjp(partial(jax.nn.gelu, approximate=False), hidden)
@@ -237,21 +280,52 @@
         jnp.sum(grad_second, axis=0),
     )
     weighted = grad_first * gain_one + grad_second * gain_two
-    local_weighted = lax.psum_scatter(
-        weighted.astype(jnp.bfloat16), "tensor", scatter_dimension=0, tiled=True
-    ).astype(jnp.float32)
+    local_weighted = scatter_rows(weighted.astype(jnp.bfloat16))
     input_grad = (grad_rows + norm_back(local_weighted, normalized, inverse)).astype(jnp.bfloat16)
-    small_sums = together(
-        (partial_sums[0], partial_sums[1], partial_sums[2], partial_sums[3], partial_sums[4]),
-        ("dp", "tensor"),
-    )
+    small_sums = sum_all(jnp.stack(partial_sums))
+    low = jnp.bfloat16
+    ff_here = w_up.shape[1]
+    model = w_up.shape[0]
+    quarter = model // 4
+    head_rows = heads_here * head_size
+    widths = heads_here * 3 * head_size
+
+    def by_columns(grad):
+        return jnp.swapaxes(grad.reshape(grad.shape[0], 4, quarter), 0, 1)
+
+    def from_columns(chunks):
+        return jnp.swapaxes(chunks, 0, 1).reshape(chunks.shape[1], model)
+
+    feed = jnp.concatenate(
+        [
+            grad_w_up.reshape(4, quarter, ff_here),
+            by_columns(grad_w_down),
+            jnp.broadcast_to(grad_b_up[None, None, :], (4, 16, ff_here)),
+        ],
+        axis=1,
+    ).astype(low)
+    feed = sum_dp(feed)
+    head_parts = jnp.concatenate(
+        [
+            jnp.pad(
+                grad_w_qkv.reshape(4, quarter, widths), ((0, 0), (0, 0), (0, quarter - widths))
+            ),
+            by_columns(grad_w_out.reshape(head_rows, model)),
+            jnp.broadcast_to(
+                jnp.pad(grad_b_qkv.reshape(widths), (0, quarter - widths))[None, None, :],
+                (4, 16, quarter),
+            ),
+        ],
+        axis=1,
+    ).astype(low)
+    head_parts = sum_dp(head_parts)
     large_sums = (
-        lax.psum(grad_w_qkv.astype(jnp.bfloat16), "dp").astype(jnp.float32),
-        lax.psum(grad_b_qkv.astype(jnp.bfloat16), "dp").astype(jnp.float32),
-        lax.psum(grad_w_out.astype(jnp.bfloat16), "dp").astype(jnp.float32),
-        lax.psum(grad_w_up.astype(jnp.bfloat16), "dp").astype(jnp.float32),
-        lax.psum(grad_b_up.astype(jnp.bfloat16), "dp").astype(jnp.float32),
-        lax.psum(grad_w_down.astype(jnp.bfloat16), "dp").astype(jnp.float32),
+        head_parts[:, :quarter, :widths].reshape(grad_w_qkv.shape),
+        head_parts[0, quarter + head_rows, :widths].reshape(grad_b_qkv.shape),
+        from_columns(head_parts[:, quarter : quarter + head_rows]).reshape(grad_w_out.shape),
+        feed[:, :quarter].reshape(grad_w_up.shape),
+        feed[0, 2 * quarter],
+        from_columns(feed[:, quarter : 2 * quarter]),
     )
     return (
         layer_out,

time: 415 us -> 427 us (1.029); the launches traced: 414 us -> 421 us
  local copies, waits for them, and re-layouts: 27.8 us -> 102 us
  waiting for transfers between devices: 169 us -> 102 us
  blocking collectives: 90.6 us -> 32.5 us
  starting transfers between devices: 0.2 us -> 43.5 us
  matrix products: 62.7 us -> 80.5 us
  between operations: 14.3 us -> 1.8 us
  other arithmetic: 35.9 us -> 44.8 us
    psum x2 -> x0, blocking collectives: 90.6 us -> none  [the longest x1 66.5 us: together(): running = lax.psum(jnp.concatenate([a.ravel() for a in arrays]), axis)]
    all_to_all x0 -> x9, waiting for transfers between devices: none -> 83.5 us  [the longest x4 48.4 us: trade_chips(): lax.all_to_all(blocks, 'tensor', 0, 0, axis_index_groups=SAME_CORE, tiled...]
    reduce_scatter x2 -> x0, waiting for transfers between devices: 62.1 us -> none  [the longest x1 62.1 us: per_device(): lax.psum_scatter(weighted.astype(jnp.bfloat16), 'tensor', scatter_dimensi...]
    psum x1 -> x0, waiting for transfers between devices: 57.7 us -> none  [per_device(): lax.psum(grad_w_qkv.astype(jnp.bfloat16), 'dp').astype(jnp.float32)]
    all_gather x2 -> x0, waiting for transfers between devices: 47.5 us -> none  [the longest x1 36.2 us: per_device(): lax.all_gather(tokens, 'tensor', axis=0, tiled=True).astype(jnp.float32)]
    all_to_all x0 -> x9, starting transfers between devices: none -> 39.2 us  [the longest x4 20.8 us: trade_chips(): lax.all_to_all(blocks, 'tensor', 0, 0, axis_index_groups=SAME_CORE, tiled...]
    all_to_all x0 -> x1, blocking collectives: none -> 32.5 us  [trade_chips(): lax.all_to_all(blocks, 'tensor', 0, 0, axis_index_groups=SAME_CORE, tiled...]
    dot_general x0 -> x3, local copies, waits for them, and re-layouts: none -> 20 us  [the longest x1 6.9 us: per_device(): jnp.einsum('td,the->dhe', first_all, grad_projected, preferred_element_ty...]
  transfers between devices with their start and end apart: 5 -> 16, of which waited for: 4 -> 9; matrix products, arithmetic and copies ran while one was open for 13% -> 18% of each run, Pallas kernels for 0% -> 0%
where the time goes in v1:
time: 427 us; the launch traced here: 421 us
  local copies, waits for them, and re-layouts  102 us (24%)
  waiting for transfers between devices  102 us (24%)
  matrix products  80.5 us (19%)
  other arithmetic  44.8 us (10%)
  starting transfers between devices  43.5 us (10%)
  blocking collectives  32.5 us (8%)
  loops' own time  13.5 us (3%)
    all_to_all x4, waiting for transfers between devices, trade_chips(): lax.all_to_all(blocks, 'tensor', 0, 0, axis_index_groups=SAME_CORE, tiled...  48.4 us
    all_to_all x1, blocking collectives, trade_chips(): lax.all_to_all(blocks, 'tensor', 0, 0, axis_index_groups=SAME_CORE, tiled...  32.5 us
    all_to_all x4, waiting for transfers between devices, trade_x(): lax.all_to_all(blocks, 'dp', 0, 0, axis_index_groups=SAME_Z, tiled=True)  27.6 us
    all_to_all x4, starting transfers between devices, trade_chips(): lax.all_to_all(blocks, 'tensor', 0, 0, axis_index_groups=SAME_CORE, tiled...  20.8 us
    unnamed x122, local copies, waits for them, and re-layouts  19.8 us
    ppermute x2, waiting for transfers between devices, sum_dp(): other = lax.ppermute(low, 'dp', Z_PAIR)  18.7 us
    dynamic_update_slice x8, local copies, waits for them, and re-layouts, attend_backward(): lax.scan(one_block, (empty, empty), jnp.arange(count, dtype=jnp.int32))  15.1 us
    all_to_all x4, starting transfers between devices, trade_x(): lax.all_to_all(blocks, 'dp', 0, 0, axis_index_groups=SAME_Z, tiled=True)  15 us
  transfers between devices with their start and end apart: 16, of which 9 were waited for; matrix products, arithmetic and copies ran while one was open for 18% of the time, Pallas kernels for 0%

profile of v1, /device:TPU:0, one launch (start us, length us, event | category | flops | bytes accessed | tf_op | source)
XLA Modules:
  0.0 421.0 jit_solution(13322345211945953171)
XLA Ops:
  1.9 32.5 %all_to_all.50 = bf16[8,128,1024]{2,1,0:T(8,128)(2,1)S(1)} all-to-all(bf16[8,128,1024]{2,1,0:T(8,128)(2,1)S(1)} %broadcast_in_dim.60), channel_id=1, replica_groups={{0,2,4,6,8,10,12,14},{1,3,5,7,9,11,13,15},{16,18,20,22,24,26,28,30},{17..., dimensions={0} | all-to-all | bytes 4194304 | tf_op jit(solution)/shard_map/all_to_all | solution.py:26
  36.5 4.3 %all-to-all-start.2 = ((bf16[8,128,1024]{2,1,0:T(8,128)(2,1)}), bf16[8,128,1024]{2,1,0:T(8,128)(2,1)}, u32[]{:S(2)}, u32[]{:S(2)}) async-start(bf16[8,128,1024]{2,1,0:T(8,128)(2,1)} %broadcast_in_dim.61), calls=%async_computation.2 | async-start | bytes 4194304 | tf_op jit(solution)/shard_map/all_to_all | solution.py:26
  42.8 30.2 %all-to-all-done.2 = bf16[8,128,1024]{2,1,0:T(8,128)(2,1)} async-done(((bf16[8,128,1024]{2,1,0:T(8,128)(2,1)}), bf16[8,128,1024]{2,1,0:T(8,128)(2,1)}, u32[]{:S(2)}, u32[]{:S(2)}) %all-to-all-start.2) | async-done | bytes 2097184 | tf_op jit(solution)/shard_map/all_to_all | solution.py:26
  88.2 27.9 %while.47 = (s32[]{:T(128)}, bf16[4,512,1,64]{1,3,2,0:T(8,128)(2,1)}, f32[4,1,512]{2,1,0:T(1,128)}, s32[4]{0:T(128)}, bf16[2048,1,64]{0,2,1:T(8,128)(2,1)}, /*in...) while((s32[]{:T(128)}, ...), condition=%wide.region_5.6_spmd, body=%wide.region_2.5_spmd.sunk | while | flops 277905408 | bytes 14311643 | solution.py:125
  116.1 4.3 %fusion.35 = bf16[2048,1,64]{0,2,1:T(8,128)(2,1)} fusion(bf16[2048,1024]{1,0:T(8,128)(2,1)} %bitcast.276, bf16[1,64,1024]{2,1,0:T(8,128)(2,1)S(1)} %copy-done.35), kind=kOutput, calls=%fused_computation.72 | convolution fusion | flops 268566528 | bytes 4587520 | tf_op jit(solution)/shard_map/td,hed->the/dot_general | solution.py:242
  120.9 64.0 %while.48 = (s32[]{:T(128)}, f32[2048,1,64]{0,2,1:T(8,128)}, f32[2048,1,64]{0,2,1:T(8,128)S(1)}, f32[4,512,1,64]{1,0,3,2:T(4,128)}, s32[4]{0:T(128)}, /*index=5*...) while((s32[]{:T(128)}, f32[2048,1,64]{0,2,1:T(8,128)}, ...), condition=%wide.region_9.10_spmd.clone, body=%wide.region_7.9_spmd.clone.sunk | while | flops 682262528 | bytes 40515944 | solution.py:166
  199.8 6.6 %copy.148 = bf16[1024,2048]{1,0:T(8,128)(2,1)} copy(bf16[1024,2048]{0,1:T(8,128)(2,1)} %bitcast.277) | data formatting | bytes 8388608 | tf_op jit(solution)/shard_map/the,td->hed/dot_general | solution.py:245
  218.3 7.0 %fusion.67 = (bf16[256]{0:T(256)(128)(2,1)S(1)}, bf16[2048,256]{1,0:T(8,128)(2,1)}, f32[2048,256]{1,0:T(8,128)}) fusion(f32[2048,256]{1,0:T(8,128)S(1)} %convolution_add_fusion, bf16[2048,1024]{1,0:T(8,128)(2,1)S(1)} %bitcast.278, bf16[256,1024]{1,0:T(8,128)(2,1)S(1)} %copy-done.33), kind=kOutput, calls=%fused_computation.173 | convolution fusion | flops 1112014592 | bytes 9961984 | tf_op jit(solution)/shard_map/td,fd->tf/dot_general | solution.py:234
  225.4 9.1 %fusion.65 = (f32[1024]{0:T(1024)}, f32[1024]{0:T(1024)}, bf16[2048,1024]{1,0:T(8,128)(2,1)S(1)}, f32[1024]{0:T(1024)}, f32[1024]{0:T(1024)}, /*index=5*/bf16[2048,1024]{1,0:T(8,128)(2,1)}, f32[2048,1024]{1,0:T(8,128)}) fusion(f32[2048]{0:T(1024)S(1)} %bitcast.304, f32[2048]{0:T(1024)S(1)} %bitcast.302, bf16[8,1,128,1024]{3,2,1,0:T(8,128)(2,1)S(1)} %copy-done.2, ...), kind=kOutput, calls=%fused_computation.171 | convolution fusion | flops 1109389312 | bytes 30978048 | tf_op jit(solution)/shard_map/tf,df->td/dot_general | solution.py:240
  237.6 6.9 %copy.162 = bf16[1024,2048]{1,0:T(8,128)(2,1)} copy(bf16[1024,2048]{0,1:T(8,128)(2,1)} %bitcast.292) | data formatting | bytes 8388608 | tf_op jit(solution)/shard_map/td,the->dhe/dot_general | solution.py:268
  244.5 3.7 convolution_convert_fusion.3
  248.6 6.6 %copy.163 = bf16[1024,2048]{1,0:T(8,128)(2,1)} copy(bf16[1024,2048]{0,1:T(8,128)(2,1)} %bitcast.286) | data formatting | bytes 8388608 | tf_op jit(solution)/shard_map/td,tf->df/dot_general | solution.py:239
  256.3 4.3 %all-to-all-start.4 = ((bf16[4,336,256]{2,1,0:T(8,128)(2,1)}), bf16[4,336,256]{2,1,0:T(8,128)(2,1)S(1)}, u32[]{:S(2)}, u32[]{:S(2)}) async-start(bf16[4,336,256]{2,1,0:T(8,128)(2,1)} %copy.150), calls=%async_computation.4 | async-start | bytes 1376256 | tf_op jit(solution)/shard_map/all_to_all | solution.py:30
  260.6 3.9 convolution_convert_fusion.2
  276.3 4.6 %fusion.32 = bf16[8,128,1024]{2,1,0:T(8,128)(2,1)} fusion(bf16[8,128,1024]{2,1,0:T(8,128)(2,1)} %collective-permute-done.3, bf16[8,2,128,1024]{3,2,1,0:T(8,128)(2,1)} %bitcast.290, s32[]{:T(128)S(6)} %select_n.69), kind=kLoop, calls=%fused_computation.63 | loop fusion | flops 4194304 | bytes 6291460 | tf_op jit(solution)/shard_map/convert_element_type | solution.py:48
  280.9 9.3 %all-to-all-done.6 = bf16[4,528,256]{2,1,0:T(8,128)(2,1)S(1)} async-done(((bf16[4,528,256]{2,1,0:T(8,128)(2,1)}), bf16[4,528,256]{2,1,0:T(8,128)(2,1)S(1)}, u32[]{:S(2)}, u32[]{:S(2)}) %all-to-all-start.6) | async-done | bytes 1081376 | tf_op jit(solution)/shard_map/all_to_all | solution.py:30
  306.7 18.7 %collective-permute-done.4 = bf16[336,256]{0,1:T(8,128)(2,1)} collective-permute-done((bf16[336,256]{0,1:T(8,128)(2,1)S(1)}, bf16[336,256]{0,1:T(8,128)(2,1)}, u32[]{:S(2)}, u32[]{:S(2)}) %collective-permute-start.4) | collective-permute-done | bytes 172064 | tf_op jit(solution)/shard_map/ppermute | solution.py:55
  334.5 6.4 %all-to-all-done.5 = bf16[4,336,256]{2,1,0:T(8,128)(2,1)S(1)} async-done(((bf16[4,336,256]{2,1,0:T(8,128)(2,1)}), bf16[4,336,256]{2,1,0:T(8,128)(2,1)S(1)}, u32[]{:S(2)}, u32[]{:S(2)}) %all-to-all-start.5) | async-done | bytes 688160 | tf_op jit(solution)/shard_map/all_to_all | solution.py:30
  348.8 9.0 %all-to-all-done.7 = bf16[4,528,256]{2,1,0:T(8,128)(2,1)S(1)} async-done(((bf16[4,528,256]{2,1,0:T(8,128)(2,1)}), bf16[4,528,256]{2,1,0:T(8,128)(2,1)S(1)}, u32[]{:S(2)}, u32[]{:S(2)}) %all-to-all-start.7) | async-done | bytes 1081376 | tf_op jit(solution)/shard_map/all_to_all | solution.py:30
  358.6 8.5 %all-to-all-start.8 = ((f32[8,5,1024]{2,1,0:T(8,128)}), f32[8,5,1024]{2,1,0:T(8,128)S(1)}, u32[]{:S(2)}, u32[]{:S(2)}) async-start(f32[8,5,1024]{2,1,0:T(8,128)} %broadcast_in_dim.68), calls=%async_computation.8 | async-start | bytes 524288 | tf_op jit(solution)/shard_map/all_to_all | solution.py:26
  367.1 4.6 %fusion.33 = bf16[8,128,1024]{2,1,0:T(8,128)(2,1)} fusion(bf16[8,128,1024]{2,1,0:T(8,128)(2,1)} %collective-permute-done.1, bf16[8,2,128,1024]{3,2,1,0:T(8,128)(2,1)} %bitcast.285, s32[]{:T(128)S(6)} %select_n.69), kind=kLoop, calls=%fused_computation.65 | loop fusion | flops 4194304 | bytes 6291460 | tf_op jit(solution)/shard_map/convert_element_type | solution.py:48
  374.7 4.4 %all-to-all-start.1 = ((bf16[8,128,1024]{2,1,0:T(8,128)(2,1)}), bf16[8,128,1024]{2,1,0:T(8,128)(2,1)}, u32[]{:S(2)}, u32[]{:S(2)}) async-start(bf16[8,128,1024]{2,1,0:T(8,128)(2,1)} %fusion.33), calls=%async_computation.1 | async-start | bytes 4194304 | tf_op jit(solution)/shard_map/all_to_all | solution.py:26
  389.8 15.9 %all-to-all-done.1 = bf16[8,128,1024]{2,1,0:T(8,128)(2,1)} async-done(((bf16[8,128,1024]{2,1,0:T(8,128)(2,1)}), bf16[8,128,1024]{2,1,0:T(8,128)(2,1)}, u32[]{:S(2)}, u32[]{:S(2)}) %all-to-all-start.1) | async-done | bytes 2097184 | tf_op jit(solution)/shard_map/all_to_all | solution.py:26
  412.6 7.6 %all-to-all-done.9 = f32[8,5,1024]{2,1,0:T(8,128)S(1)} async-done(((f32[8,5,1024]{2,1,0:T(8,128)}), f32[8,5,1024]{2,1,0:T(8,128)S(1)}, u32[]{:S(2)}, u32[]{:S(2)}) %all-to-all-start.9) | async-done | bytes 163872 | tf_op jit(solution)/shard_map/all_to_all | solution.py:64
  (338 shorter events, 197.3 us)
Async XLA Ops:
  0.6 213.8 %copy-start = (bf16[1024,256]{1,0:T(8,128)(2,1)S(1)}, bf16[1024,256]{1,0:T(8,128)(2,1)}, u32[]{:S(2)}) copy-start(bf16[1024,256]{1,0:T(8,128)(2,1)} %param.21) | copy-start | bytes 1572868
  1.9 32.5 %copy-start.28 = (bf16[128,1024]{1,0:T(8,128)(2,1)S(1)}, bf16[128,1024]{1,0:T(8,128)(2,1)}, u32[]{:S(2)}) copy-start(bf16[128,1024]{1,0:T(8,128)(2,1)} %param.29) | copy-start | bytes 786436
  34.4 38.6 %collective-permute-start = (bf16[8,128,1024]{2,1,0:T(8,128)(2,1)S(1)}, bf16[8,128,1024]{2,1,0:T(8,128)(2,1)}, u32[]{:S(2)}, u32[]{:S(2)}) collective-permute-start(bf16[8,128,1024]{2,1,0:T(8,128)(2,1)S(1)} %all_to_all.50), channel_id=1, source_target_pairs={{0,1},{1,0},{2,3},{3,2},{4,5},{5,4},{6,7},{7,6},{8,9},{9,8},{10,11... | collective-permute-start | bytes 6291464 | tf_op jit(solution)/shard_map/ppermute | solution.py:22
  36.5 36.5 %all-to-all-start.2 = ((bf16[8,128,1024]{2,1,0:T(8,128)(2,1)}), bf16[8,128,1024]{2,1,0:T(8,128)(2,1)}, u32[]{:S(2)}, u32[]{:S(2)}) async-start(bf16[8,128,1024]{2,1,0:T(8,128)(2,1)} %broadcast_in_dim.61), calls=%async_computation.2 | async-start | bytes 4194304 | tf_op jit(solution)/shard_map/all_to_all | solution.py:26
  41.5 36.3 %copy-start.38 = (f32[1024]{0:T(1024)}, f32[1024]{0:T(1024)S(1)}, u32[]{:S(2)}) copy-start(f32[1024]{0:T(1024)S(1)} %convert_element_type.220) | copy-start | bytes 12292
  41.6 36.3 %copy-start.40 = (f32[1024]{0:T(1024)}, f32[1024]{0:T(1024)S(1)}, u32[]{:S(2)}) copy-start(f32[1024]{0:T(1024)S(1)} %convert_element_type.221) | copy-start | bytes 12292
  42.8 43.8 %copy-start.44 = (f32[8]{0:T(128)}, f32[8]{0:T(128)S(1)}, u32[]{:S(2)}) copy-start(f32[8]{0:T(128)S(1)} %multiply_power_fusion) | copy-start | bytes 100
  73.0 8.9 %collective-permute-start.2 = (bf16[8,128,1024]{2,1,0:T(8,128)(2,1)}, bf16[8,128,1024]{2,1,0:T(8,128)(2,1)S(1)}, u32[]{:S(2)}, u32[]{:S(2)}) collective-permute-start(bf16[8,128,1024]{2,1,0:T(8,128)(2,1)} %all-to-all-done.2), channel_id=1, source_target_pairs={{0,1},{1,0},{2,3},{3,2},{4,5},{5,4},{6,7},{7,6},{8,9},{9,8},{10,11... | collective-permute-start | bytes 6291464 | tf_op jit(solution)/shard_map/ppermute | solution.py:22
  77.9 147.5 %copy-start.37 = (f32[8,2,128]{2,1,0:T(2,128)}, f32[8,2,128]{2,1,0:T(2,128)S(1)}, u32[]{:S(2)}) copy-start(f32[8,2,128]{2,1,0:T(2,128)S(1)} %add_rsqrt_fusion) | copy-start | bytes 24580
  88.2 27.9 %copy-start.35 = (bf16[1,64,1024]{2,1,0:T(8,128)(2,1)S(1)}, bf16[1,64,1024]{2,1,0:T(8,128)(2,1)}, u32[]{:S(2)}) copy-start(bf16[1,64,1024]{2,1,0:T(8,128)(2,1)} %param.20) | copy-start | bytes 393220
  237.1 39.1 %collective-permute-start.3 = (bf16[8,128,1024]{2,1,0:T(8,128)(2,1)}, bf16[8,128,1024]{2,1,0:T(8,128)(2,1)}, u32[]{:S(2)}, u32[]{:S(2)}) collective-permute-start(bf16[8,128,1024]{2,1,0:T(8,128)(2,1)} %dynamic-slice_bitcast_fusion), channel_id=1, source_target_pairs={{0,1},{1,0},{2,3},{3,2},{4,5},{5,4},{6,7},{7,6},{8,9},{9,8},{10,11... | collective-permute-start | bytes 6291464 | tf_op jit(solution)/shard_map/ppermute | solution.py:22
  256.3 15.7 %all-to-all-start.4 = ((bf16[4,336,256]{2,1,0:T(8,128)(2,1)}), bf16[4,336,256]{2,1,0:T(8,128)(2,1)S(1)}, u32[]{:S(2)}, u32[]{:S(2)}) async-start(bf16[4,336,256]{2,1,0:T(8,128)(2,1)} %copy.150), calls=%async_computation.4 | async-start | bytes 1376256 | tf_op jit(solution)/shard_map/all_to_all | solution.py:30
  272.0 18.2 %all-to-all-start.6 = ((bf16[4,528,256]{2,1,0:T(8,128)(2,1)}), bf16[4,528,256]{2,1,0:T(8,128)(2,1)S(1)}, u32[]{:S(2)}, u32[]{:S(2)}) async-start(bf16[4,528,256]{2,1,0:T(8,128)(2,1)} %pad_maximum_fusion.2), calls=%async_computation.6 | async-start | bytes 2162688 | tf_op jit(solution)/shard_map/all_to_all | solution.py:30
  291.2 35.3 %all-to-all-start.3 = ((bf16[8,128,1024]{2,1,0:T(8,128)(2,1)}), bf16[8,128,1024]{2,1,0:T(8,128)(2,1)S(1)}, u32[]{:S(2)}, u32[]{:S(2)}) async-start(bf16[8,128,1024]{2,1,0:T(8,128)(2,1)} %fusion.32), calls=%async_computation.3 | async-start | bytes 4194304 | tf_op jit(solution)/shard_map/all_to_all | solution.py:26
  301.1 66.0 %collective-permute-start.1 = (bf16[8,128,1024]{2,1,0:T(8,128)(2,1)}, bf16[8,128,1024]{2,1,0:T(8,128)(2,1)}, u32[]{:S(2)}, u32[]{:S(2)}) collective-permute-start(bf16[8,128,1024]{2,1,0:T(8,128)(2,1)} %dynamic-slice_bitcast_fusion.1), channel_id=1, source_target_pairs={{0,1},{1,0},{2,3},{3,2},{4,5},{5,4},{6,7},{7,6},{8,9},{9,8},{10,11... | collective-permute-start | bytes 6291464 | tf_op jit(solution)/shard_map/ppermute | solution.py:22
  301.4 24.0 %collective-permute-start.4 = (bf16[336,256]{0,1:T(8,128)(2,1)S(1)}, bf16[336,256]{0,1:T(8,128)(2,1)}, u32[]{:S(2)}, u32[]{:S(2)}) collective-permute-start(bf16[336,256]{0,1:T(8,128)(2,1)S(1)} %copy.167), channel_id=1, source_target_pairs={{0,16},{16,0},{32,48},{48,32},{64,80},{80,64},{96,112},{112,96},{1... | collective-permute-start | bytes 516104 | tf_op jit(solution)/shard_map/ppermute | solution.py:55
  306.6 25.7 %collective-permute-start.5 = (bf16[528,256]{1,0:T(8,128)(2,1)S(1)}, bf16[528,256]{1,0:T(8,128)(2,1)S(1)}, u32[]{:S(2)}, u32[]{:S(2)}) collective-permute-start(bf16[528,256]{1,0:T(8,128)(2,1)S(1)} %reduce_sum.186), channel_id=1, source_target_pairs={{0,16},{16,0},{32,48},{48,32},{64,80},{80,64},{96,112},{112,96},{1... | collective-permute-start | bytes 811016 | tf_op jit(solution)/shard_map/ppermute | solution.py:55
  328.1 12.7 %all-to-all-start.5 = ((bf16[4,336,256]{2,1,0:T(8,128)(2,1)}), bf16[4,336,256]{2,1,0:T(8,128)(2,1)S(1)}, u32[]{:S(2)}, u32[]{:S(2)}) async-start(bf16[4,336,256]{2,1,0:T(8,128)(2,1)} %broadcast_in_dim.65), calls=%async_computation.5 | async-start | bytes 1376256 | tf_op jit(solution)/shard_map/all_to_all | solution.py:30
  341.9 15.9 %all-to-all-start.7 = ((bf16[4,528,256]{2,1,0:T(8,128)(2,1)}), bf16[4,528,256]{2,1,0:T(8,128)(2,1)S(1)}, u32[]{:S(2)}, u32[]{:S(2)}) async-start(bf16[4,528,256]{2,1,0:T(8,128)(2,1)} %broadcast_in_dim.67), calls=%async_computation.7 | async-start | bytes 2162688 | tf_op jit(solution)/shard_map/all_to_all | solution.py:30
  358.6 15.4 %all-to-all-start.8 = ((f32[8,5,1024]{2,1,0:T(8,128)}), f32[8,5,1024]{2,1,0:T(8,128)S(1)}, u32[]{:S(2)}, u32[]{:S(2)}) async-start(f32[8,5,1024]{2,1,0:T(8,128)} %broadcast_in_dim.68), calls=%async_computation.8 | async-start | bytes 524288 | tf_op jit(solution)/shard_map/all_to_all | solution.py:26
  374.7 31.0 %all-to-all-start.1 = ((bf16[8,128,1024]{2,1,0:T(8,128)(2,1)}), bf16[8,128,1024]{2,1,0:T(8,128)(2,1)}, u32[]{:S(2)}, u32[]{:S(2)}) async-start(bf16[8,128,1024]{2,1,0:T(8,128)(2,1)} %fusion.33), calls=%async_computation.1 | async-start | bytes 4194304 | tf_op jit(solution)/shard_map/all_to_all | solution.py:26
  389.6 22.2 %copy-start.30 = (bf16[128,1024]{1,0:T(8,128)(2,1)S(1)}, bf16[128,1024]{1,0:T(8,128)(2,1)}, u32[]{:S(2)}) copy-start(bf16[128,1024]{1,0:T(8,128)(2,1)} %param.17) | copy-start | bytes 786436
  389.7 18.0 %collective-permute-start.6 = (f32[5,1024]{1,0:T(8,128)S(1)}, f32[5,1024]{1,0:T(8,128)S(1)}, u32[]{:S(2)}, u32[]{:S(2)}) collective-permute-start(f32[5,1024]{1,0:T(8,128)S(1)} %reduce_sum.192), channel_id=1, source_target_pairs={{0,1},{1,0},{2,3},{3,2},{4,5},{5,4},{6,7},{7,6},{8,9},{9,8},{10,11... | collective-permute-start | bytes 61448 | tf_op jit(solution)/shard_map/ppermute | solution.py:22
  408.4 11.8 %all-to-all-start.9 = ((f32[8,5,1024]{2,1,0:T(8,128)}), f32[8,5,1024]{2,1,0:T(8,128)S(1)}, u32[]{:S(2)}, u32[]{:S(2)}) async-start(f32[8,5,1024]{2,1,0:T(8,128)} %broadcast_in_dim.69), calls=%async_computation.9 | async-start | bytes 524288 | tf_op jit(solution)/shard_map/all_to_all | solution.py:64
  (63 other events, 230.0 us)

commit v2 on v0

v2 whole, which is shorter than its diff:
```python
from functools import partial

import jax
import jax.numpy as jnp
import numpy as np
from jax import lax
from jax.experimental import pallas as pl
from jax.experimental.pallas import tpu as pltpu
from jax.sharding import PartitionSpec as P

ROT = 16
LEN = 2048
EPS = 1e-05
HEAD = 64
ROWS = 256
STEPS = LEN // ROWS
HALF = ROWS // 2
SCALE = HEAD ** (-0.5)
EXTRA = 16

SAME_CORE = [[c + 2 * i for i in range(8)] for c in range(2)]
PAIR = [(i, i ^ 1) for i in range(16)]
Z_PAIR = [(i, i ^ 1) for i in range(8)]

F32 = jnp.float32
LOW = jnp.bfloat16


def swap_core(value):
    return lax.ppermute(value, "tensor", PAIR)


def trade_chips(blocks):
    return lax.all_to_all(blocks, "tensor", 0, 0, axis_index_groups=SAME_CORE, tiled=True)


def copies(block, count):
    return jnp.broadcast_to(block[None], (count,) + block.shape)


def move_x(value, distance):
    pairs = [(i, (i // 2 + distance) % 4 * 2 + i % 2) for i in range(8)]
    return lax.ppermute(value, "dp", pairs)


def add_four(own, moved):
    total = own.astype(F32)
    for part in moved:
        total = total + part.astype(F32)
    return total.astype(LOW)


def sum_z(low):
    other = lax.ppermute(low, "dp", Z_PAIR)
    return (low.astype(F32) + other.astype(F32)).astype(LOW)


def spread_x(low):
    return [low] + [move_x(low, distance) for distance in range(1, 4)]


def sum_four(rows, move):
    return (rows + move(rows, 2)) + (move(rows, 1) + move(rows, 3))


def normalize(values):
    center = values - jnp.mean(values, axis=-1, keepdims=True)
    inverse = lax.rsqrt(jnp.mean(center * center, axis=-1, keepdims=True) + EPS)
    return (center * inverse, inverse)


def norm_back(scaled, normalized, inverse):
    centered = scaled - jnp.mean(scaled, axis=-1, keepdims=True)
    return inverse * (centered - normalized * jnp.mean(scaled * normalized, axis=-1, keepdims=True))


def rotary_tables():
    lane = np.arange(2 * HEAD) % HEAD
    half = ROT // 2
    inverse = np.float32(10000.0) ** (-2.0 * (lane % half).astype(np.float32) / np.float32(ROT))
    inverse = np.where(lane < ROT, inverse, 0.0).astype(np.float32)
    angles = np.arange(LEN, dtype=np.float32)[:, None] * inverse[None, :]
    sign = np.where(lane < half, -1.0, 1.0).astype(np.float32)
    return np.cos(angles).astype(np.float32), (np.sin(angles) * sign).astype(np.float32)


def turn(values, cosine, sine):
    lane = lax.broadcasted_iota(jnp.int32, values.shape, 1) % HEAD
    partner = jnp.where(
        lane < ROT // 2,
        pltpu.roll(values, 2 * HEAD - ROT // 2, 1),
        pltpu.roll(values, ROT // 2, 1),
    )
    return values * cosine + partner * sine


def dot(left, right, left_axis=1, right_axis=0):
    return lax.dot_general(
        left,
        right,
        (((left_axis,), (right_axis,)), ((), ())),
        preferred_element_type=F32,
    )


def core_here():
    return lax.axis_index("tensor") % 2


def join_rows(mine, other, rows):
    core = core_here()
    rows[pl.ds(pl.multiple_of(core * HALF, HALF), HALF), :] = mine[0]
    rows[pl.ds(pl.multiple_of((1 - core) * HALF, HALF), HALF), :] = other[0]


def send_rows(block, send):
    core = core_here()
    send[0] = block[pl.ds(pl.multiple_of((1 - core) * HALF, HALF), HALF), :]


def x_here():
    return lax.axis_index("dp") // 2


def row_sum(values):
    return jnp.sum(values, axis=0, keepdims=True)


def project_kernel(
    mine, other, vecs, w_qkv, b_qkv, w_up, b_up, cosine, sine,
    first, second, normal, queries, keys, values, active, active_send, slope, rows,
):
    join_rows(mine, other, rows)
    here = rows[...].astype(F32)
    mean = jnp.mean(here, axis=-1, keepdims=True)
    center = here - mean
    inverse = lax.rsqrt(jnp.mean(center * center, axis=-1, keepdims=True) + EPS)
    normalized = center * inverse
    normal[...] = normalized.astype(LOW)
    one = (normalized * vecs[0:1, :] + vecs[1:2, :]).astype(LOW)
    two = (normalized * vecs[2:3, :] + vecs[3:4, :]).astype(LOW)
    first[...] = one
    second[...] = two
    projected = dot(one, w_qkv[...], 1, 1) + b_qkv[...]
    turned = turn(projected[:, : 2 * HEAD], cosine[...], sine[...])
    queries[...] = turned[:, :HEAD].astype(LOW) * SCALE
    keys[...] = turned[:, HEAD:].astype(LOW)
    values[...] = projected[:, 2 * HEAD :].astype(LOW)
    hidden = dot(two, w_up[...]) + b_up[...]
    share = 0.5 * (1.0 + lax.erf(hidden * (0.5**0.5)))
    active[...] = (hidden * share).astype(LOW)
    send_rows(active, active_send)
    slope[...] = share + hidden * (jnp.exp(-0.5 * hidden * hidden) * ((2.0 * np.pi) ** -0.5))


def attend_kernel(queries, keys, values, context, context_send, mass):
    place = lax.broadcasted_iota(jnp.int32, (ROWS, ROWS), 0)
    query = lax.broadcasted_iota(jnp.int32, (ROWS, ROWS), 1)
    seen = place <= query

    def block(index):
        low, high = index * ROWS, (index + 1) * ROWS
        asked = queries[low:high, :]
        near = jnp.where(seen, dot(keys[low:high, :], asked, 1, 1), -1e30)
        top = jnp.max(near, axis=0, keepdims=True)
        if index:
            far = dot(keys[:low, :], asked, 1, 1)
            top = jnp.maximum(top, jnp.max(far, axis=0, keepdims=True))
            far = jnp.exp(far - top)
        near = jnp.exp(near - top)
        total = row_sum(near)
        if index:
            total = total + row_sum(far)
        scale = 1.0 / total
        mass[0] = top + jnp.log(total)
        found = dot(values[low:high, :], (near * scale).astype(LOW), 0, 0)
        if index:
            found = found + dot(values[:low, :], (far * scale).astype(LOW), 0, 0)
        context[...] = found.T.astype(LOW)

    for index in range(STEPS):
        pl.when(pl.program_id(0) == index)(partial(block, index))
    send_rows(context, context_send)


def flat(block):
    return block.reshape(ROWS, block.shape[-1])


def mix_kernel(
    core, context, active, context_in, active_in, w_out, w_down, w_out_in, w_down_in, result
):
    mixed = dot(flat(context[...]), w_out[...]) + dot(flat(active[...]), w_down[...])
    mixed = mixed + dot(flat(context_in[...]), w_out_in[...])
    mixed = mixed + dot(flat(active_in[...]), w_down_in[...])
    result[...] = mixed.astype(LOW).reshape(2, HALF, mixed.shape[1])


def feed_back_kernel(
    mine, other, active, slope, second, context, w_down, w_out,
    grad_hidden, hidden_send, grad_context, feed_0, feed_1, feed_2, feed_3, grad_out,
    rows, up_sum, down_sum, out_sum, bias_sum,
):
    step = pl.program_id(0)

    @pl.when(step == 0)
    def _():
        up_sum[...] = jnp.zeros_like(up_sum)
        down_sum[...] = jnp.zeros_like(down_sum)
        out_sum[...] = jnp.zeros_like(out_sum)
        bias_sum[...] = jnp.zeros_like(bias_sum)

    join_rows(mine, other, rows)
    grads = rows[...]
    hidden = (dot(grads, w_down[...], 1, 1) * slope[...]).astype(LOW)
    grad_hidden[...] = hidden
    send_rows(grad_hidden, hidden_send)
    grad_context[...] = dot(grads, w_out[...], 1, 1).astype(LOW)
    down_sum[...] += dot(active[...], grads, 0, 0)
    out_sum[...] += dot(context[...], grads, 0, 0)
    up_sum[...] += dot(hidden, second[...], 0, 0)
    bias_sum[...] += row_sum(hidden.astype(F32))

    @pl.when(step == STEPS - 1)
    def _():
        grad_out[...] = out_sum[...].astype(LOW)
        for slot, feed in enumerate((feed_0, feed_1, feed_2, feed_3)):
            span = quarter((x_here() + slot) % 4)
            feed[0:256, :] = up_sum[:, span].T.astype(LOW)
            feed[256:512, :] = down_sum[:, span].astype(LOW)
            feed[512:528, :] = jnp.broadcast_to(bias_sum[...], (16, 256)).astype(LOW)


def quarter(part):
    return pl.ds(pl.multiple_of(part * 256, 256), 256)


def attend_back_kernel(
    queries, keys, values, grad_context, mass, cosine, sine,
    grad_projected, projected_send, query_sum, key_sum, value_sum,
):
    place = lax.broadcasted_iota(jnp.int32, (ROWS, ROWS), 0)
    query = lax.broadcasted_iota(jnp.int32, (ROWS, ROWS), 1)
    seen = place <= query

    @pl.when(pl.program_id(0) == 0)
    def _():
        key_sum[...] = jnp.zeros_like(key_sum)
        value_sum[...] = jnp.zeros_like(value_sum)

    def block(index):
        low, high = index * ROWS, (index + 1) * ROWS
        asked = queries[low:high, :]
        grads = grad_context[...]
        spans = [slice(low, high)] + ([slice(0, low)] if index else [])
        weights, pulls = [], []
        inner = 0.0
        for number, span in enumerate(spans):
            scores = dot(keys[span, :], asked, 1, 1)
            if number == 0:
                scores = jnp.where(seen, scores, -1e30)
            weight = jnp.exp(scores - mass[0])
            pull = dot(values[span, :], grads, 1, 1)
            inner = inner + row_sum(weight * pull)
            weights.append(weight)
            pulls.append(pull)
        asked_grad = 0.0
        for span, weight, pull in zip(spans, weights, pulls):
            value_sum[span, :] += dot(weight.astype(LOW), grads)
            scores_grad = (weight * (pull - inner)).astype(LOW)
            key_sum[span, :] += dot(scores_grad, asked)
            asked_grad = asked_grad + dot(keys[span, :], scores_grad, 0, 0)
        query_sum[low:high, :] = asked_grad.T * SCALE

    for index in range(STEPS):
        pl.when(pl.program_id(0) == index)(partial(block, index))

    @pl.when(pl.program_id(0) == STEPS - 1)
    def _():
        for index in range(STEPS):
            span = slice(index * ROWS, (index + 1) * ROWS)
            both = jnp.concatenate([query_sum[span, :], key_sum[span, :]], axis=1)
            turned = turn(both, cosine[span, :], -sine[span, :])
            grad_projected[span, : 2 * HEAD] = turned.astype(LOW)
            grad_projected[span, 2 * HEAD :] = value_sum[span, :].astype(LOW)
            place = index * ROWS + (1 - core_here()) * HALF
            projected_send[index] = grad_projected[pl.ds(pl.multiple_of(place, HALF), HALF), :]


def input_back_kernel(
    core, projected, hidden, projected_in, hidden_in, vecs, w_qkv, w_up, w_qkv_in, w_up_in, sums,
    result,
):
    one = dot(flat(projected[...]), w_qkv[...])
    one = one + dot(flat(projected_in[...]), w_qkv_in[...])
    two = dot(flat(hidden[...]), w_up[...], 1, 1)
    two = two + dot(flat(hidden_in[...]), w_up_in[...], 1, 1)
    weighted = one * vecs[0:1, :] + two * vecs[2:3, :]
    result[:, 0:HALF, :] = weighted.astype(LOW).reshape(2, HALF, weighted.shape[1])
    high = sums[...].astype(LOW).astype(F32)
    rest = jnp.zeros((EXTRA - 10, weighted.shape[1]), F32)
    tail = jnp.concatenate([high, sums[...] - high, rest], axis=0).astype(LOW)
    result[0, HALF:, :] = tail
    result[1, HALF:, :] = tail


def dot_full(left, right, right_axis):
    return lax.dot_general(
        left,
        right.astype(F32),
        (((1,), (right_axis,)), ((), ())),
        precision=lax.Precision.HIGHEST,
        preferred_element_type=F32,
    )


def last_grads_kernel(
    grad_projected, grad_hidden, first, normal, grad_out, w_qkv, w_up, own_sum,
    head_0, head_1, head_2, head_3, sums, qkv_sum, moments, bias_sum,
):
    step = pl.program_id(0)
    wide = 3 * HEAD

    @pl.when(step == 0)
    def _():
        qkv_sum[...] = jnp.zeros_like(qkv_sum)
        moments[...] = jnp.zeros_like(moments)
        bias_sum[...] = jnp.zeros_like(bias_sum)

    grads = grad_projected[...]
    hidden = grad_hidden[...]
    qkv_sum[...] += dot(grads, first[...], 0, 0)
    moments[0:wide, :] += dot(grads, normal[...], 0, 0)
    moments[wide:, :] += dot(hidden, normal[...], 0, 0)
    bias_sum[:, 0:wide] += row_sum(grads.astype(F32))
    bias_sum[:, 256:] += row_sum(hidden.astype(F32))

    @pl.when(step == STEPS - 1)
    def _():
        bias = bias_sum[:, 0:wide]
        for slot, head in enumerate((head_0, head_1, head_2, head_3)):
            span = quarter((x_here() + slot) % 4)
            head[0:wide, :] = qkv_sum[:, span].astype(LOW)
            head[wide:256, :] = grad_out[:, span]
            head[256:272, :wide] = jnp.broadcast_to(bias, (16, wide)).astype(LOW)
            head[256:272, wide:] = jnp.zeros((16, 256 - wide), LOW)
        sums[0:1, :] = row_sum(moments[0:wide, :] * w_qkv[...].astype(F32))
        sums[1:2, :] = dot_full(bias, w_qkv[...], 0)
        sums[2:3, :] = row_sum(moments[wide:, :] * w_up[...].astype(F32).T)
        sums[3:4, :] = dot_full(bias_sum[:, 256:], w_up[...], 1)
        sums[4:5, :] = own_sum[...]


def finish_grads_kernel(
    feed_0, feed_1, feed_2, feed_3, head_0, head_1, head_2, head_3,
    grad_qkv, grad_qkv_bias, grad_out, grad_up, grad_up_bias, grad_down,
):
    wide = 3 * HEAD
    for slot, feed in enumerate((feed_0, feed_1, feed_2, feed_3)):
        span = quarter((x_here() + 4 - slot) % 4)
        grad_up[span, :] = feed[0:256, :].astype(F32)
        grad_down[:, span] = feed[256:512, :].astype(F32)
    for slot, head in enumerate((head_0, head_1, head_2, head_3)):
        span = quarter((x_here() + 4 - slot) % 4)
        grad_qkv[:, span] = head[0:wide, :].astype(F32)
        grad_out[:, span] = head[wide:256, :].astype(F32)
    grad_up_bias[...] = feed_0[512:513, :].astype(F32)
    grad_qkv_bias[...] = head_0[256:257, :wide].astype(F32)


def finish_out_kernel(parts, tokens, out_bias, layer_out):
    total = jnp.sum(parts[...].astype(F32), axis=0)
    layer_out[...] = (tokens[...].astype(F32) + total + out_bias[...].astype(F32)).astype(LOW)


def finish_back_kernel(parts, tokens, cotangent, input_grad, sums):
    scaled = jnp.sum(parts[:, 0:HALF, :].astype(F32), axis=0)
    normalized, inverse = normalize(tokens[...].astype(F32))
    input_grad[...] = (
        cotangent[...].astype(F32) + norm_back(scaled, normalized, inverse)
    ).astype(LOW)
    tail = jnp.sum(parts[:, HALF:, :].astype(F32), axis=0)
    sums[...] = tail[0:5] + tail[5:10]


def whole(shape):
    return pl.BlockSpec(shape, lambda step: (0,) * len(shape))


def by_rows(columns):
    return pl.BlockSpec((ROWS, columns), lambda step: (step, 0))


HALVES = pl.BlockSpec((1, HALF, 1024), lambda step: (step, 0, 0))
MASS = pl.BlockSpec((1, 1, ROWS), lambda step: (step, 0, 0))


def shape(dims, kind):
    return jax.ShapeDtypeStruct(dims, kind)


COST = pl.CostEstimate(flops=1, bytes_accessed=1, transcendentals=0)


def launch(kernel, name, ins, outs, out_shapes, scratch, steps=STEPS, scalars=0):
    return pl.pallas_call(
        kernel,
        name=name,
        grid_spec=pltpu.PrefetchScalarGridSpec(
            num_scalar_prefetch=scalars,
            grid=(steps,),
            in_specs=ins,
            out_specs=outs,
            scratch_shapes=scratch,
        ),
        out_shape=out_shapes,
        compiler_params=pltpu.CompilerParams(vmem_limit_bytes=40 * 2**20),
        cost_estimate=COST,
    )


def fixed(dims):
    return pl.BlockSpec(dims, lambda step, core: (0,) * len(dims))


def parity(columns):
    return pl.BlockSpec((2, 1, HALF, columns), lambda step, core: (step, core[0], 0, 0))


def double(columns):
    return pl.BlockSpec((2, HALF, columns), lambda step, core: (step, 0, 0))


def half_rows(columns):
    return pl.BlockSpec((1, HALF, columns), lambda step: (step, 0, 0))


def four(value):
    return value.reshape(STEPS, 2, HALF, value.shape[1])


def per_device(
    tokens, w_qkv, b_qkv, w_out, w_up, b_up, w_down, out_bias,
    ln1_gain, ln1_shift, ln2_gain, ln2_shift, cotangent,
):
    model = w_up.shape[0]
    feed_here = w_up.shape[1]
    wide = 3 * HEAD
    core = core_here().astype(jnp.int32).reshape(1)
    w_qkv = w_qkv.transpose(1, 2, 0).reshape(wide, model)
    w_out = w_out.reshape(HEAD, model)
    vecs = jnp.stack([ln1_gain, ln1_shift, ln2_gain, ln2_shift]).astype(F32)
    cosine, sine = rotary_tables()
    own_sum = jnp.sum(cotangent.astype(F32), axis=0)[None, :]

    held = copies(cotangent, 8)
    mine = trade_chips(copies(tokens, 8))
    weights_in = [swap_core(w) for w in (w_out, w_down, w_qkv, w_up)]
    held, vecs, b_qkv, b_up, core, own_sum, mine, *weights_in = lax.optimization_barrier(
        (held, vecs, b_qkv.astype(F32), b_up.astype(F32)[None, :], core, own_sum, mine)
        + tuple(weights_in)
    )
    w_out_in, w_down_in, w_qkv_in, w_up_in = weights_in
    other = swap_core(mine)
    grad_mine = trade_chips(held)

    halves = shape((STEPS, HALF, feed_here), LOW)
    first, second, normal, queries, keys, values, active, active_send, slope = launch(
        project_kernel,
        "project",
        [
            HALVES, HALVES, whole((4, model)), whole((wide, model)), whole((1, wide)),
            whole((model, feed_here)), whole((1, feed_here)), by_rows(128), by_rows(128),
        ],
        [
            by_rows(model), by_rows(model), by_rows(model), by_rows(HEAD), by_rows(HEAD),
            by_rows(HEAD), by_rows(feed_here), half_rows(feed_here), by_rows(feed_here),
        ],
        [
            shape((LEN, model), LOW), shape((LEN, model), LOW), shape((LEN, model), LOW),
            shape((LEN, HEAD), LOW), shape((LEN, HEAD), LOW), shape((LEN, HEAD), LOW),
            shape((LEN, feed_here), LOW), halves, shape((LEN, feed_here), F32),
        ],
        [pltpu.VMEM((ROWS, model), LOW)],
    )(mine, other, vecs, w_qkv, b_qkv, w_up, b_up, cosine, sine)
    active_in = swap_core(active_send)

    context, context_send, mass = launch(
        attend_kernel,
        "attend",
        [whole((LEN, HEAD))] * 3,
        [by_rows(HEAD), half_rows(HEAD), MASS],
        [
            shape((LEN, HEAD), LOW), shape((STEPS, HALF, HEAD), LOW),
            shape((STEPS, 1, ROWS), F32),
        ],
        [],
    )(queries, keys, values)
    context_in = swap_core(context_send)

    mixed = launch(
        mix_kernel,
        "mix",
        [
            parity(HEAD), parity(feed_here), double(HEAD), double(feed_here),
            fixed((HEAD, model)), fixed((feed_here, model)),
            fixed((HEAD, model)), fixed((feed_here, model)),
        ],
        double(model),
        shape((STEPS, HALF, model), LOW),
        [],
        steps=4,
        scalars=1,
    )(
        core, four(context), four(active), context_in, active_in,
        w_out, w_down, w_out_in, w_down_in,
    )

    grad_mine, mixed = lax.optimization_barrier((grad_mine, mixed))
    grad_other = swap_core(grad_mine)
    branch = trade_chips(mixed)

    grad_hidden, hidden_send, grad_context, *feed, grad_out = launch(
        feed_back_kernel,
        "feed_back",
        [
            HALVES, HALVES, by_rows(feed_here), by_rows(feed_here), by_rows(model),
            by_rows(HEAD), whole((feed_here, model)), whole((HEAD, model)),
        ],
        [by_rows(feed_here), half_rows(feed_here), by_rows(HEAD)]
        + [whole((528, 256))] * 4 + [whole((HEAD, model))],
        [shape((LEN, feed_here), LOW), halves, shape((LEN, HEAD), LOW)]
        + [shape((528, 256), LOW)] * 4 + [shape((HEAD, model), LOW)],
        [
            pltpu.VMEM((ROWS, model), LOW), pltpu.VMEM((feed_here, model), F32),
            pltpu.VMEM((feed_here, model), F32), pltpu.VMEM((HEAD, model), F32),
            pltpu.VMEM((1, feed_here), F32),
        ],
    )(grad_mine, grad_other, active, slope, second, context, w_down, w_out)
    hidden_in = swap_core(hidden_send)
    feed_moved = [move_x(feed[distance], distance) for distance in range(1, 4)]

    grad_projected, projected_send = launch(
        attend_back_kernel,
        "attend_back",
        [
            whole((LEN, HEAD)), whole((LEN, HEAD)), whole((LEN, HEAD)), by_rows(HEAD), MASS,
            whole((LEN, 128)), whole((LEN, 128)),
        ],
        [whole((LEN, wide)), whole((STEPS, HALF, wide))],
        [shape((LEN, wide), LOW), shape((STEPS, HALF, wide), LOW)],
        [pltpu.VMEM((LEN, HEAD), F32)] * 3,
    )(queries, keys, values, grad_context, mass, cosine, sine)
    grad_projected, projected_send, branch, hidden_in, *feed_moved = lax.optimization_barrier(
        (grad_projected, projected_send, branch, hidden_in, *feed_moved)
    )
    projected_in = swap_core(projected_send)
    feed_low = sum_z(add_four(feed[0], feed_moved))

    *head, sums = launch(
        last_grads_kernel,
        "last_grads",
        [
            by_rows(wide), by_rows(feed_here), by_rows(model), by_rows(model),
            whole((HEAD, model)), whole((wide, model)), whole((model, feed_here)),
            whole((1, model)),
        ],
        [whole((272, 256))] * 4 + [whole((5, model))],
        [shape((272, 256), LOW)] * 4 + [shape((5, model), F32)],
        [
            pltpu.VMEM((wide, model), F32), pltpu.VMEM((wide + feed_here, model), F32),
            pltpu.VMEM((1, 512), F32),
        ],
    )(grad_projected, grad_hidden, first, normal, grad_out, w_qkv, w_up, own_sum)
    sums = sums + swap_core(sums)
    head_moved = [move_x(head[distance], distance) for distance in range(1, 4)]

    both = launch(
        input_back_kernel,
        "input_back",
        [
            parity(wide), parity(feed_here), double(wide), double(feed_here), fixed((4, model)),
            fixed((wide, model)), fixed((model, feed_here)),
            fixed((wide, model)), fixed((model, feed_here)), fixed((5, model)),
        ],
        pl.BlockSpec((2, HALF + EXTRA, model), lambda step, core: (step, 0, 0)),
        shape((STEPS, HALF + EXTRA, model), LOW),
        [],
        steps=4,
        scalars=1,
    )(
        core, four(grad_projected), four(grad_hidden), projected_in, hidden_in, vecs,
        w_qkv, w_up, w_qkv_in, w_up_in, sums,
    )
    both, feed_low, *head_moved = lax.optimization_barrier((both, feed_low, *head_moved))
    scaled = trade_chips(both)
    head_low = sum_z(add_four(head[0], head_moved))
    feed_parts = spread_x(feed_low)
    head_parts = spread_x(head_low)

    layer_out = pl.pallas_call(
        finish_out_kernel,
        name="finish_out",
        out_shape=shape(tokens.shape, LOW),
        cost_estimate=COST,
    )(branch, tokens, out_bias[None, :])
    grad_qkv, grad_qkv_bias, grad_out, grad_up, grad_up_bias, grad_down = pl.pallas_call(
        finish_grads_kernel,
        name="finish_grads",
        out_shape=[
            shape((wide, model), F32), shape((1, wide), F32), shape((HEAD, model), F32),
            shape((model, feed_here), F32), shape((1, feed_here), F32),
            shape((feed_here, model), F32),
        ],
        cost_estimate=COST,
    )(*feed_parts, *head_parts)
    input_grad, small = pl.pallas_call(
        finish_back_kernel,
        name="finish_back",
        out_shape=[shape(tokens.shape, LOW), shape((5, model), F32)],
        cost_estimate=COST,
    )(scaled, tokens, cotangent)
    small = sum_four(small + lax.ppermute(small, "dp", Z_PAIR), move_x)

    return (
        layer_out,
        input_grad,
        grad_qkv.reshape(1, wide, model).transpose(2, 0, 1),
        grad_qkv_bias,
        grad_out.reshape(1, HEAD, model),
        grad_up,
        grad_up_bias[0],
        grad_down,
        small[4],
        small[0],
        small[1],
        small[2],
        small[3],
    )


def solution(mesh):
    placed = (
        P(("dp", "tensor"), None),
        P(None, "tensor", None),
        P("tensor", None),
        P("tensor", None, None),
        P(None, "tensor"),
        P("tensor"),
        P("tensor", None),
        P(),
        P(),
        P(),
        P(),
        P(),
        P(("dp", "tensor"), None),
    )
    return jax.shard_map(
        per_device,
        mesh=mesh,
        in_specs=placed,
        out_specs=(
            P(("dp", "tensor"), None),
            P(("dp", "tensor"), None),
            P(None, "tensor", None),
            P("tensor", None),
            P("tensor", None, None),
            P(None, "tensor"),
            P("tensor"),
            P("tensor", None),
            P(),
            P(),
            P(),
            P(),
            P(),
        ),
        check_vma=False,
    )
```

time: 415 us -> 216 us (0.52)
  waiting for transfers between devices: 169 us -> 58.8 us
  blocking collectives: 90.6 us -> 0 us
  Pallas kernels: 0 us -> 63.1 us
  matrix products: 62.7 us -> 0 us
  starting transfers between devices: 0.2 us -> 53.2 us
  other arithmetic: 35.9 us -> 5.71 us
  loops' own time: 13.4 us -> 0 us
  between operations: 14.3 us -> 1.19 us
  local copies, waits for them, and re-layouts: 27.8 us -> 32.4 us
    psum x2 -> x0, blocking collectives: 90.6 us -> none  [the longest x1 66.5 us: together(): running = lax.psum(jnp.concatenate([a.ravel() for a in arrays]), axis)]
    pallas_call x0 -> x10, Pallas kernels: none -> 63.1 us  [the longest x1 11.6 us: per_device(): launch(project_kernel, 'project', [HALVES, HALVES, whole((4, model)), who...]
    dot_general x40 -> x0, matrix products: 62.7 us -> none  [the longest x8 10.8 us: block_scores(): jnp.einsum('bhe,the->hbt', query_rows, keys_all, preferred_element_type=j...]
    reduce_scatter x2 -> x0, waiting for transfers between devices: 62.1 us -> none  [the longest x1 62.1 us: per_device(): lax.psum_scatter(weighted.astype(jnp.bfloat16), 'tensor', scatter_dimensi...]
    psum x1 -> x0, waiting for transfers between devices: 57.7 us -> none  [per_device(): lax.psum(grad_w_qkv.astype(jnp.bfloat16), 'dp').astype(jnp.float32)]
    all_to_all x0 -> x4, waiting for transfers between devices: none -> 54.8 us  [trade_chips(): lax.all_to_all(blocks, 'tensor', 0, 0, axis_index_groups=SAME_CORE, tiled...]
    all_gather x2 -> x0, waiting for transfers between devices: 47.5 us -> none  [the longest x1 36.2 us: per_device(): lax.all_gather(tokens, 'tensor', axis=0, tiled=True).astype(jnp.float32)]
    ppermute x0 -> x29, starting transfers between devices: none -> 33.6 us  [the longest x15 25 us: move_x(): return lax.ppermute(value, 'dp', pairs)]
  transfers between devices with their start and end apart: 5 -> 33, of which waited for: 4 -> 8; matrix products, arithmetic and copies ran while one was open for 13% -> 2% of each run, Pallas kernels for 0% -> 29%
where the time goes in v2:
time: 216 us; the launch traced here: 214 us
  Pallas kernels  63.1 us (29%)
  waiting for transfers between devices  58.8 us (27%)
  starting transfers between devices  53.2 us (25%)
  local copies, waits for them, and re-layouts  32.4 us (15%)
  other arithmetic  5.71 us (3%)
    all_to_all x4, waiting for transfers between devices, trade_chips(): lax.all_to_all(blocks, 'tensor', 0, 0, axis_index_groups=SAME_CORE, tiled...  54.8 us
    unnamed x130, local copies, waits for them, and re-layouts  27 us
    ppermute x15, starting transfers between devices, move_x(): return lax.ppermute(value, 'dp', pairs)  25 us
    all_to_all x4, starting transfers between devices, trade_chips(): lax.all_to_all(blocks, 'tensor', 0, 0, axis_index_groups=SAME_CORE, tiled...  19.7 us
    pallas_call x1, Pallas kernels, per_device(): launch(project_kernel, 'project', [HALVES, HALVES, whole((4, model)), who...  11.6 us
    pallas_call x1, Pallas kernels, per_device(): launch(attend_back_kernel, 'attend_back', [whole((LEN, HEAD)), whole((LEN...  10.7 us
    pallas_call x1, Pallas kernels, per_device(): launch(feed_back_kernel, 'feed_back', [HALVES, HALVES, by_rows(feed_here)...  10.4 us
    pallas_call x1, Pallas kernels, per_device(): launch(attend_kernel, 'attend', [whole((LEN, HEAD))] * 3, [by_rows(HEAD),...  8.44 us
  transfers between devices with their start and end apart: 33, of which 8 were waited for; matrix products, arithmetic and copies ran while one was open for 2% of the time, Pallas kernels for 29%

profile of v2, /device:TPU:0, one launch (start us, length us, event | category | flops | bytes accessed | tf_op | source)
XLA Modules:
  0.0 214.4 jit_solution(8180884519493457085)
XLA Ops:
  0.6 2.5 %broadcast_in_dim.28 = bf16[8,128,1024]{2,1,0:T(8,128)(2,1)} broadcast(bf16[128,1024]{1,0:T(8,128)(2,1)} %tokens.3), dimensions={1,2} | broadcast | bytes 2359296 | tf_op jit(solution)/shard_map/broadcast_in_dim | solution.py:38
  3.3 6.1 %all-to-all-start = ((bf16[8,128,1024]{2,1,0:T(8,128)(2,1)}), bf16[8,128,1024]{2,1,0:T(8,128)(2,1)}, u32[]{:S(2)}, u32[]{:S(2)}) async-start(bf16[8,128,1024]{2,1,0:T(8,128)(2,1)} %broadcast_in_dim.28), calls=%async_computation | async-start | bytes 4194304 | tf_op jit(solution)/shard_map/all_to_all | solution.py:34
  12.9 27.7 %all-to-all-done.mine = bf16[8,128,1024]{2,1,0:T(8,128)(2,1)} async-done(((bf16[8,128,1024]{2,1,0:T(8,128)(2,1)}), bf16[8,128,1024]{2,1,0:T(8,128)(2,1)}, u32[]{:S(2)}, u32[]{:S(2)}) %all-to-all-start) | async-done | bytes 2097184 | tf_op jit(solution)/shard_map/all_to_all | solution.py:34
  42.2 3.6 %all-to-all-start.1 = ((bf16[8,128,1024]{2,1,0:T(8,128)(2,1)}), bf16[8,128,1024]{2,1,0:T(8,128)(2,1)S(1)}, u32[]{:S(2)}, u32[]{:S(2)}) async-start(bf16[8,128,1024]{2,1,0:T(8,128)(2,1)} %broadcast_in_dim.24), calls=%async_computation.1 | async-start | bytes 4194304 | tf_op jit(solution)/shard_map/all_to_all | solution.py:34
  50.5 11.6 %project.1 = (bf16[2048,1024]{1,0:T(8,128)(2,1)}, bf16[2048,1024]{1,0:T(8,128)(2,1)}, bf16[2048,1024]{1,0:T(8,128)(2,1)}, bf16[2048,64]{1,0:T(8,128)(2,1)S(1)}, ...) custom-call(bf16[8,128,1024]{2,1,0:T(8,128)(2,1)} %all-to-all-done.m, ...), custom_call_target="tpu_custom_call" | custom-call | flops 1 | bytes 1 | tf_op jit(solution)/shard_map/project/pallas_call | solution.py:468
  63.5 8.4 %attend.1 = (bf16[2048,64]{1,0:T(8,128)(2,1)S(1)}, bf16[8,128,64]{2,1,0:T(8,128)(2,1)S(1)}, f32[8,1,256]{2,1,0:T(1,128)S(1)}) custom-call(bf16[2048,64]{1,0:T(8,128)(2,1)S(1)} %get-tuple-element.77.queries, bf16[2048,64]{1,0:T(8,128)(2,1)S(1)} %get-tuple-element.78.keys, bf16[2048,64]{1,0:T(8,128)(2,1)S(1)} %get-tuple-element.79.values), custom_call_target="tpu_custom_call" | custom-call | flops 1 | bytes 1 | tf_op jit(solution)/shard_map/attend/pallas_call | solution.py:488
  75.8 3.0 %mix.1 = bf16[8,128,1024]{2,1,0:T(8,128)(2,1)S(1)} custom-call(s32[1]{0:T(128)} %bitcast.1.core, bf16[8,2,128,64]{3,2,1,0:T(8,128)(2,1)S(1)} %bitcast.28, bf16[8,2,128,256]{3,2,1,0:T(8,128)(2,1)S(1)} %bitcast.21, bf16[8,128,64]{2,1,0:T(8,128)(2,1)S(1)} %collective-permute-done.5.context_in, bf16[8,128,256]{2,1,0:T(8,128)(2,1)S(1)} %collective-permute-done.6.active_in, ...), custom_call_target="tpu_custom_call" | custom-call | flops 1 | bytes 1 | tf_op jit(solution)/shard_map/mix/pallas_call | solution.py:501
  81.3 4.8 %all-to-all-start.2 = ((bf16[8,128,1024]{2,1,0:T(8,128)(2,1)}), bf16[8,128,1024]{2,1,0:T(8,128)(2,1)}, u32[]{:S(2)}, u32[]{:S(2)}) async-start(bf16[8,128,1024]{2,1,0:T(8,128)(2,1)} %copy-done), calls=%async_computation.2 | async-start | bytes 4194304 | tf_op jit(solution)/shard_map/all_to_all | solution.py:34
  90.9 10.4 %feed_back.1 = (bf16[2048,256]{1,0:T(8,128)(2,1)S(1)}, bf16[8,128,256]{2,1,0:T(8,128)(2,1)}, bf16[2048,64]{1,0:T(8,128)(2,1)S(1)}, bf16[528,256]{1,0:T(8,128)(2,...) custom-call(bf16[8,128,1024]{2,1,0:T(8,128)(2,1)S(1)} %all-to-all-do, ...), custom_call_target="tpu_custom_call" | custom-call | flops 1 | bytes 1 | tf_op jit(solution)/shard_map/feed_back/pallas_call | solution.py:523
  103.7 3.0 %collective-permute-start.10 = (bf16[528,256]{1,0:T(8,128)(2,1)}, bf16[528,256]{1,0:T(8,128)(2,1)}, u32[]{:S(2)}, u32[]{:S(2)}) collective-permute-start(bf16[528,256]{1,0:T(8,128)(2,1)} %get-tuple-element.98), channel_id=1, source_target_pairs={{0,64},{16,80},{32,96},{48,112},{64,0},{80,16},{96,32},{112,48},{1... | collective-permute-start | bytes 811016 | tf_op jit(solution)/shard_map/ppermute | solution.py:43
  108.8 10.7 %attend_back.1 = (bf16[2048,192]{1,0:T(8,128)(2,1)S(1)}, bf16[8,128,192]{2,1,0:T(8,128)(2,1)S(1)}) custom-call(bf16[2048,64]{1,0:T(8,128)(2,1)S(1)} %copy-done.19, bf16[2048,64]{1,0:T(8,128)(2,1)S(1)} %copy-done.21, bf16[2048,64]{1,0:T(8,128)(2,1)S(1)} %copy-done.23, bf16[2048,64]{1,0:T(8,128)(2,1)S(1)} %get-tuple-element.91.grad_context, ...), custom_call_target="tpu_custom_call" | custom-call | flops 1 | bytes 1 | tf_op jit(solution)/shard_map/attend_back/pallas_call | solution.py:543
  121.7 3.7 %collective-permute-start.14 = (bf16[528,256]{1,0:T(8,128)(2,1)S(1)}, bf16[528,256]{1,0:T(8,128)(2,1)S(1)}, u32[]{:S(2)}, u32[]{:S(2)}) collective-permute-start(bf16[528,256]{1,0:T(8,128)(2,1)S(1)} %add_convert_fusion.1), channel_id=1, source_target_pairs={{0,16},{16,0},{32,48},{48,32},{64,80},{80,64},{96,112},{112,96},{1... | collective-permute-start | bytes 811016 | tf_op jit(solution)/shard_map/ppermute | solution.py:54
  127.5 2.2 %copy-done.3 = bf16[2048,1024]{1,0:T(8,128)(2,1)S(1)} copy-done((bf16[2048,1024]{1,0:T(8,128)(2,1)S(1)}, bf16[2048,1024]{1,0:T(8,128)(2,1)}, u32[]{:S(2)}) %copy-start.3) | copy-done | bytes 4194328
  131.3 6.1 %last_grads.1 = (bf16[272,256]{1,0:T(8,128)(2,1)S(1)}, bf16[272,256]{1,0:T(8,128)(2,1)S(1)}, bf16[272,256]{1,0:T(8,128)(2,1)S(1)}, bf16[272,256]{1,0:T(8,128)(2,1)S(1)}, f32[5,1024]{1,0:T(8,128)S(1)}) custom-call(bf16[2048,192]{1,0:T(8,128)(2,1)S(1)} %get-tuple-element.101.grad_projected, bf16[2048,256]{1,0:T(8,128)(2,1)S(1)} %copy-done.11, ...), custom_call_target="tpu_custom_call" | custom-call | flops 1 | bytes 1 | tf_op jit(solution)/shard_map/last_grads/pallas_call | solution.py:560
  139.3 2.6 %collective-permute-start.16 = (bf16[272,256]{1,0:T(8,128)(2,1)S(1)}, bf16[272,256]{1,0:T(8,128)(2,1)S(1)}, u32[]{:S(2)}, u32[]{:S(2)}) collective-permute-start(bf16[272,256]{1,0:T(8,128)(2,1)S(1)} %get-tuple-element.117), channel_id=1, source_target_pairs={{0,64},{16,80},{32,96},{48,112},{64,0},{80,16},{96,32},{112,48},{1... | collective-permute-start | bytes 417800 | tf_op jit(solution)/shard_map/ppermute | solution.py:43
  144.2 3.9 %input_back.1 = bf16[8,144,1024]{2,1,0:T(8,128)(2,1)} custom-call(s32[1]{0:T(128)} %bitcast.1.core, bf16[8,2,128,192]{3,2,1,0:T(8,128)(2,1)S(1)} %bitcast.23, bf16[8,2,128,256]{3,2,1,0:T(8,128)(2,1)S(1)} %bitcast.22, bf16[8,128,192]{2,1,0:T(8,128)(2,1)S(1)} %collective-permute-done.12.projected_in, ...), custom_call_target="tpu_custom_call" | custom-call | flops 1 | bytes 1 | tf_op jit(solution)/shard_map/input_back/pallas_call | solution.py:578
  149.4 5.2 %all-to-all-start.3 = ((bf16[8,144,1024]{2,1,0:T(8,128)(2,1)}), bf16[8,144,1024]{2,1,0:T(8,128)(2,1)S(1)}, u32[]{:S(2)}, u32[]{:S(2)}) async-start(bf16[8,144,1024]{2,1,0:T(8,128)(2,1)} %input_back.1), calls=%async_computation.3 | async-start | bytes 4718592 | tf_op jit(solution)/shard_map/all_to_all | solution.py:34
  157.7 2.4 %collective-permute-start.19 = (bf16[528,256]{1,0:T(8,128)(2,1)S(1)}, bf16[528,256]{1,0:T(8,128)(2,1)}, u32[]{:S(2)}, u32[]{:S(2)}) collective-permute-start(bf16[528,256]{1,0:T(8,128)(2,1)S(1)} %copy-done.48), channel_id=1, source_target_pairs={{0,64},{16,80},{32,96},{48,112},{64,0},{80,16},{96,32},{112,48},{1... | collective-permute-start | bytes 811016 | tf_op jit(solution)/shard_map/ppermute | solution.py:43
  161.5 27.1 %all-to-all-done.3.parts = bf16[8,144,1024]{2,1,0:T(8,128)(2,1)S(1)} async-done(((bf16[8,144,1024]{2,1,0:T(8,128)(2,1)}), bf16[8,144,1024]{2,1,0:T(8,128)(2,1)S(1)}, u32[]{:S(2)}, u32[]{:S(2)}) %all-to-all-start.3) | async-done | bytes 2359328 | tf_op jit(solution)/shard_map/all_to_all | solution.py:34
  189.9 3.1 %finish_back.1 = (bf16[128,1024]{1,0:T(8,128)(2,1)}, f32[5,1024]{1,0:T(8,128)}) custom-call(bf16[8,144,1024]{2,1,0:T(8,128)(2,1)} %copy-done.46, bf16[128,1024]{1,0:T(8,128)(2,1)} %tokens.3, bf16[128,1024]{1,0:T(8,128)(2,1)} %cotangent.1), custom_call_target="tpu_custom_call" | custom-call | flops 1 | bytes 1 | tf_op jit(solution)/shard_map/finish_back/pallas_call | solution.py:617
  195.4 2.3 %collective-permute-start.23 = (bf16[272,256]{1,0:T(8,128)(2,1)S(1)}, bf16[272,256]{1,0:T(8,128)(2,1)S(1)}, u32[]{:S(2)}, u32[]{:S(2)}) collective-permute-start(bf16[272,256]{1,0:T(8,128)(2,1)S(1)} %add_convert_fusion.2.head_0), channel_id=1, source_target_pairs={{0,64},{16,80},{32,96},{48,112},{64,0},{80,16},{96,32},{112,48},{1... | collective-permute-start | bytes 417800 | tf_op jit(solution)/shard_map/ppermute | solution.py:43
  202.7 3.2 %collective-permute-start.28 = (f32[5,1024]{1,0:T(8,128)S(1)}, f32[5,1024]{1,0:T(8,128)S(1)}, u32[]{:S(2)}, u32[]{:S(2)}) collective-permute-start(f32[5,1024]{1,0:T(8,128)S(1)} %add.53), channel_id=1, source_target_pairs={{0,96},{16,112},{32,0},{48,16},{64,32},{80,48},{96,64},{112,80},{1... | collective-permute-start | bytes 61448 | tf_op jit(solution)/shard_map/ppermute | solution.py:43
  206.5 2.7 %finish_out.1 = bf16[128,1024]{1,0:T(8,128)(2,1)} custom-call(bf16[8,128,1024]{2,1,0:T(8,128)(2,1)} %all-to-all-done.2.parts, bf16[128,1024]{1,0:T(8,128)(2,1)} %tokens.3, bf16[1,1024]{1,0:T(2,128)(2,1)} %broadcast_in_dim.29.out_bias), custom_call_target="tpu_custom_call" | custom-call | flops 1 | bytes 1 | tf_op jit(solution)/shard_map/finish_out/pallas_call | solution.py:601
  210.5 3.2 %finish_grads.1 = (f32[192,1024]{1,0:T(8,128)}, f32[1,192]{1,0:T(1,128)}, f32[64,1024]{1,0:T(8,128)}, f32[1024,256]{1,0:T(8,128)}, f32[1,256]{1,0:T(1,128)}, /*index=5*/f32[256,1024]{1,0:T(8,128)}) custom-call(bf16[528,256]{1,0:T(8,128)(2,1)} %add_convert_fusion.feed_0, bf16[528,256]{1,0:T(8,128)(2,1)} %copy-done.50, ...), custom_call_target="tpu_custom_call" | custom-call | flops 1 | bytes 1 | tf_op jit(solution)/shard_map/finish_grads/pallas_call | solution.py:607
  (201 shorter events, 53.7 us)
Async XLA Ops:
  3.3 37.3 %all-to-all-start = ((bf16[8,128,1024]{2,1,0:T(8,128)(2,1)}), bf16[8,128,1024]{2,1,0:T(8,128)(2,1)}, u32[]{:S(2)}, u32[]{:S(2)}) async-start(bf16[8,128,1024]{2,1,0:T(8,128)(2,1)} %broadcast_in_dim.28), calls=%async_computation | async-start | bytes 4194304 | tf_op jit(solution)/shard_map/all_to_all | solution.py:34
  42.2 38.7 %all-to-all-start.1 = ((bf16[8,128,1024]{2,1,0:T(8,128)(2,1)}), bf16[8,128,1024]{2,1,0:T(8,128)(2,1)S(1)}, u32[]{:S(2)}, u32[]{:S(2)}) async-start(bf16[8,128,1024]{2,1,0:T(8,128)(2,1)} %broadcast_in_dim.24), calls=%async_computation.1 | async-start | bytes 4194304 | tf_op jit(solution)/shard_map/all_to_all | solution.py:34
  63.4 12.3 %collective-permute-start.6 = (bf16[8,128,256]{2,1,0:T(8,128)(2,1)S(1)}, bf16[8,128,256]{2,1,0:T(8,128)(2,1)S(1)}, u32[]{:S(2)}, u32[]{:S(2)}) collective-permute-start(bf16[8,128,256]{2,1,0:T(8,128)(2,1)S(1)} %get-tuple-element.85), channel_id=1, source_target_pairs={{0,1},{1,0},{2,3},{3,2},{4,5},{5,4},{6,7},{7,6},{8,9},{9,8},{10,11... | collective-permute-start | bytes 1572872 | tf_op jit(solution)/shard_map/ppermute | solution.py:30
  81.3 38.9 %all-to-all-start.2 = ((bf16[8,128,1024]{2,1,0:T(8,128)(2,1)}), bf16[8,128,1024]{2,1,0:T(8,128)(2,1)}, u32[]{:S(2)}, u32[]{:S(2)}) async-start(bf16[8,128,1024]{2,1,0:T(8,128)(2,1)} %copy-done), calls=%async_computation.2 | async-start | bytes 4194304 | tf_op jit(solution)/shard_map/all_to_all | solution.py:34
  103.7 16.6 %collective-permute-start.8 = (bf16[8,128,256]{2,1,0:T(8,128)(2,1)}, bf16[8,128,256]{2,1,0:T(8,128)(2,1)S(1)}, u32[]{:S(2)}, u32[]{:S(2)}) collective-permute-start(bf16[8,128,256]{2,1,0:T(8,128)(2,1)} %get-tuple-element.96), channel_id=1, source_target_pairs={{0,1},{1,0},{2,3},{3,2},{4,5},{5,4},{6,7},{7,6},{8,9},{9,8},{10,11... | collective-permute-start | bytes 1572872 | tf_op jit(solution)/shard_map/ppermute | solution.py:30
  103.7 16.6 %collective-permute-start.10 = (bf16[528,256]{1,0:T(8,128)(2,1)}, bf16[528,256]{1,0:T(8,128)(2,1)}, u32[]{:S(2)}, u32[]{:S(2)}) collective-permute-start(bf16[528,256]{1,0:T(8,128)(2,1)} %get-tuple-element.98), channel_id=1, source_target_pairs={{0,64},{16,80},{32,96},{48,112},{64,0},{80,16},{96,32},{112,48},{1... | collective-permute-start | bytes 811016 | tf_op jit(solution)/shard_map/ppermute | solution.py:43
  106.7 13.6 %collective-permute-start.11 = (bf16[528,256]{1,0:T(8,128)(2,1)}, bf16[528,256]{1,0:T(8,128)(2,1)}, u32[]{:S(2)}, u32[]{:S(2)}) collective-permute-start(bf16[528,256]{1,0:T(8,128)(2,1)} %get-tuple-element.99), channel_id=1, source_target_pairs={{0,96},{16,112},{32,0},{48,16},{64,32},{80,48},{96,64},{112,80},{1... | collective-permute-start | bytes 811016 | tf_op jit(solution)/shard_map/ppermute | solution.py:43
  107.8 12.5 %collective-permute-start.9 = (bf16[528,256]{1,0:T(8,128)(2,1)}, bf16[528,256]{1,0:T(8,128)(2,1)}, u32[]{:S(2)}, u32[]{:S(2)}) collective-permute-start(bf16[528,256]{1,0:T(8,128)(2,1)} %get-tuple-element.97), channel_id=1, source_target_pairs={{0,32},{16,48},{32,64},{48,80},{64,96},{80,112},{96,0},{112,16},{1... | collective-permute-start | bytes 811016 | tf_op jit(solution)/shard_map/ppermute | solution.py:43
  121.7 21.7 %collective-permute-start.14 = (bf16[528,256]{1,0:T(8,128)(2,1)S(1)}, bf16[528,256]{1,0:T(8,128)(2,1)S(1)}, u32[]{:S(2)}, u32[]{:S(2)}) collective-permute-start(bf16[528,256]{1,0:T(8,128)(2,1)S(1)} %add_convert_fusion.1), channel_id=1, source_target_pairs={{0,16},{16,0},{32,48},{48,32},{64,80},{80,64},{96,112},{112,96},{1... | collective-permute-start | bytes 811016 | tf_op jit(solution)/shard_map/ppermute | solution.py:54
  125.3 18.9 %collective-permute-start.12 = (bf16[8,128,192]{2,1,0:T(8,128)(2,1)}, bf16[8,128,192]{2,1,0:T(8,128)(2,1)S(1)}, u32[]{:S(2)}, u32[]{:S(2)}) collective-permute-start(bf16[8,128,192]{2,1,0:T(8,128)(2,1)} %copy-done.45), channel_id=1, source_target_pairs={{0,1},{1,0},{2,3},{3,2},{4,5},{5,4},{6,7},{7,6},{8,9},{9,8},{10,11... | collective-permute-start | bytes 1179656 | tf_op jit(solution)/shard_map/ppermute | solution.py:30
  137.9 10.2 %collective-permute-start.15 = (bf16[272,256]{1,0:T(8,128)(2,1)S(1)}, bf16[272,256]{1,0:T(8,128)(2,1)S(1)}, u32[]{:S(2)}, u32[]{:S(2)}) collective-permute-start(bf16[272,256]{1,0:T(8,128)(2,1)S(1)} %get-tuple-element.116), channel_id=1, source_target_pairs={{0,32},{16,48},{32,64},{48,80},{64,96},{80,112},{96,0},{112,16},{1... | collective-permute-start | bytes 417800 | tf_op jit(solution)/shard_map/ppermute | solution.py:43
  139.3 9.2 %collective-permute-start.16 = (bf16[272,256]{1,0:T(8,128)(2,1)S(1)}, bf16[272,256]{1,0:T(8,128)(2,1)S(1)}, u32[]{:S(2)}, u32[]{:S(2)}) collective-permute-start(bf16[272,256]{1,0:T(8,128)(2,1)S(1)} %get-tuple-element.117), channel_id=1, source_target_pairs={{0,64},{16,80},{32,96},{48,112},{64,0},{80,16},{96,32},{112,48},{1... | collective-permute-start | bytes 417800 | tf_op jit(solution)/shard_map/ppermute | solution.py:43
  142.0 7.5 %collective-permute-start.17 = (bf16[272,256]{1,0:T(8,128)(2,1)S(1)}, bf16[272,256]{1,0:T(8,128)(2,1)}, u32[]{:S(2)}, u32[]{:S(2)}) collective-permute-start(bf16[272,256]{1,0:T(8,128)(2,1)S(1)} %get-tuple-element.118), channel_id=1, source_target_pairs={{0,96},{16,112},{32,0},{48,16},{64,32},{80,48},{96,64},{112,80},{1... | collective-permute-start | bytes 417800 | tf_op jit(solution)/shard_map/ppermute | solution.py:43
  149.4 39.1 %all-to-all-start.3 = ((bf16[8,144,1024]{2,1,0:T(8,128)(2,1)}), bf16[8,144,1024]{2,1,0:T(8,128)(2,1)S(1)}, u32[]{:S(2)}, u32[]{:S(2)}) async-start(bf16[8,144,1024]{2,1,0:T(8,128)(2,1)} %input_back.1), calls=%async_computation.3 | async-start | bytes 4718592 | tf_op jit(solution)/shard_map/all_to_all | solution.py:34
  155.7 38.6 %collective-permute-start.21 = (bf16[272,256]{1,0:T(8,128)(2,1)S(1)}, bf16[272,256]{1,0:T(8,128)(2,1)S(1)}, u32[]{:S(2)}, u32[]{:S(2)}) collective-permute-start(bf16[272,256]{1,0:T(8,128)(2,1)S(1)} %add_convert_fusion.3), channel_id=1, source_target_pairs={{0,16},{16,0},{32,48},{48,32},{64,80},{80,64},{96,112},{112,96},{1... | collective-permute-start | bytes 417800 | tf_op jit(solution)/shard_map/ppermute | solution.py:54
  156.9 38.5 %collective-permute-start.18 = (bf16[528,256]{1,0:T(8,128)(2,1)S(1)}, bf16[528,256]{1,0:T(8,128)(2,1)S(1)}, u32[]{:S(2)}, u32[]{:S(2)}) collective-permute-start(bf16[528,256]{1,0:T(8,128)(2,1)S(1)} %copy-done.48), channel_id=1, source_target_pairs={{0,32},{16,48},{32,64},{48,80},{64,96},{80,112},{96,0},{112,16},{1... | collective-permute-start | bytes 811016 | tf_op jit(solution)/shard_map/ppermute | solution.py:43
  157.7 43.7 %collective-permute-start.19 = (bf16[528,256]{1,0:T(8,128)(2,1)S(1)}, bf16[528,256]{1,0:T(8,128)(2,1)}, u32[]{:S(2)}, u32[]{:S(2)}) collective-permute-start(bf16[528,256]{1,0:T(8,128)(2,1)S(1)} %copy-done.48), channel_id=1, source_target_pairs={{0,64},{16,80},{32,96},{48,112},{64,0},{80,16},{96,32},{112,48},{1... | collective-permute-start | bytes 811016 | tf_op jit(solution)/shard_map/ppermute | solution.py:43
  160.0 42.6 %collective-permute-start.20 = (bf16[528,256]{1,0:T(8,128)(2,1)S(1)}, bf16[528,256]{1,0:T(8,128)(2,1)}, u32[]{:S(2)}, u32[]{:S(2)}) collective-permute-start(bf16[528,256]{1,0:T(8,128)(2,1)S(1)} %copy-done.48), channel_id=1, source_target_pairs={{0,96},{16,112},{32,0},{48,16},{64,32},{80,48},{96,64},{112,80},{1... | collective-permute-start | bytes 811016 | tf_op jit(solution)/shard_map/ppermute | solution.py:43
  194.3 8.4 %collective-permute-start.22 = (bf16[272,256]{1,0:T(8,128)(2,1)S(1)}, bf16[272,256]{1,0:T(8,128)(2,1)S(1)}, u32[]{:S(2)}, u32[]{:S(2)}) collective-permute-start(bf16[272,256]{1,0:T(8,128)(2,1)S(1)} %add_convert_fusion.2.head_0), channel_id=1, source_target_pairs={{0,32},{16,48},{32,64},{48,80},{64,96},{80,112},{96,0},{112,16},{1... | collective-permute-start | bytes 417800 | tf_op jit(solution)/shard_map/ppermute | solution.py:43
  195.4 13.8 %collective-permute-start.23 = (bf16[272,256]{1,0:T(8,128)(2,1)S(1)}, bf16[272,256]{1,0:T(8,128)(2,1)S(1)}, u32[]{:S(2)}, u32[]{:S(2)}) collective-permute-start(bf16[272,256]{1,0:T(8,128)(2,1)S(1)} %add_convert_fusion.2.head_0), channel_id=1, source_target_pairs={{0,64},{16,80},{32,96},{48,112},{64,0},{80,16},{96,32},{112,48},{1... | collective-permute-start | bytes 417800 | tf_op jit(solution)/shard_map/ppermute | solution.py:43
  198.7 10.5 %collective-permute-start.24 = (bf16[272,256]{1,0:T(8,128)(2,1)S(1)}, bf16[272,256]{1,0:T(8,128)(2,1)S(1)}, u32[]{:S(2)}, u32[]{:S(2)}) collective-permute-start(bf16[272,256]{1,0:T(8,128)(2,1)S(1)} %add_convert_fusion.2.head_0), channel_id=1, source_target_pairs={{0,96},{16,112},{32,0},{48,16},{64,32},{80,48},{96,64},{112,80},{1... | collective-permute-start | bytes 417800 | tf_op jit(solution)/shard_map/ppermute | solution.py:43
  201.3 12.4 %collective-permute-start.26 = (f32[5,1024]{1,0:T(8,128)S(1)}, f32[5,1024]{1,0:T(8,128)S(1)}, u32[]{:S(2)}, u32[]{:S(2)}) collective-permute-start(f32[5,1024]{1,0:T(8,128)S(1)} %add.53), channel_id=1, source_target_pairs={{0,64},{16,80},{32,96},{48,112},{64,0},{80,16},{96,32},{112,48},{1... | collective-permute-start | bytes 61448 | tf_op jit(solution)/shard_map/ppermute | solution.py:43
  202.6 11.1 %collective-permute-start.27 = (f32[5,1024]{1,0:T(8,128)S(1)}, f32[5,1024]{1,0:T(8,128)S(1)}, u32[]{:S(2)}, u32[]{:S(2)}) collective-permute-start(f32[5,1024]{1,0:T(8,128)S(1)} %add.53), channel_id=1, source_target_pairs={{0,32},{16,48},{32,64},{48,80},{64,96},{80,112},{96,0},{112,16},{1... | collective-permute-start | bytes 61448 | tf_op jit(solution)/shard_map/ppermute | solution.py:43
  202.7 11.1 %collective-permute-start.28 = (f32[5,1024]{1,0:T(8,128)S(1)}, f32[5,1024]{1,0:T(8,128)S(1)}, u32[]{:S(2)}, u32[]{:S(2)}) collective-permute-start(f32[5,1024]{1,0:T(8,128)S(1)} %add.53), channel_id=1, source_target_pairs={{0,96},{16,112},{32,0},{48,16},{64,32},{80,48},{96,64},{112,80},{1... | collective-permute-start | bytes 61448 | tf_op jit(solution)/shard_map/ppermute | solution.py:43
  (74 other events, 630.8 us)

commit v3 on v2

v3 whole, which is shorter than its diff:
```python
from functools import partial

import jax
import jax.numpy as jnp
import numpy as np
from jax import lax
from jax.experimental import pallas as pl
from jax.experimental.pallas import tpu as pltpu
from jax.sharding import PartitionSpec as P

ROT = 16
LEN = 2048
EPS = 1e-05
HEAD = 64
ROWS = 256
STEPS = LEN // ROWS
HALF = ROWS // 2
SCALE = HEAD ** (-0.5)
EXTRA = 16

SAME_CORE = [[c + 2 * i for i in range(8)] for c in range(2)]
PAIR = [(i, i ^ 1) for i in range(16)]
Z_PAIR = [(i, i ^ 1) for i in range(8)]

F32 = jnp.float32
LOW = jnp.bfloat16


def swap_core(value):
    return lax.ppermute(value, "tensor", PAIR)


def trade_chips(blocks):
    return lax.all_to_all(blocks, "tensor", 0, 0, axis_index_groups=SAME_CORE, tiled=True)


def copies(block, count):
    return jnp.broadcast_to(block[None], (count,) + block.shape)


def move_x(value, distance):
    pairs = [(i, (i // 2 + distance) % 4 * 2 + i % 2) for i in range(8)]
    return lax.ppermute(value, "dp", pairs)


def add_four(own, moved):
    total = own.astype(F32)
    for part in moved:
        total = total + part.astype(F32)
    return total.astype(LOW)


def add_low(left, right):
    return (left.astype(F32) + right.astype(F32)).astype(LOW)


def sum_z(low):
    return add_low(low, lax.ppermute(low, "dp", Z_PAIR))


def spread_x(low):
    return [low] + [move_x(low, distance) for distance in range(1, 4)]


def sum_four(rows, move):
    return (rows + move(rows, 2)) + (move(rows, 1) + move(rows, 3))


def normalize(values):
    center = values - jnp.mean(values, axis=-1, keepdims=True)
    inverse = lax.rsqrt(jnp.mean(center * center, axis=-1, keepdims=True) + EPS)
    return (center * inverse, inverse)


def norm_back(scaled, normalized, inverse):
    centered = scaled - jnp.mean(scaled, axis=-1, keepdims=True)
    return inverse * (centered - normalized * jnp.mean(scaled * normalized, axis=-1, keepdims=True))


def rotary_tables():
    lane = np.arange(2 * HEAD) % HEAD
    half = ROT // 2
    inverse = np.float32(10000.0) ** (-2.0 * (lane % half).astype(np.float32) / np.float32(ROT))
    inverse = np.where(lane < ROT, inverse, 0.0).astype(np.float32)
    angles = np.arange(LEN, dtype=np.float32)[:, None] * inverse[None, :]
    sign = np.where(lane < half, -1.0, 1.0).astype(np.float32)
    return np.cos(angles).astype(np.float32), (np.sin(angles) * sign).astype(np.float32)


def turn(values, cosine, sine):
    lane = lax.broadcasted_iota(jnp.int32, values.shape, 1) % HEAD
    partner = jnp.where(
        lane < ROT // 2,
        pltpu.roll(values, 2 * HEAD - ROT // 2, 1),
        pltpu.roll(values, ROT // 2, 1),
    )
    return values * cosine + partner * sine


def dot(left, right, left_axis=1, right_axis=0):
    return lax.dot_general(
        left,
        right,
        (((left_axis,), (right_axis,)), ((), ())),
        preferred_element_type=F32,
    )


def core_here():
    return lax.axis_index("tensor") % 2


def stream(count, moves):
    step = pl.program_id(0)

    @pl.when(step == 0)
    def _():
        for place in range(count):
            for move in moves:
                move(place).start()

    for move in moves:
        move(step).wait()


def fetch(source, target, done):
    def move(place):
        return pltpu.make_async_copy(source(place), target(place), done.at[place])

    return move


def fetch_rows(source, target, done):
    return fetch(
        lambda place: source.at[pl.ds(place * ROWS, ROWS)], lambda place: target.at[place], done
    )


def fetch_parity(source, target, done):
    core = core_here()
    return fetch(
        lambda place: source.at[pl.ds(place * 2, 2), core], lambda place: target.at[place], done
    )


def fetch_double(source, target, done):
    return fetch(
        lambda place: source.at[pl.ds(place * 2, 2)], lambda place: target.at[place], done
    )


def fetch_joined(source, target, done, core):
    start = pl.multiple_of(core * HALF, HALF)
    return fetch(
        lambda place: source.at[place],
        lambda place: target.at[place, pl.ds(start, HALF)],
        done,
    )


def send_rows(block, send):
    core = core_here()
    send[0] = block[pl.ds(pl.multiple_of((1 - core) * HALF, HALF), HALF), :]


def x_here():
    return lax.axis_index("dp") // 2


def row_sum(values):
    return jnp.sum(values, axis=0, keepdims=True)


def forward_kernel(
    mine, other, vecs, w_qkv, b_qkv, w_up, b_up, cosine, sine,
    first, second, normal, queries, keys, values, active, active_send, slope,
    context, context_send, mass, rows, mine_done, other_done,
):
    core = core_here()
    stream(
        STEPS,
        [
            fetch_joined(mine, rows, mine_done, core),
            fetch_joined(other, rows, other_done, 1 - core),
        ],
    )
    step = pl.program_id(0)
    for part in range(0, ROWS, 32):
        span = slice(part, part + 32)
        here = rows[step, span, :].astype(F32)
        center = here - jnp.mean(here, axis=-1, keepdims=True)
        inverse = lax.rsqrt(jnp.mean(center * center, axis=-1, keepdims=True) + EPS)
        normalized = center * inverse
        normal[span, :] = normalized.astype(LOW)
        first[span, :] = (normalized * vecs[0:1, :] + vecs[1:2, :]).astype(LOW)
        second[span, :] = (normalized * vecs[2:3, :] + vecs[3:4, :]).astype(LOW)
    projected = dot(first[...], w_qkv[...], 1, 1) + b_qkv[...]
    turned = turn(projected[:, : 2 * HEAD], cosine[...], sine[...])
    here = pl.ds(pl.multiple_of(step * ROWS, ROWS), ROWS)
    queries[here, :] = turned[:, :HEAD].astype(LOW) * SCALE
    keys[here, :] = turned[:, HEAD:].astype(LOW)
    values[here, :] = projected[:, 2 * HEAD :].astype(LOW)
    for part in range(0, ROWS, 64):
        span = slice(part, part + 64)
        hidden = dot(second[span, :], w_up[...]) + b_up[...]
        share = 0.5 * (1.0 + lax.erf(hidden * (0.5**0.5)))
        active[span, :] = (hidden * share).astype(LOW)
        bell = jnp.exp(-0.5 * hidden * hidden) * ((2.0 * np.pi) ** -0.5)
        slope[span, :] = share + hidden * bell
    send_rows(active, active_send)

    place = lax.broadcasted_iota(jnp.int32, (ROWS, ROWS), 0)
    query = lax.broadcasted_iota(jnp.int32, (ROWS, ROWS), 1)
    seen = place <= query

    def block(index):
        low, high = index * ROWS, (index + 1) * ROWS
        asked = queries[low:high, :]
        near = jnp.where(seen, dot(keys[low:high, :], asked, 1, 1), -1e30)
        top = jnp.max(near, axis=0, keepdims=True)
        if index:
            far = dot(keys[:low, :], asked, 1, 1)
            top = jnp.maximum(top, jnp.max(far, axis=0, keepdims=True))
            far = jnp.exp(far - top)
        near = jnp.exp(near - top)
        total = row_sum(near)
        if index:
            total = total + row_sum(far)
        scale = 1.0 / total
        mass[0] = top + jnp.log(total)
        found = dot(values[low:high, :], (near * scale).astype(LOW), 0, 0)
        if index:
            found = found + dot(values[:low, :], (far * scale).astype(LOW), 0, 0)
        context[...] = found.T.astype(LOW)

    for index in range(STEPS):
        pl.when(step == index)(partial(block, index))
    send_rows(context, context_send)


def flat(block):
    return block.reshape(ROWS, block.shape[-1])


def mix_kernel(
    context, active, context_in, active_in, w_out, w_down, w_out_in, w_down_in, result,
    context_rows, active_rows, context_other, active_other, *done,
):
    stream(
        4,
        [
            fetch_parity(context, context_rows, done[0]),
            fetch_parity(active, active_rows, done[1]),
            fetch_double(context_in, context_other, done[2]),
            fetch_double(active_in, active_other, done[3]),
        ],
    )
    step = pl.program_id(0)
    mixed = dot(flat(context_rows[step]), w_out[...])
    mixed = mixed + dot(flat(active_rows[step]), w_down[...])
    mixed = mixed + dot(flat(context_other[step]), w_out_in[...])
    mixed = mixed + dot(flat(active_other[step]), w_down_in[...])
    result[...] = mixed.astype(LOW).reshape(2, HALF, mixed.shape[1])


def feed_back_kernel(
    mine, other, active, slope, second, context, w_down, w_out,
    grad_hidden, hidden_send, grad_context, feed_0, feed_1, feed_2, feed_3, grad_out,
    rows, active_rows, slope_rows, second_rows, up_sum, down_sum, out_sum, bias_sum, *done,
):
    step = pl.program_id(0)
    core = core_here()
    stream(
        STEPS,
        [
            fetch_joined(mine, rows, done[0], core),
            fetch_joined(other, rows, done[1], 1 - core),
            fetch_rows(active, active_rows, done[2]),
            fetch_rows(slope, slope_rows, done[3]),
            fetch_rows(second, second_rows, done[4]),
        ],
    )

    @pl.when(step == 0)
    def _():
        up_sum[...] = jnp.zeros_like(up_sum)
        down_sum[...] = jnp.zeros_like(down_sum)
        out_sum[...] = jnp.zeros_like(out_sum)
        bias_sum[...] = jnp.zeros_like(bias_sum)

    grads = rows[step]
    hidden = (dot(grads, w_down[...], 1, 1) * slope_rows[step]).astype(LOW)
    grad_hidden[...] = hidden
    send_rows(grad_hidden, hidden_send)
    grad_context[...] = dot(grads, w_out[...], 1, 1).astype(LOW)
    down_sum[...] += dot(active_rows[step], grads, 0, 0)
    out_sum[...] += dot(context[...], grads, 0, 0)
    up_sum[...] += dot(hidden, second_rows[step], 0, 0)
    bias_sum[...] += row_sum(hidden.astype(F32))

    @pl.when(step == STEPS - 1)
    def _():
        grad_out[...] = out_sum[...].astype(LOW)
        for slot, feed in enumerate((feed_0, feed_1, feed_2, feed_3)):
            span = quarter((x_here() + slot) % 4)
            feed[0:256, :] = up_sum[:, span].T.astype(LOW)
            feed[256:512, :] = down_sum[:, span].astype(LOW)
            feed[512:528, :] = jnp.broadcast_to(bias_sum[...], (16, 256)).astype(LOW)


def quarter(part):
    return pl.ds(pl.multiple_of(part * 256, 256), 256)


def attend_back_kernel(
    queries, keys, values, grad_context, mass, cosine, sine, grad_hidden, normal, w_qkv, w_up,
    own_sum, grad_projected, projected_send, sums, bias, query_sum, key_sum, value_sum,
    moments, hidden_rows, normal_rows, *done,
):
    stream(
        STEPS,
        [
            fetch_rows(grad_hidden, hidden_rows, done[0]),
            fetch_rows(normal, normal_rows, done[1]),
        ],
    )
    wide = 3 * HEAD
    place = lax.broadcasted_iota(jnp.int32, (ROWS, ROWS), 0)
    query = lax.broadcasted_iota(jnp.int32, (ROWS, ROWS), 1)
    seen = place <= query

    @pl.when(pl.program_id(0) == 0)
    def _():
        key_sum[...] = jnp.zeros_like(key_sum)
        value_sum[...] = jnp.zeros_like(value_sum)

    def block(index):
        low, high = index * ROWS, (index + 1) * ROWS
        asked = queries[low:high, :]
        grads = grad_context[...]
        spans = [slice(low, high)] + ([slice(0, low)] if index else [])
        weights, pulls = [], []
        inner = 0.0
        for number, span in enumerate(spans):
            scores = dot(keys[span, :], asked, 1, 1)
            if number == 0:
                scores = jnp.where(seen, scores, -1e30)
            weight = jnp.exp(scores - mass[0])
            pull = dot(values[span, :], grads, 1, 1)
            inner = inner + row_sum(weight * pull)
            weights.append(weight)
            pulls.append(pull)
        asked_grad = 0.0
        for span, weight, pull in zip(spans, weights, pulls):
            value_sum[span, :] += dot(weight.astype(LOW), grads)
            scores_grad = (weight * (pull - inner)).astype(LOW)
            key_sum[span, :] += dot(scores_grad, asked)
            asked_grad = asked_grad + dot(keys[span, :], scores_grad, 0, 0)
        query_sum[low:high, :] = asked_grad.T * SCALE

    for index in range(STEPS):
        pl.when(pl.program_id(0) == index)(partial(block, index))

    @pl.when(pl.program_id(0) == STEPS - 1)
    def _():
        for index in range(STEPS):
            span = slice(index * ROWS, (index + 1) * ROWS)
            both = jnp.concatenate([query_sum[span, :], key_sum[span, :]], axis=1)
            turned = turn(both, cosine[span, :], -sine[span, :])
            grad_projected[span, : 2 * HEAD] = turned.astype(LOW)
            grad_projected[span, 2 * HEAD :] = value_sum[span, :].astype(LOW)
            place = index * ROWS + (1 - core_here()) * HALF
            projected_send[index] = grad_projected[pl.ds(pl.multiple_of(place, HALF), HALF), :]
        hidden_bias, bias_here = 0.0, 0.0
        for index in range(STEPS):
            span = slice(index * ROWS, (index + 1) * ROWS)
            grads = grad_projected[span, :]
            hidden = hidden_rows[index]
            both = [dot(grads, normal_rows[index], 0, 0), dot(hidden, normal_rows[index], 0, 0)]
            if index:
                moments[0:wide, :] += both[0]
                moments[wide:, :] += both[1]
            else:
                moments[0:wide, :] = both[0]
                moments[wide:, :] = both[1]
            bias_here = bias_here + row_sum(grads.astype(F32))
            hidden_bias = hidden_bias + row_sum(hidden.astype(F32))
        bias[...] = bias_here
        sums[0:1, :] = row_sum(moments[0:wide, :] * w_qkv[...].astype(F32))
        sums[1:2, :] = dot_full(bias_here, w_qkv[...], 0)
        sums[2:3, :] = row_sum(moments[wide:, :] * w_up[...].astype(F32).T)
        sums[3:4, :] = dot_full(hidden_bias, w_up[...], 1)
        sums[4:5, :] = own_sum[...]


def input_back_kernel(
    projected, hidden, projected_in, hidden_in, vecs, w_qkv, w_up, w_qkv_in, w_up_in, sums,
    result, projected_rows, hidden_rows, projected_other, hidden_other, *done,
):
    stream(
        4,
        [
            fetch_parity(projected, projected_rows, done[0]),
            fetch_parity(hidden, hidden_rows, done[1]),
            fetch_double(projected_in, projected_other, done[2]),
            fetch_double(hidden_in, hidden_other, done[3]),
        ],
    )
    step = pl.program_id(0)
    one = dot(flat(projected_rows[step]), w_qkv[...])
    one = one + dot(flat(projected_other[step]), w_qkv_in[...])
    two = dot(flat(hidden_rows[step]), w_up[...], 1, 1)
    two = two + dot(flat(hidden_other[step]), w_up_in[...], 1, 1)
    weighted = one * vecs[0:1, :] + two * vecs[2:3, :]
    result[:, 0:HALF, :] = weighted.astype(LOW).reshape(2, HALF, weighted.shape[1])
    high = sums[...].astype(LOW).astype(F32)
    rest = jnp.zeros((EXTRA - 10, weighted.shape[1]), F32)
    tail = jnp.concatenate([high, sums[...] - high, rest], axis=0).astype(LOW)
    result[0, HALF:, :] = tail
    result[1, HALF:, :] = tail


def dot_full(left, right, right_axis):
    return lax.dot_general(
        left,
        right.astype(F32),
        (((1,), (right_axis,)), ((), ())),
        precision=lax.Precision.HIGHEST,
        preferred_element_type=F32,
    )


def qkv_grad_kernel(
    grad_projected, first, grad_out, bias, head_0, head_1, head_2, head_3, qkv_sum,
    first_rows, done,
):
    step = pl.program_id(0)
    wide = 3 * HEAD
    stream(STEPS, [fetch_rows(first, first_rows, done)])

    @pl.when(step == 0)
    def _():
        qkv_sum[...] = jnp.zeros_like(qkv_sum)

    qkv_sum[...] += dot(grad_projected[...], first_rows[step], 0, 0)

    @pl.when(step == STEPS - 1)
    def _():
        for slot, head in enumerate((head_0, head_1, head_2, head_3)):
            span = quarter((x_here() + slot) % 4)
            head[0:wide, :] = qkv_sum[:, span].astype(LOW)
            head[wide:256, :] = grad_out[:, span]
            head[256:272, :wide] = jnp.broadcast_to(bias[...], (16, wide)).astype(LOW)
            head[256:272, wide:] = jnp.zeros((16, 256 - wide), LOW)


def small_kernel(parts, sums):
    tail = jnp.sum(parts[...].astype(F32), axis=0)
    sums[...] = tail[0:5] + tail[5:10]


def finish_grads_kernel(
    feed_0, feed_1, feed_2, feed_3, head_0, head_1, head_2, head_3,
    grad_qkv, grad_qkv_bias, grad_out, grad_up, grad_up_bias, grad_down,
):
    wide = 3 * HEAD
    for slot, feed in enumerate((feed_0, feed_1, feed_2, feed_3)):
        span = quarter((x_here() + 4 - slot) % 4)
        grad_up[span, :] = feed[0:256, :].astype(F32)
        grad_down[:, span] = feed[256:512, :].astype(F32)
    for slot, head in enumerate((head_0, head_1, head_2, head_3)):
        span = quarter((x_here() + 4 - slot) % 4)
        grad_qkv[:, span] = head[0:wide, :].astype(F32)
        grad_out[:, span] = head[wide:256, :].astype(F32)
    grad_up_bias[...] = feed_0[512:513, :].astype(F32)
    grad_qkv_bias[...] = head_0[256:257, :wide].astype(F32)


def finish_out_kernel(parts, tokens, out_bias, layer_out):
    total = jnp.sum(parts[...].astype(F32), axis=0)
    layer_out[...] = (tokens[...].astype(F32) + total + out_bias[...].astype(F32)).astype(LOW)


def finish_back_kernel(parts, tokens, cotangent, input_grad):
    scaled = jnp.sum(parts[:, 0:HALF, :].astype(F32), axis=0)
    normalized, inverse = normalize(tokens[...].astype(F32))
    input_grad[...] = (
        cotangent[...].astype(F32) + norm_back(scaled, normalized, inverse)
    ).astype(LOW)


def arrivals(count):
    return pltpu.SemaphoreType.DMA((count,))


def whole(shape):
    return pl.BlockSpec(shape, lambda step: (0,) * len(shape))


def by_rows(columns):
    return pl.BlockSpec((ROWS, columns), lambda step: (step, 0))


LEFT = pl.BlockSpec(memory_space=pltpu.HBM)
MASS = pl.BlockSpec((1, 1, ROWS), lambda step: (step, 0, 0))


def shape(dims, kind):
    return jax.ShapeDtypeStruct(dims, kind)


COST = pl.CostEstimate(flops=1, bytes_accessed=1, transcendentals=0)


def left(dims, kind):
    return pltpu.HBM(dims, kind)


def launch(kernel, name, ins, outs, out_shapes, scratch, steps=STEPS, room=60):
    return pl.pallas_call(
        kernel,
        name=name,
        grid=(steps,),
        in_specs=ins,
        out_specs=outs,
        scratch_shapes=scratch,
        out_shape=out_shapes,
        compiler_params=pltpu.CompilerParams(vmem_limit_bytes=room * 2**20),
        cost_estimate=COST,
    )


def half_rows(columns):
    return pl.BlockSpec((1, HALF, columns), lambda step: (step, 0, 0))


def four(value):
    return value.reshape(STEPS, 2, HALF, value.shape[1])


def per_device(
    tokens, w_qkv, b_qkv, w_out, w_up, b_up, w_down, out_bias,
    ln1_gain, ln1_shift, ln2_gain, ln2_shift, cotangent,
):
    model = w_up.shape[0]
    feed_here = w_up.shape[1]
    wide = 3 * HEAD
    w_qkv = w_qkv.transpose(1, 2, 0).reshape(wide, model)
    w_out = w_out.reshape(HEAD, model)
    vecs = jnp.stack([ln1_gain, ln1_shift, ln2_gain, ln2_shift]).astype(F32)
    cosine, sine = rotary_tables()
    own_sum = jnp.sum(cotangent.astype(F32), axis=0)[None, :]

    held = copies(cotangent, 8)
    mine = trade_chips(copies(tokens, 8))
    weights_in = [swap_core(w) for w in (w_out, w_down, w_qkv, w_up)]
    held, vecs, b_qkv, b_up, own_sum, mine, *weights_in = lax.optimization_barrier(
        (held, vecs, b_qkv.astype(F32), b_up.astype(F32)[None, :], own_sum, mine)
        + tuple(weights_in)
    )
    w_out_in, w_down_in, w_qkv_in, w_up_in = weights_in
    other = swap_core(mine)
    grad_mine = trade_chips(held)

    halves = shape((STEPS, HALF, feed_here), LOW)
    (
        first, second, normal, queries, keys, values, active, active_send, slope,
        context, context_send, mass,
    ) = launch(
        forward_kernel,
        "forward",
        [
            LEFT, LEFT, whole((4, model)), whole((wide, model)), whole((1, wide)),
            whole((model, feed_here)), whole((1, feed_here)), by_rows(128), by_rows(128),
        ],
        [
            by_rows(model), by_rows(model), by_rows(model), whole((LEN, HEAD)),
            whole((LEN, HEAD)), whole((LEN, HEAD)), by_rows(feed_here), half_rows(feed_here),
            by_rows(feed_here), by_rows(HEAD), half_rows(HEAD), MASS,
        ],
        [
            left((LEN, model), LOW), left((LEN, model), LOW), left((LEN, model), LOW),
            shape((LEN, HEAD), LOW), shape((LEN, HEAD), LOW), shape((LEN, HEAD), LOW),
            left((LEN, feed_here), LOW), halves, left((LEN, feed_here), F32),
            shape((LEN, HEAD), LOW), shape((STEPS, HALF, HEAD), LOW),
            shape((STEPS, 1, ROWS), F32),
        ],
        [pltpu.VMEM((STEPS, ROWS, model), LOW), arrivals(STEPS), arrivals(STEPS)],
    )(mine, other, vecs, w_qkv, b_qkv, w_up, b_up, cosine, sine)
    active_in = swap_core(active_send)
    context_in = swap_core(context_send)

    mixed = launch(
        mix_kernel,
        "mix",
        [LEFT] * 4 + [whole((HEAD, model)), whole((feed_here, model))] * 2,
        pl.BlockSpec((2, HALF, model), lambda step: (step, 0, 0)),
        left((STEPS, HALF, model), LOW),
        [pltpu.VMEM((4, 2, HALF, HEAD), LOW), pltpu.VMEM((4, 2, HALF, feed_here), LOW)] * 2
        + [arrivals(4)] * 4,
        steps=4,
    )(four(context), four(active), context_in, active_in, w_out, w_down, w_out_in, w_down_in)

    grad_mine, mixed = lax.optimization_barrier((grad_mine, mixed))
    grad_other = swap_core(grad_mine)
    branch = trade_chips(mixed)

    grad_hidden, hidden_send, grad_context, *feed, grad_out = launch(
        feed_back_kernel,
        "feed_back",
        [
            LEFT, LEFT, LEFT, LEFT, LEFT,
            by_rows(HEAD), whole((feed_here, model)), whole((HEAD, model)),
        ],
        [by_rows(feed_here), half_rows(feed_here), by_rows(HEAD)]
        + [whole((528, 256))] * 4 + [whole((HEAD, model))],
        [shape((LEN, feed_here), LOW), halves, shape((LEN, HEAD), LOW)]
        + [shape((528, 256), LOW)] * 4 + [shape((HEAD, model), LOW)],
        [
            pltpu.VMEM((STEPS, ROWS, model), LOW), pltpu.VMEM((STEPS, ROWS, feed_here), LOW),
            pltpu.VMEM((STEPS, ROWS, feed_here), F32), pltpu.VMEM((STEPS, ROWS, model), LOW),
            pltpu.VMEM((feed_here, model), F32), pltpu.VMEM((feed_here, model), F32),
            pltpu.VMEM((HEAD, model), F32), pltpu.VMEM((1, feed_here), F32),
        ]
        + [arrivals(STEPS)] * 5,
    )(grad_mine, grad_other, active, slope, second, context, w_down, w_out)
    hidden_in = swap_core(hidden_send)
    feed_moved = [move_x(feed[distance], distance) for distance in range(1, 4)]

    grad_projected, projected_send, sums, bias = launch(
        attend_back_kernel,
        "attend_back",
        [
            whole((LEN, HEAD)), whole((LEN, HEAD)), whole((LEN, HEAD)), by_rows(HEAD), MASS,
            whole((LEN, 128)), whole((LEN, 128)), LEFT, LEFT, whole((wide, model)),
            whole((model, feed_here)), whole((1, model)),
        ],
        [whole((LEN, wide)), whole((STEPS, HALF, wide)), whole((5, model)), whole((1, wide))],
        [
            shape((LEN, wide), LOW), shape((STEPS, HALF, wide), LOW), shape((5, model), F32),
            shape((1, wide), F32),
        ],
        [pltpu.VMEM((LEN, HEAD), F32)] * 3
        + [
            pltpu.VMEM((wide + feed_here, model), F32),
            pltpu.VMEM((STEPS, ROWS, feed_here), LOW), pltpu.VMEM((STEPS, ROWS, model), LOW),
        ]
        + [arrivals(STEPS)] * 2,
    )(
        queries, keys, values, grad_context, mass, cosine, sine, grad_hidden, normal,
        w_qkv, w_up, own_sum,
    )
    sums = sums + swap_core(sums)
    grad_projected, projected_send, branch, hidden_in, *feed_moved = lax.optimization_barrier(
        (grad_projected, projected_send, branch, hidden_in, *feed_moved)
    )
    projected_in = swap_core(projected_send)
    feed_half = add_four(feed[0], feed_moved)
    feed_other = lax.ppermute(feed_half, "dp", Z_PAIR)

    both = launch(
        input_back_kernel,
        "input_back",
        [LEFT] * 4 + [whole((4, model))] + [whole((wide, model)), whole((model, feed_here))] * 2
        + [whole((5, model))],
        pl.BlockSpec((2, HALF + EXTRA, model), lambda step: (step, 0, 0)),
        left((STEPS, HALF + EXTRA, model), LOW),
        [pltpu.VMEM((4, 2, HALF, wide), LOW), pltpu.VMEM((4, 2, HALF, feed_here), LOW)] * 2
        + [arrivals(4)] * 4,
        steps=4,
    )(
        four(grad_projected), four(grad_hidden), projected_in, hidden_in, vecs,
        w_qkv, w_up, w_qkv_in, w_up_in, sums,
    )
    both, grad_projected, feed_other = lax.optimization_barrier(
        (both, grad_projected, feed_other)
    )
    feed_low = add_low(feed_half, feed_other)
    scaled = trade_chips(both)
    head = launch(
        qkv_grad_kernel,
        "qkv_grad",
        [by_rows(wide), LEFT, whole((HEAD, model)), whole((1, wide))],
        [whole((272, 256))] * 4,
        [shape((272, 256), LOW)] * 4,
        [
            pltpu.VMEM((wide, model), F32), pltpu.VMEM((STEPS, ROWS, model), LOW),
            arrivals(STEPS),
        ],
        room=40,
    )(grad_projected, first, grad_out, bias)
    head_moved = [move_x(head[distance], distance) for distance in range(1, 4)]
    head_low = sum_z(add_four(head[0], head_moved))
    feed_parts = spread_x(feed_low)
    head_parts = spread_x(head_low)

    layer_out = pl.pallas_call(
        finish_out_kernel,
        name="finish_out",
        out_shape=shape(tokens.shape, LOW),
        cost_estimate=COST,
    )(branch, tokens, out_bias[None, :])
    scaled, layer_out, *parts = lax.optimization_barrier(
        (scaled, layer_out, *feed_parts, *head_parts)
    )
    small = pl.pallas_call(
        small_kernel,
        name="small",
        grid=(1,),
        in_specs=[pl.BlockSpec((STEPS, EXTRA, model), lambda step: (0, HALF // EXTRA, 0))],
        out_specs=whole((5, model)),
        out_shape=shape((5, model), F32),
        cost_estimate=COST,
    )(scaled)
    small_moved = lax.ppermute(small, "dp", Z_PAIR)
    input_grad = pl.pallas_call(
        finish_back_kernel,
        name="finish_back",
        grid=(1,),
        in_specs=[
            whole((STEPS, HALF, model)), whole(tokens.shape), whole(tokens.shape),
        ],
        out_specs=whole(tokens.shape),
        out_shape=shape(tokens.shape, LOW),
        cost_estimate=COST,
    )(scaled, tokens, cotangent)
    small_moved, input_grad = lax.optimization_barrier((small_moved, input_grad))
    grad_qkv, grad_qkv_bias, grad_out, grad_up, grad_up_bias, grad_down = pl.pallas_call(
        finish_grads_kernel,
        name="finish_grads",
        out_shape=[
            shape((wide, model), F32), shape((1, wide), F32), shape((HEAD, model), F32),
            shape((model, feed_here), F32), shape((1, feed_here), F32),
            shape((feed_here, model), F32),
        ],
        cost_estimate=COST,
    )(*parts)
    small = sum_four(small + small_moved, move_x)

    return (
        layer_out,
        input_grad,
        grad_qkv.reshape(1, wide, model).transpose(2, 0, 1),
        grad_qkv_bias,
        grad_out.reshape(1, HEAD, model),
        grad_up,
        grad_up_bias[0],
        grad_down,
        small[4],
        small[0],
        small[1],
        small[2],
        small[3],
    )


def solution(mesh):
    placed = (
        P(("dp", "tensor"), None),
        P(None, "tensor", None),
        P("tensor", None),
        P("tensor", None, None),
        P(None, "tensor"),
        P("tensor"),
        P("tensor", None),
        P(),
        P(),
        P(),
        P(),
        P(),
        P(("dp", "tensor"), None),
    )
    return jax.shard_map(
        per_device,
        mesh=mesh,
        in_specs=placed,
        out_specs=(
            P(("dp", "tensor"), None),
            P(("dp", "tensor"), None),
            P(None, "tensor", None),
            P("tensor", None),
            P("tensor", None, None),
            P(None, "tensor"),
            P("tensor"),
            P("tensor", None),
            P(),
            P(),
            P(),
            P(),
            P(),
        ),
        check_vma=False,
    )
```

time: 216 us -> 200 us (0.926)
  local copies, waits for them, and re-layouts: 32.4 us -> 12.1 us
  Pallas kernels: 63.1 us -> 78.6 us
  waiting for transfers between devices: 58.8 us -> 49.8 us
  starting transfers between devices: 53.2 us -> 50.1 us
    all_to_all x4, waiting for transfers between devices: 54.8 us -> 28.3 us  [trade_chips(): lax.all_to_all(blocks, 'tensor', 0, 0, axis_index_groups=SAME_CORE, tiled...]
    unnamed x130 -> x70, local copies, waits for them, and re-layouts: 27 us -> 6.71 us
    ppermute x15, waiting for transfers between devices: 0.55 us -> 9.02 us  [move_x(): return lax.ppermute(value, 'dp', pairs)]
    pallas_call x1, Pallas kernels: 10.7 us -> 18.7 us  [per_device(): launch(attend_back_kernel, 'attend_back', [whole((LEN, HEAD)), whole((LEN...]
    pallas_call x7, Pallas kernels: 46.5 us -> 54 us  [the longest x1 21 us: per_device(): launch(forward_kernel, 'forward', [LEFT, LEFT, whole((4, model)), whole((...]
    ppermute x3, waiting for transfers between devices: 0.97 us -> 8.42 us  [the longest x1 8.15 us: sum_z(): return add_low(low, lax.ppermute(low, 'dp', Z_PAIR))]
    ppermute x15, starting transfers between devices: 25 us -> 21.3 us  [move_x(): return lax.ppermute(value, 'dp', pairs)]
  transfers between devices with their start and end apart: 33 -> 33, of which waited for: 8 -> 11; matrix products, arithmetic and copies ran while one was open for 2% -> 3% of each run, Pallas kernels for 29% -> 39%
where the time goes in v3:
time: 200 us; the launch traced here: 197 us
  Pallas kernels  78.6 us (39%)
  starting transfers between devices  50.1 us (25%)
  waiting for transfers between devices  49.8 us (25%)
  local copies, waits for them, and re-layouts  12.1 us (6%)
  other arithmetic  5.08 us (3%)
    all_to_all x4, waiting for transfers between devices, trade_chips(): lax.all_to_all(blocks, 'tensor', 0, 0, axis_index_groups=SAME_CORE, tiled...  28.3 us
    ppermute x15, starting transfers between devices, move_x(): return lax.ppermute(value, 'dp', pairs)  21.3 us
    pallas_call x1, Pallas kernels, per_device(): launch(forward_kernel, 'forward', [LEFT, LEFT, whole((4, model)), whole((...  21 us
    all_to_all x4, starting transfers between devices, trade_chips(): lax.all_to_all(blocks, 'tensor', 0, 0, axis_index_groups=SAME_CORE, tiled...  19.1 us
    pallas_call x1, Pallas kernels, per_device(): launch(attend_back_kernel, 'attend_back', [whole((LEN, HEAD)), whole((LEN...  18.7 us
    pallas_call x1, Pallas kernels, per_device(): launch(feed_back_kernel, 'feed_back', [LEFT, LEFT, LEFT, LEFT, LEFT, by_r...  12.7 us
    ppermute x15, waiting for transfers between devices, move_x(): return lax.ppermute(value, 'dp', pairs)  9.02 us
    ppermute x1, waiting for transfers between devices, sum_z(): return add_low(low, lax.ppermute(low, 'dp', Z_PAIR))  8.15 us
  transfers between devices with their start and end apart: 33, of which 11 were waited for; matrix products, arithmetic and copies ran while one was open for 3% of the time, Pallas kernels for 39%

profile of v3, /device:TPU:0, one launch (start us, length us, event | category | flops | bytes accessed | tf_op | source)
XLA Modules:
  0.0 196.9 jit_solution(7395168253347332954)
XLA Ops:
  0.6 2.5 %broadcast_in_dim.28 = bf16[8,128,1024]{2,1,0:T(8,128)(2,1)} broadcast(bf16[128,1024]{1,0:T(8,128)(2,1)} %tokens.3), dimensions={1,2} | broadcast | bytes 2359296 | tf_op jit(solution)/shard_map/broadcast_in_dim | solution.py:38
  3.3 6.1 %all-to-all-start = ((bf16[8,128,1024]{2,1,0:T(8,128)(2,1)}), bf16[8,128,1024]{2,1,0:T(8,128)(2,1)}, u32[]{:S(2)}, u32[]{:S(2)}) async-start(bf16[8,128,1024]{2,1,0:T(8,128)(2,1)} %broadcast_in_dim.28), calls=%async_computation | async-start | bytes 4194304 | tf_op jit(solution)/shard_map/all_to_all | solution.py:34
  13.0 27.6 %all-to-all-done.mine = bf16[8,128,1024]{2,1,0:T(8,128)(2,1)} async-done(((bf16[8,128,1024]{2,1,0:T(8,128)(2,1)}), bf16[8,128,1024]{2,1,0:T(8,128)(2,1)}, u32[]{:S(2)}, u32[]{:S(2)}) %all-to-all-start) | async-done | bytes 2097184 | tf_op jit(solution)/shard_map/all_to_all | solution.py:34
  42.2 3.6 %all-to-all-start.1 = ((bf16[8,128,1024]{2,1,0:T(8,128)(2,1)}), bf16[8,128,1024]{2,1,0:T(8,128)(2,1)S(1)}, u32[]{:S(2)}, u32[]{:S(2)}) async-start(bf16[8,128,1024]{2,1,0:T(8,128)(2,1)} %broadcast_in_dim.24), calls=%async_computation.1 | async-start | bytes 4194304 | tf_op jit(solution)/shard_map/all_to_all | solution.py:34
  46.7 21.0 %forward.1 = (bf16[2048,1024]{1,0:T(8,128)(2,1)}, bf16[2048,1024]{1,0:T(8,128)(2,1)}, bf16[2048,1024]{1,0:T(8,128)(2,1)}, bf16[2048,64]{1,0:T(8,128)(2,1)}, bf16...) custom-call(bf16[8,128,1024]{2,1,0:T(8,128)(2,1)} %all-to-all-done.m, ...), custom_call_target="tpu_custom_call" | custom-call | flops 1 | bytes 1 | tf_op jit(solution)/shard_map/forward/pallas_call | solution.py:569
  71.2 6.3 %mix.1 = bf16[8,128,1024]{2,1,0:T(8,128)(2,1)} custom-call(bf16[8,2,128,64]{3,2,1,0:T(8,128)(2,1)} %bitcast.27, bf16[8,2,128,256]{3,2,1,0:T(8,128)(2,1)} %bitcast.21, bf16[8,128,64]{2,1,0:T(8,128)(2,1)} %copy-done.24, bf16[8,128,256]{2,1,0:T(8,128)(2,1)} %copy-done.19, bf16[64,1024]{1,0:T(8,128)(2,1)} %bitcast.28, bf16[256,1024]{1,0:T(8,128)(2,1)} %w_down.3, ...), custom_call_target="tpu_custom_call" | custom-call | flops 1 | bytes 1 | tf_op jit(solution)/shard_map/mix/pallas_call | solution.py:593
  79.5 4.3 %all-to-all-start.2 = ((bf16[8,128,1024]{2,1,0:T(8,128)(2,1)}), bf16[8,128,1024]{2,1,0:T(8,128)(2,1)}, u32[]{:S(2)}, u32[]{:S(2)}) async-start(bf16[8,128,1024]{2,1,0:T(8,128)(2,1)} %mix.1), calls=%async_computation.2 | async-start | bytes 4194304 | tf_op jit(solution)/shard_map/all_to_all | solution.py:34
  83.9 12.7 %feed_back.1 = (bf16[2048,256]{1,0:T(8,128)(2,1)}, bf16[8,128,256]{2,1,0:T(8,128)(2,1)}, bf16[2048,64]{1,0:T(8,128)(2,1)}, bf16[528,256]{1,0:T(8,128)(2,1)}, bf1...) custom-call(bf16[8,128,1024]{2,1,0:T(8,128)(2,1)} %copy-done.5, ...), custom_call_target="tpu_custom_call" | custom-call | flops 1 | bytes 1 | tf_op jit(solution)/shard_map/feed_back/pallas_call | solution.py:608
  96.6 3.3 %collective-permute-start.10 = (bf16[528,256]{1,0:T(8,128)(2,1)}, bf16[528,256]{1,0:T(8,128)(2,1)S(1)}, u32[]{:S(2)}, u32[]{:S(2)}) collective-permute-start(bf16[528,256]{1,0:T(8,128)(2,1)} %get-tuple-element.108), channel_id=1, source_target_pairs={{0,64},{16,80},{32,96},{48,112},{64,0},{80,16},{96,32},{112,48},{1... | collective-permute-start | bytes 811016 | tf_op jit(solution)/shard_map/ppermute | solution.py:43
  102.0 18.7 %attend_back.1 = (bf16[2048,192]{1,0:T(8,128)(2,1)}, bf16[8,128,192]{2,1,0:T(8,128)(2,1)}, f32[5,1024]{1,0:T(8,128)}, f32[1,192]{1,0:T(1,128)}) custom-call(bf16[2048,64]{1,0:T(8,128)(2,1)} %get-tuple-element.85.queries, bf16[2048,64]{1,0:T(8,128)(2,1)} %get-tuple-element.86.keys, bf16[2048,64]{1,0:T(8,128)(2,1)} %get-tuple-element.87.values, ...), custom_call_target="tpu_custom_call" | custom-call | flops 1 | bytes 1 | tf_op jit(solution)/shard_map/attend_back/pallas_call | solution.py:630
  121.2 3.7 %collective-permute-start.14 = (bf16[528,256]{1,0:T(8,128)(2,1)S(1)}, bf16[528,256]{1,0:T(8,128)(2,1)}, u32[]{:S(2)}, u32[]{:S(2)}) collective-permute-start(bf16[528,256]{1,0:T(8,128)(2,1)S(1)} %add_convert_fusion.1), channel_id=1, source_target_pairs={{0,16},{16,0},{32,48},{48,32},{64,80},{80,64},{96,112},{112,96},{1... | collective-permute-start | bytes 811016 | tf_op jit(solution)/shard_map/ppermute | solution.py:659
  128.4 6.5 %input_back.1 = bf16[8,144,1024]{2,1,0:T(8,128)(2,1)} custom-call(bf16[8,2,128,192]{3,2,1,0:T(8,128)(2,1)} %bitcast.20, bf16[8,2,128,256]{3,2,1,0:T(8,128)(2,1)} %bitcast.22, bf16[8,128,192]{2,1,0:T(8,128)(2,1)} %copy-done.17, bf16[8,128,256]{2,1,0:T(8,128)(2,1)} %copy-done.16, f32[4,1024]{1,0:T(4,128)} %maximum_convert_fusion.vecs, ...), custom_call_target="tpu_custom_call" | custom-call | flops 1 | bytes 1 | tf_op jit(solution)/shard_map/input_back/pallas_call | solution.py:661
  135.0 5.1 %all-to-all-start.3 = ((bf16[8,144,1024]{2,1,0:T(8,128)(2,1)}), bf16[8,144,1024]{2,1,0:T(8,128)(2,1)S(1)}, u32[]{:S(2)}, u32[]{:S(2)}) async-start(bf16[8,144,1024]{2,1,0:T(8,128)(2,1)} %input_back.1), calls=%async_computation.3 | async-start | bytes 4718592 | tf_op jit(solution)/shard_map/all_to_all | solution.py:34
  142.4 2.9 %qkv_grad.1 = (bf16[272,256]{1,0:T(8,128)(2,1)S(1)}, bf16[272,256]{1,0:T(8,128)(2,1)S(1)}, bf16[272,256]{1,0:T(8,128)(2,1)S(1)}, bf16[272,256]{1,0:T(8,128)(2,1)S(1)}) custom-call(bf16[2048,192]{1,0:T(8,128)(2,1)S(1)} %copy-done.1, bf16[2048,1024]{1,0:T(8,128)(2,1)S(1)} %copy-done, bf16[64,1024]{1,0:T(8,128)(2,1)S(1)} %copy-done.2, f32[1,192]{1,0:T(1,128)S(1)} %copy-done.3), custom_call_target="tpu_custom_call" | custom-call | flops 1 | bytes 1 | tf_op jit(solution)/shard_map/qkv_grad/pallas_call | solution.py:680
  145.9 3.2 %collective-permute-start.19 = (bf16[272,256]{1,0:T(8,128)(2,1)S(1)}, bf16[272,256]{1,0:T(8,128)(2,1)S(1)}, u32[]{:S(2)}, u32[]{:S(2)}) collective-permute-start(bf16[272,256]{1,0:T(8,128)(2,1)S(1)} %get-tuple-element.129), channel_id=1, source_target_pairs={{0,64},{16,80},{32,96},{48,112},{64,0},{80,16},{96,32},{112,48},{1... | collective-permute-start | bytes 417800 | tf_op jit(solution)/shard_map/ppermute | solution.py:43
  149.2 3.4 %collective-permute-done.18 = bf16[272,256]{1,0:T(8,128)(2,1)S(1)} collective-permute-done((bf16[272,256]{1,0:T(8,128)(2,1)S(1)}, bf16[272,256]{1,0:T(8,128)(2,1)S(1)}, u32[]{:S(2)}, u32[]{:S(2)}) %collective-permute-start.18) | collective-permute-done | bytes 139296 | tf_op jit(solution)/shard_map/ppermute | solution.py:43
  152.5 3.1 %collective-permute-done.19 = bf16[272,256]{1,0:T(8,128)(2,1)S(1)} collective-permute-done((bf16[272,256]{1,0:T(8,128)(2,1)S(1)}, bf16[272,256]{1,0:T(8,128)(2,1)S(1)}, u32[]{:S(2)}, u32[]{:S(2)}) %collective-permute-start.19) | collective-permute-done | bytes 139296 | tf_op jit(solution)/shard_map/ppermute | solution.py:43
  158.5 3.7 %collective-permute-start.16 = (bf16[528,256]{1,0:T(8,128)(2,1)S(1)}, bf16[528,256]{1,0:T(8,128)(2,1)S(1)}, u32[]{:S(2)}, u32[]{:S(2)}) collective-permute-start(bf16[528,256]{1,0:T(8,128)(2,1)S(1)} %add_convert_fusion.feed_0), channel_id=1, source_target_pairs={{0,64},{16,80},{32,96},{48,112},{64,0},{80,16},{96,32},{112,48},{1... | collective-permute-start | bytes 811016 | tf_op jit(solution)/shard_map/ppermute | solution.py:43
  162.2 8.1 %collective-permute-done.21 = bf16[272,256]{1,0:T(8,128)(2,1)S(1)} collective-permute-done((bf16[272,256]{1,0:T(8,128)(2,1)S(1)}, bf16[272,256]{1,0:T(8,128)(2,1)S(1)}, u32[]{:S(2)}, u32[]{:S(2)}) %collective-permute-start.21) | collective-permute-done | bytes 139296 | tf_op jit(solution)/shard_map/ppermute | solution.py:58
  171.1 3.2 %collective-permute-start.23 = (bf16[272,256]{1,0:T(8,128)(2,1)S(1)}, bf16[272,256]{1,0:T(8,128)(2,1)}, u32[]{:S(2)}, u32[]{:S(2)}) collective-permute-start(bf16[272,256]{1,0:T(8,128)(2,1)S(1)} %add_convert_fusion.2.head_0), channel_id=1, source_target_pairs={{0,64},{16,80},{32,96},{48,112},{64,0},{80,16},{96,32},{112,48},{1... | collective-permute-start | bytes 417800 | tf_op jit(solution)/shard_map/ppermute | solution.py:43
  174.9 2.7 %finish_out.1 = bf16[128,1024]{1,0:T(8,128)(2,1)} custom-call(bf16[8,128,1024]{2,1,0:T(8,128)(2,1)} %all-to-all-done.2.parts, bf16[128,1024]{1,0:T(8,128)(2,1)} %tokens.3, bf16[1,1024]{1,0:T(2,128)(2,1)} %broadcast_in_dim.29.out_bias), custom_call_target="tpu_custom_call" | custom-call | flops 1 | bytes 1 | tf_op jit(solution)/shard_map/finish_out/pallas_call | solution.py:697
  183.2 2.4 %collective-permute-start.25 = (f32[5,1024]{1,0:T(8,128)}, f32[5,1024]{1,0:T(8,128)S(1)}, u32[]{:S(2)}, u32[]{:S(2)}) collective-permute-start(f32[5,1024]{1,0:T(8,128)} %small.1), channel_id=1, source_target_pairs={{0,16},{16,0},{32,48},{48,32},{64,80},{80,64},{96,112},{112,96},{1... | collective-permute-start | bytes 61448 | tf_op jit(solution)/shard_map/ppermute | solution.py:715
  185.7 3.0 %finish_back.1 = bf16[128,1024]{1,0:T(8,128)(2,1)} custom-call(bf16[8,144,1024]{2,1,0:T(8,128)(2,1)} %copy-done.4, bf16[128,1024]{1,0:T(8,128)(2,1)} %tokens.3, bf16[128,1024]{1,0:T(8,128)(2,1)} %cotangent.1), custom_call_target="tpu_custom_call" | custom-call | flops 1 | bytes 1 | tf_op jit(solution)/shard_map/finish_back/pallas_call | solution.py:716
  193.0 3.2 %finish_grads.1 = (f32[192,1024]{1,0:T(8,128)}, f32[1,192]{1,0:T(1,128)}, f32[64,1024]{1,0:T(8,128)}, f32[1024,256]{1,0:T(8,128)}, f32[1,256]{1,0:T(1,128)}, /*index=5*/f32[256,1024]{1,0:T(8,128)}) custom-call(bf16[528,256]{1,0:T(8,128)(2,1)} %copy-done.10, bf16[528,256]{1,0:T(8,128)(2,1)} %copy-done.21, bf16[528,256]{1,0:T(8,128)(2,1)} %copy-done.22, ...), custom_call_target="tpu_custom_call" | custom-call | flops 1 | bytes 1 | tf_op jit(solution)/shard_map/finish_grads/pallas_call | solution.py:728
  (141 shorter events, 35.3 us)
Async XLA Ops:
  3.3 37.3 %all-to-all-start = ((bf16[8,128,1024]{2,1,0:T(8,128)(2,1)}), bf16[8,128,1024]{2,1,0:T(8,128)(2,1)}, u32[]{:S(2)}, u32[]{:S(2)}) async-start(bf16[8,128,1024]{2,1,0:T(8,128)(2,1)} %broadcast_in_dim.28), calls=%async_computation | async-start | bytes 4194304 | tf_op jit(solution)/shard_map/all_to_all | solution.py:34
  42.2 35.9 %all-to-all-start.1 = ((bf16[8,128,1024]{2,1,0:T(8,128)(2,1)}), bf16[8,128,1024]{2,1,0:T(8,128)(2,1)S(1)}, u32[]{:S(2)}, u32[]{:S(2)}) async-start(bf16[8,128,1024]{2,1,0:T(8,128)(2,1)} %broadcast_in_dim.24), calls=%async_computation.1 | async-start | bytes 4194304 | tf_op jit(solution)/shard_map/all_to_all | solution.py:34
  78.2 5.7 %collective-permute-start.7 = (bf16[8,128,1024]{2,1,0:T(8,128)(2,1)S(1)}, bf16[8,128,1024]{2,1,0:T(8,128)(2,1)}, u32[]{:S(2)}, u32[]{:S(2)}) collective-permute-start(bf16[8,128,1024]{2,1,0:T(8,128)(2,1)S(1)} %all-to-all-done.1.mine), channel_id=1, source_target_pairs={{0,1},{1,0},{2,3},{3,2},{4,5},{5,4},{6,7},{7,6},{8,9},{9,8},{10,11... | collective-permute-start | bytes 6291464 | tf_op jit(solution)/shard_map/ppermute | solution.py:30
  79.5 41.1 %all-to-all-start.2 = ((bf16[8,128,1024]{2,1,0:T(8,128)(2,1)}), bf16[8,128,1024]{2,1,0:T(8,128)(2,1)}, u32[]{:S(2)}, u32[]{:S(2)}) async-start(bf16[8,128,1024]{2,1,0:T(8,128)(2,1)} %mix.1), calls=%async_computation.2 | async-start | bytes 4194304 | tf_op jit(solution)/shard_map/all_to_all | solution.py:34
  96.6 24.1 %collective-permute-start.8 = (bf16[8,128,256]{2,1,0:T(8,128)(2,1)}, bf16[8,128,256]{2,1,0:T(8,128)(2,1)S(1)}, u32[]{:S(2)}, u32[]{:S(2)}) collective-permute-start(bf16[8,128,256]{2,1,0:T(8,128)(2,1)} %get-tuple-element.106), channel_id=1, source_target_pairs={{0,1},{1,0},{2,3},{3,2},{4,5},{5,4},{6,7},{7,6},{8,9},{9,8},{10,11... | collective-permute-start | bytes 1572872 | tf_op jit(solution)/shard_map/ppermute | solution.py:30
  96.6 24.0 %collective-permute-start.10 = (bf16[528,256]{1,0:T(8,128)(2,1)}, bf16[528,256]{1,0:T(8,128)(2,1)S(1)}, u32[]{:S(2)}, u32[]{:S(2)}) collective-permute-start(bf16[528,256]{1,0:T(8,128)(2,1)} %get-tuple-element.108), channel_id=1, source_target_pairs={{0,64},{16,80},{32,96},{48,112},{64,0},{80,16},{96,32},{112,48},{1... | collective-permute-start | bytes 811016 | tf_op jit(solution)/shard_map/ppermute | solution.py:43
  99.9 20.7 %collective-permute-start.11 = (bf16[528,256]{1,0:T(8,128)(2,1)}, bf16[528,256]{1,0:T(8,128)(2,1)S(1)}, u32[]{:S(2)}, u32[]{:S(2)}) collective-permute-start(bf16[528,256]{1,0:T(8,128)(2,1)} %get-tuple-element.109), channel_id=1, source_target_pairs={{0,96},{16,112},{32,0},{48,16},{64,32},{80,48},{96,64},{112,80},{1... | collective-permute-start | bytes 811016 | tf_op jit(solution)/shard_map/ppermute | solution.py:43
  101.1 19.6 %collective-permute-start.9 = (bf16[528,256]{1,0:T(8,128)(2,1)}, bf16[528,256]{1,0:T(8,128)(2,1)S(1)}, u32[]{:S(2)}, u32[]{:S(2)}) collective-permute-start(bf16[528,256]{1,0:T(8,128)(2,1)} %get-tuple-element.107), channel_id=1, source_target_pairs={{0,32},{16,48},{32,64},{48,80},{64,96},{80,112},{96,0},{112,16},{1... | collective-permute-start | bytes 811016 | tf_op jit(solution)/shard_map/ppermute | solution.py:43
  120.7 7.0 %collective-permute-start.12 = (bf16[8,128,192]{2,1,0:T(8,128)(2,1)}, bf16[8,128,192]{2,1,0:T(8,128)(2,1)S(1)}, u32[]{:S(2)}, u32[]{:S(2)}) collective-permute-start(bf16[8,128,192]{2,1,0:T(8,128)(2,1)} %get-tuple-element.111), channel_id=1, source_target_pairs={{0,1},{1,0},{2,3},{3,2},{4,5},{5,4},{6,7},{7,6},{8,9},{9,8},{10,11... | collective-permute-start | bytes 1179656 | tf_op jit(solution)/shard_map/ppermute | solution.py:30
  121.2 13.9 %collective-permute-start.14 = (bf16[528,256]{1,0:T(8,128)(2,1)S(1)}, bf16[528,256]{1,0:T(8,128)(2,1)}, u32[]{:S(2)}, u32[]{:S(2)}) collective-permute-start(bf16[528,256]{1,0:T(8,128)(2,1)S(1)} %add_convert_fusion.1), channel_id=1, source_target_pairs={{0,16},{16,0},{32,48},{48,32},{64,80},{80,64},{96,112},{112,96},{1... | collective-permute-start | bytes 811016 | tf_op jit(solution)/shard_map/ppermute | solution.py:659
  135.0 45.2 %all-to-all-start.3 = ((bf16[8,144,1024]{2,1,0:T(8,128)(2,1)}), bf16[8,144,1024]{2,1,0:T(8,128)(2,1)S(1)}, u32[]{:S(2)}, u32[]{:S(2)}) async-start(bf16[8,144,1024]{2,1,0:T(8,128)(2,1)} %input_back.1), calls=%async_computation.3 | async-start | bytes 4718592 | tf_op jit(solution)/shard_map/all_to_all | solution.py:34
  145.3 7.3 %collective-permute-start.18 = (bf16[272,256]{1,0:T(8,128)(2,1)S(1)}, bf16[272,256]{1,0:T(8,128)(2,1)S(1)}, u32[]{:S(2)}, u32[]{:S(2)}) collective-permute-start(bf16[272,256]{1,0:T(8,128)(2,1)S(1)} %get-tuple-element.128), channel_id=1, source_target_pairs={{0,32},{16,48},{32,64},{48,80},{64,96},{80,112},{96,0},{112,16},{1... | collective-permute-start | bytes 417800 | tf_op jit(solution)/shard_map/ppermute | solution.py:43
  145.9 9.7 %collective-permute-start.19 = (bf16[272,256]{1,0:T(8,128)(2,1)S(1)}, bf16[272,256]{1,0:T(8,128)(2,1)S(1)}, u32[]{:S(2)}, u32[]{:S(2)}) collective-permute-start(bf16[272,256]{1,0:T(8,128)(2,1)S(1)} %get-tuple-element.129), channel_id=1, source_target_pairs={{0,64},{16,80},{32,96},{48,112},{64,0},{80,16},{96,32},{112,48},{1... | collective-permute-start | bytes 417800 | tf_op jit(solution)/shard_map/ppermute | solution.py:43
  149.1 6.5 %collective-permute-start.20 = (bf16[272,256]{1,0:T(8,128)(2,1)S(1)}, bf16[272,256]{1,0:T(8,128)(2,1)S(1)}, u32[]{:S(2)}, u32[]{:S(2)}) collective-permute-start(bf16[272,256]{1,0:T(8,128)(2,1)S(1)} %get-tuple-element.130), channel_id=1, source_target_pairs={{0,96},{16,112},{32,0},{48,16},{64,32},{80,48},{96,64},{112,80},{1... | collective-permute-start | bytes 417800 | tf_op jit(solution)/shard_map/ppermute | solution.py:43
  155.7 14.6 %collective-permute-start.21 = (bf16[272,256]{1,0:T(8,128)(2,1)S(1)}, bf16[272,256]{1,0:T(8,128)(2,1)S(1)}, u32[]{:S(2)}, u32[]{:S(2)}) collective-permute-start(bf16[272,256]{1,0:T(8,128)(2,1)S(1)} %add_convert_fusion.3), channel_id=1, source_target_pairs={{0,16},{16,0},{32,48},{48,32},{64,80},{80,64},{96,112},{112,96},{1... | collective-permute-start | bytes 417800 | tf_op jit(solution)/shard_map/ppermute | solution.py:58
  158.0 16.3 %collective-permute-start.15 = (bf16[528,256]{1,0:T(8,128)(2,1)S(1)}, bf16[528,256]{1,0:T(8,128)(2,1)S(1)}, u32[]{:S(2)}, u32[]{:S(2)}) collective-permute-start(bf16[528,256]{1,0:T(8,128)(2,1)S(1)} %add_convert_fusion.feed_0), channel_id=1, source_target_pairs={{0,32},{16,48},{32,64},{48,80},{64,96},{80,112},{96,0},{112,16},{1... | collective-permute-start | bytes 811016 | tf_op jit(solution)/shard_map/ppermute | solution.py:43
  158.5 19.2 %collective-permute-start.16 = (bf16[528,256]{1,0:T(8,128)(2,1)S(1)}, bf16[528,256]{1,0:T(8,128)(2,1)S(1)}, u32[]{:S(2)}, u32[]{:S(2)}) collective-permute-start(bf16[528,256]{1,0:T(8,128)(2,1)S(1)} %add_convert_fusion.feed_0), channel_id=1, source_target_pairs={{0,64},{16,80},{32,96},{48,112},{64,0},{80,16},{96,32},{112,48},{1... | collective-permute-start | bytes 811016 | tf_op jit(solution)/shard_map/ppermute | solution.py:43
  162.2 15.5 %collective-permute-start.17 = (bf16[528,256]{1,0:T(8,128)(2,1)S(1)}, bf16[528,256]{1,0:T(8,128)(2,1)}, u32[]{:S(2)}, u32[]{:S(2)}) collective-permute-start(bf16[528,256]{1,0:T(8,128)(2,1)S(1)} %add_convert_fusion.feed_0), channel_id=1, source_target_pairs={{0,96},{16,112},{32,0},{48,16},{64,32},{80,48},{96,64},{112,80},{1... | collective-permute-start | bytes 811016 | tf_op jit(solution)/shard_map/ppermute | solution.py:43
  170.4 7.9 %collective-permute-start.22 = (bf16[272,256]{1,0:T(8,128)(2,1)S(1)}, bf16[272,256]{1,0:T(8,128)(2,1)S(1)}, u32[]{:S(2)}, u32[]{:S(2)}) collective-permute-start(bf16[272,256]{1,0:T(8,128)(2,1)S(1)} %add_convert_fusion.2.head_0), channel_id=1, source_target_pairs={{0,32},{16,48},{32,64},{48,80},{64,96},{80,112},{96,0},{112,16},{1... | collective-permute-start | bytes 417800 | tf_op jit(solution)/shard_map/ppermute | solution.py:43
  171.1 9.1 %collective-permute-start.23 = (bf16[272,256]{1,0:T(8,128)(2,1)S(1)}, bf16[272,256]{1,0:T(8,128)(2,1)}, u32[]{:S(2)}, u32[]{:S(2)}) collective-permute-start(bf16[272,256]{1,0:T(8,128)(2,1)S(1)} %add_convert_fusion.2.head_0), channel_id=1, source_target_pairs={{0,64},{16,80},{32,96},{48,112},{64,0},{80,16},{96,32},{112,48},{1... | collective-permute-start | bytes 417800 | tf_op jit(solution)/shard_map/ppermute | solution.py:43
  174.3 5.9 %collective-permute-start.24 = (bf16[272,256]{1,0:T(8,128)(2,1)S(1)}, bf16[272,256]{1,0:T(8,128)(2,1)}, u32[]{:S(2)}, u32[]{:S(2)}) collective-permute-start(bf16[272,256]{1,0:T(8,128)(2,1)S(1)} %add_convert_fusion.2.head_0), channel_id=1, source_target_pairs={{0,96},{16,112},{32,0},{48,16},{64,32},{80,48},{96,64},{112,80},{1... | collective-permute-start | bytes 417800 | tf_op jit(solution)/shard_map/ppermute | solution.py:43
  183.2 5.7 %collective-permute-start.25 = (f32[5,1024]{1,0:T(8,128)}, f32[5,1024]{1,0:T(8,128)S(1)}, u32[]{:S(2)}, u32[]{:S(2)}) collective-permute-start(f32[5,1024]{1,0:T(8,128)} %small.1), channel_id=1, source_target_pairs={{0,16},{16,0},{32,48},{48,32},{64,80},{80,64},{96,112},{112,96},{1... | collective-permute-start | bytes 61448 | tf_op jit(solution)/shard_map/ppermute | solution.py:715
  188.9 7.3 %collective-permute-start.26 = (f32[5,1024]{1,0:T(8,128)S(1)}, f32[5,1024]{1,0:T(8,128)S(1)}, u32[]{:S(2)}, u32[]{:S(2)}) collective-permute-start(f32[5,1024]{1,0:T(8,128)S(1)} %add.48), channel_id=1, source_target_pairs={{0,64},{16,80},{32,96},{48,112},{64,0},{80,16},{96,32},{112,48},{1... | collective-permute-start | bytes 61448 | tf_op jit(solution)/shard_map/ppermute | solution.py:43
  189.8 6.4 %collective-permute-start.27 = (f32[5,1024]{1,0:T(8,128)S(1)}, f32[5,1024]{1,0:T(8,128)S(1)}, u32[]{:S(2)}, u32[]{:S(2)}) collective-permute-start(f32[5,1024]{1,0:T(8,128)S(1)} %add.48), channel_id=1, source_target_pairs={{0,32},{16,48},{32,64},{48,80},{64,96},{80,112},{96,0},{112,16},{1... | collective-permute-start | bytes 61448 | tf_op jit(solution)/shard_map/ppermute | solution.py:43
  (44 other events, 417.6 us)

commit v4 on v3

v4 whole, which is shorter than its diff:
```python
from functools import partial

import jax
import jax.numpy as jnp
import numpy as np
from jax import lax
from jax.experimental import pallas as pl
from jax.experimental.pallas import tpu as pltpu
from jax.sharding import PartitionSpec as P

ROT = 16
LEN = 2048
EPS = 1e-05
HEAD = 64
ROWS = 256
STEPS = LEN // ROWS
HALF = ROWS // 2
SCALE = HEAD ** (-0.5)

SAME_CORE = [[c + 2 * i for i in range(8)] for c in range(2)]
SAME_Y = [[c + 4 * i for i in range(4)] for c in range(4)]
PAIR = [(i, i ^ 1) for i in range(16)]
Z_NEAR = [(i, i ^ 2) for i in range(16)]
Z_PAIR = [(i, i ^ 1) for i in range(8)]

F32 = jnp.float32
LOW = jnp.bfloat16


def swap_core(value):
    return lax.ppermute(value, "tensor", PAIR)


def trade_chips(blocks):
    return lax.all_to_all(blocks, "tensor", 0, 0, axis_index_groups=SAME_CORE, tiled=True)


def trade_y(blocks):
    return lax.all_to_all(blocks, "tensor", 0, 0, axis_index_groups=SAME_Y, tiled=True)


def copies(block, count):
    return jnp.broadcast_to(block[None], (count,) + block.shape)


def move_x(value, distance):
    pairs = [(i, (i // 2 + distance) % 4 * 2 + i % 2) for i in range(8)]
    return lax.ppermute(value, "dp", pairs)


def add_four(own, moved):
    total = own.astype(F32)
    for part in moved:
        total = total + part.astype(F32)
    return total.astype(LOW)


def add_low(left, right):
    return (left.astype(F32) + right.astype(F32)).astype(LOW)


def sum_four(rows, move):
    return (rows + move(rows, 2)) + (move(rows, 1) + move(rows, 3))


def move_y(value, distance):
    pairs = [(i, (i // 4 + distance) % 4 * 4 + i % 4) for i in range(16)]
    return lax.ppermute(value, "tensor", pairs)


def spread_x(low):
    return [low] + [move_x(low, distance) for distance in range(1, 4)]


def normalize(values):
    center = values - jnp.mean(values, axis=-1, keepdims=True)
    inverse = lax.rsqrt(jnp.mean(center * center, axis=-1, keepdims=True) + EPS)
    return (center * inverse, inverse)


def norm_back(scaled, normalized, inverse):
    centered = scaled - jnp.mean(scaled, axis=-1, keepdims=True)
    return inverse * (centered - normalized * jnp.mean(scaled * normalized, axis=-1, keepdims=True))


def rotary_tables():
    lane = np.arange(2 * HEAD) % HEAD
    half = ROT // 2
    inverse = np.float32(10000.0) ** (-2.0 * (lane % half).astype(np.float32) / np.float32(ROT))
    inverse = np.where(lane < ROT, inverse, 0.0).astype(np.float32)
    angles = np.arange(LEN, dtype=np.float32)[:, None] * inverse[None, :]
    sign = np.where(lane < half, -1.0, 1.0).astype(np.float32)
    return np.cos(angles).astype(np.float32), (np.sin(angles) * sign).astype(np.float32)


def turn(values, cosine, sine):
    lane = lax.broadcasted_iota(jnp.int32, values.shape, 1) % HEAD
    partner = jnp.where(
        lane < ROT // 2,
        pltpu.roll(values, 2 * HEAD - ROT // 2, 1),
        pltpu.roll(values, ROT // 2, 1),
    )
    return values * cosine + partner * sine


def dot(left, right, left_axis=1, right_axis=0):
    return lax.dot_general(
        left,
        right,
        (((left_axis,), (right_axis,)), ((), ())),
        preferred_element_type=F32,
    )


def core_here():
    return lax.axis_index("tensor") % 2


def stream(steps, each, moves):
    step = pl.program_id(0)

    @pl.when(step == 0)
    def _():
        for place in range(steps // each):
            for move in moves:
                move(place).start()

    @pl.when(step % each == 0)
    def _():
        for move in moves:
            move(step // each).wait()


def fetch(source, target, done):
    def move(place):
        return pltpu.make_async_copy(source(place), target(place), done.at[place])

    return move


def fetch_rows(source, target, done, each):
    return fetch(
        lambda place: source.at[pl.ds(place * each, each)],
        lambda place: target.at[pl.ds(place * each, each)],
        done,
    )


def fetch_parity(source, target, done, each):
    core = core_here()
    return fetch(
        lambda place: source.at[pl.ds(place * each, each), core],
        lambda place: target.at[pl.ds(place * each, each)],
        done,
    )


def fetch_joined(source, target, done, each, core):
    start = pl.multiple_of(core * HALF, HALF)
    return fetch(
        lambda place: source.at[pl.ds(place * each, each)],
        lambda place: target.at[pl.ds(place * each, each), pl.ds(start, HALF)],
        done,
    )


def send_rows(block, send):
    core = core_here()
    send[0] = block[pl.ds(pl.multiple_of((1 - core) * HALF, HALF), HALF), :]


def x_here():
    return lax.axis_index("dp") // 2


def renormalize(rows, stats):
    return (rows.astype(F32) - stats[:, 0:1]) * stats[:, 1:2]


def row_sum(values):
    return jnp.sum(values, axis=0, keepdims=True)


def forward_kernel(
    mine, other, vecs, w_qkv, b_qkv, w_up, b_up, cosine, sine,
    stats, queries, keys, values, active, active_send, slope,
    context, context_send, mass, rows, first, second, mine_done, other_done,
):
    core = core_here()
    stream(
        STEPS,
        2,
        [
            fetch_joined(mine, rows, mine_done, 2, core),
            fetch_joined(other, rows, other_done, 2, 1 - core),
        ],
    )
    step = pl.program_id(0)
    for part in range(0, ROWS, 32):
        span = slice(part, part + 32)
        here = rows[step, span, :].astype(F32)
        mean = jnp.mean(here, axis=-1, keepdims=True)
        center = here - mean
        inverse = lax.rsqrt(jnp.mean(center * center, axis=-1, keepdims=True) + EPS)
        normalized = center * inverse
        lane = lax.broadcasted_iota(jnp.int32, (32, 128), 1)
        stats[span, :] = jnp.where(lane == 0, mean, inverse)
        first[span, :] = (normalized * vecs[0:1, :] + vecs[1:2, :]).astype(LOW)
        second[span, :] = (normalized * vecs[2:3, :] + vecs[3:4, :]).astype(LOW)
    projected = dot(first[...], w_qkv[...], 1, 1) + b_qkv[...]
    turned = turn(projected[:, : 2 * HEAD], cosine[...], sine[...])
    here = pl.ds(pl.multiple_of(step * ROWS, ROWS), ROWS)
    queries[here, :] = turned[:, :HEAD].astype(LOW) * SCALE
    keys[here, :] = turned[:, HEAD:].astype(LOW)
    values[here, :] = projected[:, 2 * HEAD :].astype(LOW)
    for part in range(0, ROWS, 64):
        span = slice(part, part + 64)
        hidden = dot(second[span, :], w_up[...]) + b_up[...]
        share = 0.5 * (1.0 + lax.erf(hidden * (0.5**0.5)))
        active[span, :] = (hidden * share).astype(LOW)
        bell = jnp.exp(-0.5 * hidden * hidden) * ((2.0 * np.pi) ** -0.5)
        slope[span, :] = share + hidden * bell
    send_rows(active, active_send)

    place = lax.broadcasted_iota(jnp.int32, (ROWS, ROWS), 0)
    query = lax.broadcasted_iota(jnp.int32, (ROWS, ROWS), 1)
    seen = place <= query

    def block(index):
        low, high = index * ROWS, (index + 1) * ROWS
        asked = queries[low:high, :]
        near = jnp.where(seen, dot(keys[low:high, :], asked, 1, 1), -1e30)
        top = jnp.max(near, axis=0, keepdims=True)
        if index:
            far = dot(keys[:low, :], asked, 1, 1)
            top = jnp.maximum(top, jnp.max(far, axis=0, keepdims=True))
            far = jnp.exp(far - top)
        near = jnp.exp(near - top)
        total = row_sum(near)
        if index:
            total = total + row_sum(far)
        scale = 1.0 / total
        mass[0] = top + jnp.log(total)
        found = dot(values[low:high, :], (near * scale).astype(LOW), 0, 0)
        if index:
            found = found + dot(values[:low, :], (far * scale).astype(LOW), 0, 0)
        context[...] = found.T.astype(LOW)

    for index in range(STEPS):
        pl.when(step == index)(partial(block, index))
    send_rows(context, context_send)


def flat(block):
    return block.reshape(ROWS, block.shape[-1])


def mix_kernel(
    context, active, context_in, active_in, w_out, w_down, w_out_in, w_down_in, result,
    context_rows, active_rows, context_other, active_other, *done,
):
    stream(
        STEPS // 2,
        STEPS // 2,
        [
            fetch_parity(context, context_rows, done[0], STEPS),
            fetch_parity(active, active_rows, done[1], STEPS),
            fetch_rows(context_in, context_other, done[2], STEPS),
            fetch_rows(active_in, active_other, done[3], STEPS),
        ],
    )
    here = pl.ds(pl.program_id(0) * 2, 2)
    mixed = dot(flat(context_rows[here]), w_out[...])
    mixed = mixed + dot(flat(active_rows[here]), w_down[...])
    mixed = mixed + dot(flat(context_other[here]), w_out_in[...])
    mixed = mixed + dot(flat(active_other[here]), w_down_in[...])
    result[...] = mixed.astype(LOW).reshape(2, HALF, mixed.shape[1])


def feed_back_kernel(
    mine, other, active, slope, tokens_mine, tokens_other, stats, vecs, context, w_down, w_out,
    grad_hidden, hidden_send, grad_context, feed_0, feed_1, feed_2, feed_3, grad_out,
    rows, active_rows, slope_rows, token_rows, stats_rows, second, up_sum, down_sum, out_sum,
    bias_sum, *done,
):
    step = pl.program_id(0)
    core = core_here()
    stream(
        STEPS,
        2,
        [
            fetch_joined(mine, rows, done[0], 2, core),
            fetch_joined(other, rows, done[1], 2, 1 - core),
            fetch_rows(active, active_rows, done[2], 2),
            fetch_rows(slope, slope_rows, done[3], 2),
            fetch_rows(stats, stats_rows, done[4], 2),
            fetch_joined(tokens_mine, token_rows, done[5], 2, core),
            fetch_joined(tokens_other, token_rows, done[6], 2, 1 - core),
        ],
    )

    @pl.when(step == 0)
    def _():
        up_sum[...] = jnp.zeros_like(up_sum)
        down_sum[...] = jnp.zeros_like(down_sum)
        out_sum[...] = jnp.zeros_like(out_sum)
        bias_sum[...] = jnp.zeros_like(bias_sum)

    grads = rows[step]
    hidden = (dot(grads, w_down[...], 1, 1) * slope_rows[step]).astype(LOW)
    grad_hidden[...] = hidden
    send_rows(grad_hidden, hidden_send)
    grad_context[...] = dot(grads, w_out[...], 1, 1).astype(LOW)
    down_sum[...] += dot(active_rows[step], grads, 0, 0)
    out_sum[...] += dot(context[...], grads, 0, 0)
    for part in range(0, ROWS, 32):
        span = slice(part, part + 32)
        normalized = renormalize(token_rows[step, span, :], stats_rows[step, span, :])
        second[span, :] = (normalized * vecs[2:3, :] + vecs[3:4, :]).astype(LOW)
    up_sum[...] += dot(hidden, second[...], 0, 0)
    bias_sum[...] += row_sum(hidden.astype(F32))

    @pl.when(step == STEPS - 1)
    def _():
        grad_out[...] = out_sum[...].astype(LOW)
        for slot, feed in enumerate((feed_0, feed_1, feed_2, feed_3)):
            span = quarter((x_here() + slot) % 4)
            feed[0:256, :] = up_sum[:, span].T.astype(LOW)
            feed[256:512, :] = down_sum[:, span].astype(LOW)
            feed[512:528, :] = jnp.broadcast_to(bias_sum[...], (16, 256)).astype(LOW)


def quarter(part):
    return pl.ds(pl.multiple_of(part * 256, 256), 256)


def attend_back_kernel(
    queries, keys, values, grad_context, mass, cosine, sine, grad_hidden, stats, mine, other,
    w_qkv, w_up, vecs, own_sum, grad_out,
    grad_projected, projected_send, head_0, head_1, head_2, head_3, sums,
    query_sum, key_sum, value_sum, qkv_sum, moments, first, normal,
    cosine_rows, sine_rows, hidden_rows, stats_rows, token_rows, qkv_rows, up_rows, *done,
):
    wide = 3 * HEAD

    def later():
        pairs = [
            (cosine, cosine_rows), (sine, sine_rows), (grad_hidden, hidden_rows),
            (stats, stats_rows), (w_qkv, qkv_rows), (w_up, up_rows),
        ]
        for source, core in ((mine, core_here()), (other, 1 - core_here())):
            start = pl.multiple_of(core * HALF, HALF)
            pairs.append((source, token_rows.at[:, pl.ds(start, HALF)]))
        return [pltpu.make_async_copy(*pair, mark) for pair, mark in zip(pairs, done)]

    @pl.when(pl.program_id(0) == 0)
    def _():
        for copy in later():
            copy.start()

    place = lax.broadcasted_iota(jnp.int32, (ROWS, ROWS), 0)
    query = lax.broadcasted_iota(jnp.int32, (ROWS, ROWS), 1)
    seen = place <= query

    @pl.when(pl.program_id(0) == 0)
    def _():
        key_sum[...] = jnp.zeros_like(key_sum)
        value_sum[...] = jnp.zeros_like(value_sum)

    def block(index):
        low, high = index * ROWS, (index + 1) * ROWS
        asked = queries[low:high, :]
        grads = grad_context[...]
        spans = [slice(low, high)] + ([slice(0, low)] if index else [])
        weights, pulls = [], []
        inner = 0.0
        for number, span in enumerate(spans):
            scores = dot(keys[span, :], asked, 1, 1)
            if number == 0:
                scores = jnp.where(seen, scores, -1e30)
            weight = jnp.exp(scores - mass[0])
            pull = dot(values[span, :], grads, 1, 1)
            inner = inner + row_sum(weight * pull)
            weights.append(weight)
            pulls.append(pull)
        asked_grad = 0.0
        for span, weight, pull in zip(spans, weights, pulls):
            value_sum[span, :] += dot(weight.astype(LOW), grads)
            scores_grad = (weight * (pull - inner)).astype(LOW)
            key_sum[span, :] += dot(scores_grad, asked)
            asked_grad = asked_grad + dot(keys[span, :], scores_grad, 0, 0)
        query_sum[low:high, :] = asked_grad.T * SCALE

    for index in range(STEPS):
        pl.when(pl.program_id(0) == index)(partial(block, index))

    @pl.when(pl.program_id(0) == STEPS - 1)
    def _():
        for copy in later():
            copy.wait()
        for index in range(STEPS):
            span = slice(index * ROWS, (index + 1) * ROWS)
            both = jnp.concatenate([query_sum[span, :], key_sum[span, :]], axis=1)
            turned = turn(both, cosine_rows[span, :], -sine_rows[span, :])
            grad_projected[span, : 2 * HEAD] = turned.astype(LOW)
            grad_projected[span, 2 * HEAD :] = value_sum[span, :].astype(LOW)
            place = index * ROWS + (1 - core_here()) * HALF
            projected_send[index] = grad_projected[pl.ds(pl.multiple_of(place, HALF), HALF), :]
        hidden_bias, bias = 0.0, 0.0
        for index in range(STEPS):
            span = slice(index * ROWS, (index + 1) * ROWS)
            for part in range(0, ROWS, 32):
                rows = slice(part, part + 32)
                place = slice(index * ROWS + part, index * ROWS + part + 32)
                normalized = renormalize(token_rows[index, rows, :], stats_rows[place, :])
                normal[rows, :] = normalized.astype(LOW)
                first[rows, :] = (normalized * vecs[0:1, :] + vecs[1:2, :]).astype(LOW)
            grads = grad_projected[span, :]
            hidden = hidden_rows[span, :]
            here = normal[...]
            added = dot(grads, first[...], 0, 0), dot(grads, here, 0, 0), dot(hidden, here, 0, 0)
            if index:
                qkv_sum[...] += added[0]
                moments[0:wide, :] += added[1]
                moments[wide:, :] += added[2]
            else:
                qkv_sum[...] = added[0]
                moments[0:wide, :] = added[1]
                moments[wide:, :] = added[2]
            bias = bias + row_sum(grads.astype(F32))
            hidden_bias = hidden_bias + row_sum(hidden.astype(F32))
        for slot, head in enumerate((head_0, head_1, head_2, head_3)):
            span = quarter((x_here() + slot) % 4)
            head[0:wide, :] = qkv_sum[:, span].astype(LOW)
            head[wide:256, :] = grad_out[:, span]
            head[256:272, :wide] = jnp.broadcast_to(bias, (16, wide)).astype(LOW)
            head[256:272, wide:] = jnp.zeros((16, 256 - wide), LOW)
        sums[0:1, :] = row_sum(moments[0:wide, :] * qkv_rows[...].astype(F32))
        sums[1:2, :] = dot_full(bias, qkv_rows[...], 0)
        sums[2:3, :] = row_sum(moments[wide:, :] * up_rows[...].astype(F32).T)
        sums[3:4, :] = dot_full(hidden_bias, up_rows[...], 1)
        sums[4:5, :] = own_sum[...]


def input_back_kernel(
    projected, hidden, projected_in, hidden_in, vecs, w_qkv, w_up, w_qkv_in, w_up_in,
    result, projected_rows, hidden_rows, projected_other, hidden_other, *done,
):
    stream(
        STEPS // 2,
        STEPS // 2,
        [
            fetch_parity(projected, projected_rows, done[0], STEPS),
            fetch_parity(hidden, hidden_rows, done[1], STEPS),
            fetch_rows(projected_in, projected_other, done[2], STEPS),
            fetch_rows(hidden_in, hidden_other, done[3], STEPS),
        ],
    )
    here = pl.ds(pl.program_id(0) * 2, 2)
    one = dot(flat(projected_rows[here]), w_qkv[...])
    one = one + dot(flat(projected_other[here]), w_qkv_in[...])
    two = dot(flat(hidden_rows[here]), w_up[...], 1, 1)
    two = two + dot(flat(hidden_other[here]), w_up_in[...], 1, 1)
    weighted = one * vecs[0:1, :] + two * vecs[2:3, :]
    result[...] = weighted.astype(LOW).reshape(2, HALF, weighted.shape[1])


def dot_full(left, right, right_axis):
    return lax.dot_general(
        left,
        right.astype(F32),
        (((1,), (right_axis,)), ((), ())),
        precision=lax.Precision.HIGHEST,
        preferred_element_type=F32,
    )


def fold_kernel(parts, keep, send):
    own = lax.axis_index("tensor") // 2 % 2

    def total(start):
        span = pl.ds(pl.multiple_of(start, HALF), HALF)
        result = parts[0, span, :].astype(F32)
        for number in range(1, 4):
            result = result + parts[number, span, :].astype(F32)
        return result

    keep[...] = total(own * HALF)
    send[...] = total((1 - own) * HALF).astype(LOW)


def finish_grads_kernel(
    part_0, part_1, part_2, part_3,
    grad_qkv, grad_qkv_bias, grad_out, grad_up, grad_up_bias, grad_down,
):
    wide = 3 * HEAD
    for slot, part in enumerate((part_0, part_1, part_2, part_3)):
        span = quarter((x_here() + 4 - slot) % 4)
        grad_up[span, :] = part[0:256, :].astype(F32)
        grad_down[:, span] = part[256:512, :].astype(F32)
        grad_qkv[:, span] = part[528 : 528 + wide, :].astype(F32)
        grad_out[:, span] = part[528 + wide : 784, :].astype(F32)
    grad_up_bias[...] = part_0[512:513, :].astype(F32)
    grad_qkv_bias[...] = part_0[784:785, :wide].astype(F32)


def finish_out_kernel(parts, tokens, out_bias, layer_out):
    total = jnp.sum(parts[...].astype(F32), axis=0)
    layer_out[...] = (tokens[...].astype(F32) + total + out_bias[...].astype(F32)).astype(LOW)


def finish_back_kernel(keep, part, tokens, cotangent, input_grad):
    scaled = keep[...] + part[...].astype(F32)
    normalized, inverse = normalize(tokens[...].astype(F32))
    input_grad[...] = (
        cotangent[...].astype(F32) + norm_back(scaled, normalized, inverse)
    ).astype(LOW)


def arrivals(count):
    return pltpu.SemaphoreType.DMA((count,))


def whole(shape):
    return pl.BlockSpec(shape, lambda step: (0,) * len(shape))


def by_rows(columns):
    return pl.BlockSpec((ROWS, columns), lambda step: (step, 0))


LEFT = pl.BlockSpec(memory_space=pltpu.HBM)
MASS = pl.BlockSpec((1, 1, ROWS), lambda step: (step, 0, 0))


def shape(dims, kind):
    return jax.ShapeDtypeStruct(dims, kind)


COST = pl.CostEstimate(flops=1, bytes_accessed=1, transcendentals=0)


def left(dims, kind):
    return pltpu.HBM(dims, kind)


def launch(kernel, name, ins, outs, out_shapes, scratch, steps=STEPS, room=60):
    return pl.pallas_call(
        kernel,
        name=name,
        grid=(steps,),
        in_specs=ins,
        out_specs=outs,
        scratch_shapes=scratch,
        out_shape=out_shapes,
        compiler_params=pltpu.CompilerParams(vmem_limit_bytes=room * 2**20),
        cost_estimate=COST,
    )


def half_rows(columns):
    return pl.BlockSpec((1, HALF, columns), lambda step: (step, 0, 0))


def blocks(value):
    return value.reshape(STEPS, ROWS, value.shape[1])


def four(value):
    return value.reshape(STEPS, 2, HALF, value.shape[1])


def per_device(
    tokens, w_qkv, b_qkv, w_out, w_up, b_up, w_down, out_bias,
    ln1_gain, ln1_shift, ln2_gain, ln2_shift, cotangent,
):
    model = w_up.shape[0]
    feed_here = w_up.shape[1]
    wide = 3 * HEAD
    w_qkv = w_qkv.transpose(1, 2, 0).reshape(wide, model)
    w_out = w_out.reshape(HEAD, model)
    vecs = jnp.stack([ln1_gain, ln1_shift, ln2_gain, ln2_shift]).astype(F32)
    cosine, sine = rotary_tables()
    own_sum = jnp.sum(cotangent.astype(F32), axis=0)[None, :]

    held = copies(cotangent, 8)
    mine = trade_chips(copies(tokens, 8))
    weights_in = [swap_core(w) for w in (w_out, w_down, w_qkv, w_up)]
    held, vecs, b_qkv, b_up, own_sum, mine, *weights_in = lax.optimization_barrier(
        (held, vecs, b_qkv.astype(F32), b_up.astype(F32)[None, :], own_sum, mine)
        + tuple(weights_in)
    )
    w_out_in, w_down_in, w_qkv_in, w_up_in = weights_in
    other = swap_core(mine)
    grad_mine = trade_chips(held)

    halves = shape((STEPS, HALF, feed_here), LOW)
    (
        stats, queries, keys, values, active, active_send, slope, context, context_send, mass,
    ) = launch(
        forward_kernel,
        "forward",
        [
            LEFT, LEFT, whole((4, model)), whole((wide, model)), whole((1, wide)),
            whole((model, feed_here)), whole((1, feed_here)), by_rows(128), by_rows(128),
        ],
        [
            by_rows(128), whole((LEN, HEAD)),
            whole((LEN, HEAD)), whole((LEN, HEAD)), by_rows(feed_here), half_rows(feed_here),
            by_rows(feed_here), by_rows(HEAD), half_rows(HEAD), MASS,
        ],
        [
            left((LEN, 128), F32),
            shape((LEN, HEAD), LOW), shape((LEN, HEAD), LOW), shape((LEN, HEAD), LOW),
            left((LEN, feed_here), LOW), halves, left((LEN, feed_here), F32),
            shape((LEN, HEAD), LOW), shape((STEPS, HALF, HEAD), LOW),
            shape((STEPS, 1, ROWS), F32),
        ],
        [
            pltpu.VMEM((STEPS, ROWS, model), LOW), pltpu.VMEM((ROWS, model), LOW),
            pltpu.VMEM((ROWS, model), LOW), arrivals(STEPS), arrivals(STEPS),
        ],
    )(mine, other, vecs, w_qkv, b_qkv, w_up, b_up, cosine, sine)
    active_in = swap_core(active_send)
    context_in = swap_core(context_send)

    mixed = launch(
        mix_kernel,
        "mix",
        [LEFT] * 4 + [whole((HEAD, model)), whole((feed_here, model))] * 2,
        pl.BlockSpec((2, HALF, model), lambda step: (step, 0, 0)),
        left((STEPS, HALF, model), LOW),
        [pltpu.VMEM((STEPS, HALF, HEAD), LOW), pltpu.VMEM((STEPS, HALF, feed_here), LOW)] * 2
        + [arrivals(1)] * 4,
        steps=4,
    )(four(context), four(active), context_in, active_in, w_out, w_down, w_out_in, w_down_in)

    grad_mine, mixed = lax.optimization_barrier((grad_mine, mixed))
    grad_other = swap_core(grad_mine)
    branch = trade_chips(mixed)

    grad_hidden, hidden_send, grad_context, *feed, grad_out = launch(
        feed_back_kernel,
        "feed_back",
        [
            *[LEFT] * 7, whole((4, model)),
            by_rows(HEAD), whole((feed_here, model)), whole((HEAD, model)),
        ],
        [by_rows(feed_here), half_rows(feed_here), by_rows(HEAD)]
        + [whole((528, 256))] * 4 + [whole((HEAD, model))],
        [shape((LEN, feed_here), LOW), halves, shape((LEN, HEAD), LOW)]
        + [shape((528, 256), LOW)] * 4 + [shape((HEAD, model), LOW)],
        [
            pltpu.VMEM((STEPS, ROWS, model), LOW), pltpu.VMEM((STEPS, ROWS, feed_here), LOW),
            pltpu.VMEM((STEPS, ROWS, feed_here), F32), pltpu.VMEM((STEPS, ROWS, model), LOW),
            pltpu.VMEM((STEPS, ROWS, 128), F32), pltpu.VMEM((ROWS, model), LOW),
            pltpu.VMEM((feed_here, model), F32), pltpu.VMEM((feed_here, model), F32),
            pltpu.VMEM((HEAD, model), F32), pltpu.VMEM((1, feed_here), F32),
        ]
        + [arrivals(STEPS)] * 7,
    )(
        grad_mine, grad_other, blocks(active), blocks(slope), mine, other, blocks(stats), vecs,
        context, w_down, w_out,
    )
    hidden_in = swap_core(hidden_send)
    feed_moved = [move_x(feed[distance], distance) for distance in range(1, 4)]

    grad_projected, projected_send, *head, sums = launch(
        attend_back_kernel,
        "attend_back",
        [
            whole((LEN, HEAD)), whole((LEN, HEAD)), whole((LEN, HEAD)), by_rows(HEAD), MASS,
            *[LEFT] * 8, whole((4, model)), whole((1, model)), whole((HEAD, model)),
        ],
        [whole((LEN, wide)), whole((STEPS, HALF, wide))] + [whole((272, 256))] * 4
        + [whole((5, model))],
        [shape((LEN, wide), LOW), shape((STEPS, HALF, wide), LOW)]
        + [shape((272, 256), LOW)] * 4 + [shape((5, model), F32)],
        [pltpu.VMEM((LEN, HEAD), F32)] * 3
        + [
            pltpu.VMEM((wide, model), F32), pltpu.VMEM((wide + feed_here, model), F32),
            pltpu.VMEM((ROWS, model), LOW), pltpu.VMEM((ROWS, model), LOW),
            pltpu.VMEM((LEN, 128), F32), pltpu.VMEM((LEN, 128), F32),
            pltpu.VMEM((LEN, feed_here), LOW), pltpu.VMEM((LEN, 128), F32),
            pltpu.VMEM((STEPS, ROWS, model), LOW), pltpu.VMEM((wide, model), LOW),
            pltpu.VMEM((model, feed_here), LOW),
        ]
        + [pltpu.SemaphoreType.DMA] * 8,
    )(
        queries, keys, values, grad_context, mass, cosine, sine, grad_hidden, stats, mine, other,
        w_qkv, w_up, vecs, own_sum, grad_out,
    )
    sums_in = swap_core(sums)
    head_moved = [move_x(head[distance], distance) for distance in range(1, 4)]
    grad_projected, projected_send, branch, hidden_in, *feed_moved = lax.optimization_barrier(
        (grad_projected, projected_send, branch, hidden_in, *feed_moved)
    )
    projected_in = swap_core(projected_send)

    both = launch(
        input_back_kernel,
        "input_back",
        [LEFT] * 4 + [whole((4, model))] + [whole((wide, model)), whole((model, feed_here))] * 2,
        pl.BlockSpec((2, HALF, model), lambda step: (step, 0, 0)),
        left((STEPS, HALF, model), LOW),
        [pltpu.VMEM((STEPS, HALF, wide), LOW), pltpu.VMEM((STEPS, HALF, feed_here), LOW)] * 2
        + [arrivals(1)] * 4,
        steps=4,
    )(
        four(grad_projected), four(grad_hidden), projected_in, hidden_in, vecs,
        w_qkv, w_up, w_qkv_in, w_up_in,
    )
    both, sums, sums_in, *head_moved = lax.optimization_barrier(
        (both, sums, sums_in, *head_moved)
    )
    half = jnp.concatenate([add_four(feed[0], feed_moved), add_four(head[0], head_moved)], axis=0)
    other_half = lax.ppermute(half, "dp", Z_PAIR)
    scaled = trade_y(both.reshape(4, 2 * HALF, model))
    small = sums + sums_in
    near = lax.ppermute(small, "tensor", Z_NEAR)
    far = lax.ppermute(small, "dp", Z_PAIR)
    both_z = [(d * 16 + t, (d ^ 1) * 16 + (t ^ 2)) for d in range(8) for t in range(16)]
    across = lax.ppermute(small, ("dp", "tensor"), both_z)
    other_half, small = lax.optimization_barrier((other_half, (small + near) + (far + across)))
    small = sum_four(small, move_x)
    parts = spread_x(add_low(half, other_half))
    small = sum_four(small, move_y)

    layer_out = pl.pallas_call(
        finish_out_kernel,
        name="finish_out",
        out_shape=shape(tokens.shape, LOW),
        cost_estimate=COST,
    )(branch, tokens, out_bias[None, :])
    grad_qkv, grad_qkv_bias, grad_out, grad_up, grad_up_bias, grad_down = pl.pallas_call(
        finish_grads_kernel,
        name="finish_grads",
        out_shape=[
            shape((wide, model), F32), shape((1, wide), F32), shape((HEAD, model), F32),
            shape((model, feed_here), F32), shape((1, feed_here), F32),
            shape((feed_here, model), F32),
        ],
        cost_estimate=COST,
    )(*parts)
    scaled, layer_out, small = lax.optimization_barrier((scaled, layer_out, small))
    keep, send = pl.pallas_call(
        fold_kernel,
        name="fold",
        out_shape=[
            shape((HALF, model), F32), shape((HALF, model), LOW),
        ],
        cost_estimate=COST,
    )(scaled)
    received = lax.ppermute(send, "tensor", Z_NEAR)
    input_grad = pl.pallas_call(
        finish_back_kernel,
        name="finish_back",
        grid=(1,),
        in_specs=[
            whole((HALF, model)), whole((HALF, model)), whole(tokens.shape),
            whole(tokens.shape),
        ],
        out_specs=whole(tokens.shape),
        out_shape=shape(tokens.shape, LOW),
        cost_estimate=COST,
    )(keep, received, tokens, cotangent)

    return (
        layer_out,
        input_grad,
        grad_qkv.reshape(1, wide, model).transpose(2, 0, 1),
        grad_qkv_bias,
        grad_out.reshape(1, HEAD, model),
        grad_up,
        grad_up_bias[0],
        grad_down,
        small[4],
        small[0],
        small[1],
        small[2],
        small[3],
    )


def solution(mesh):
    placed = (
        P(("dp", "tensor"), None),
        P(None, "tensor", None),
        P("tensor", None),
        P("tensor", None, None),
        P(None, "tensor"),
        P("tensor"),
        P("tensor", None),
        P(),
        P(),
        P(),
        P(),
        P(),
        P(("dp", "tensor"), None),
    )
    return jax.shard_map(
        per_device,
        mesh=mesh,
        in_specs=placed,
        out_specs=(
            P(("dp", "tensor"), None),
            P(("dp", "tensor"), None),
            P(None, "tensor", None),
            P("tensor", None),
            P("tensor", None, None),
            P(None, "tensor"),
            P("tensor"),
            P("tensor", None),
            P(),
            P(),
            P(),
            P(),
            P(),
        ),
        check_vma=False,
    )
```

time: 200 us -> 192 us (0.960); the launches traced: 197 us -> 191 us
  waiting for transfers between devices: 49.8 us -> 39.3 us
  starting transfers between devices: 50.1 us -> 54.4 us
    ppermute x3 -> x8, starting transfers between devices: 7.36 us -> 16.5 us  [the longest x3 6.94 us: move_y(): return lax.ppermute(value, 'tensor', pairs)]
    ppermute x15 -> x12, waiting for transfers between devices: 9.02 us -> 0.22 us  [move_x(): return lax.ppermute(value, 'dp', pairs)]
    all_to_all x4 -> x3, starting transfers between devices: 19.1 us -> 14 us  [trade_chips(): lax.all_to_all(blocks, 'tensor', 0, 0, axis_index_groups=SAME_CORE, tiled...]
    all_to_all x0 -> x1, starting transfers between devices: none -> 4.08 us  [trade_y(): lax.all_to_all(blocks, 'tensor', 0, 0, axis_index_groups=SAME_Y, tiled=True)]
    ppermute x15 -> x12, starting transfers between devices: 21.3 us -> 17.9 us  [move_x(): return lax.ppermute(value, 'dp', pairs)]
    pallas_call x1, Pallas kernels: 18.7 us -> 21.4 us  [per_device(): launch(attend_back_kernel, 'attend_back', [whole((LEN, HEAD)), whole((LEN...]
    all_to_all x4 -> x3, waiting for transfers between devices: 28.3 us -> 27 us  [trade_chips(): lax.all_to_all(blocks, 'tensor', 0, 0, axis_index_groups=SAME_CORE, tiled...]
    pallas_call x3 -> x2, Pallas kernels: 17.2 us -> 16.4 us  [the longest x1 13.7 us: per_device(): launch(feed_back_kernel, 'feed_back', [*[LEFT] * 7, whole((4, model)), by...]
  transfers between devices with their start and end apart: 33 -> 35, of which waited for: 11 -> 8; matrix products, arithmetic and copies ran while one was open for 3% -> 3% of each run, Pallas kernels for 39% -> 40%
where the time goes in v4:
time: 192 us; the launch traced here: 191 us
  Pallas kernels  79.3 us (41%)
  starting transfers between devices  54.4 us (28%)
  waiting for transfers between devices  39.3 us (20%)
  local copies, waits for them, and re-layouts  11.8 us (6%)
  other arithmetic  5.18 us (3%)
    all_to_all x3, waiting for transfers between devices, trade_chips(): lax.all_to_all(blocks, 'tensor', 0, 0, axis_index_groups=SAME_CORE, tiled...  27 us
    pallas_call x1, Pallas kernels, per_device(): launch(attend_back_kernel, 'attend_back', [whole((LEN, HEAD)), whole((LEN...  21.4 us
    pallas_call x1, Pallas kernels, per_device(): launch(forward_kernel, 'forward', [LEFT, LEFT, whole((4, model)), whole((...  20 us
    ppermute x12, starting transfers between devices, move_x(): return lax.ppermute(value, 'dp', pairs)  17.9 us
    all_to_all x3, starting transfers between devices, trade_chips(): lax.all_to_all(blocks, 'tensor', 0, 0, axis_index_groups=SAME_CORE, tiled...  14 us
    pallas_call x1, Pallas kernels, per_device(): launch(feed_back_kernel, 'feed_back', [*[LEFT] * 7, whole((4, model)), by...  13.7 us
    ppermute x3, starting transfers between devices, move_y(): return lax.ppermute(value, 'tensor', pairs)  6.94 us
    pallas_call x1, Pallas kernels, per_device(): launch(input_back_kernel, 'input_back', [LEFT] * 4 + [whole((4, model))]...  6.77 us
  transfers between devices with their start and end apart: 35, of which 8 were waited for; matrix products, arithmetic and copies ran while one was open for 3% of the time, Pallas kernels for 40%

profile of v4, /device:TPU:0, one launch (start us, length us, event | category | flops | bytes accessed | tf_op | source)
XLA Modules:
  0.0 191.1 jit_solution(9751073286041221527)
XLA Ops:
  0.6 2.5 %broadcast_in_dim.28 = bf16[8,128,1024]{2,1,0:T(8,128)(2,1)} broadcast(bf16[128,1024]{1,0:T(8,128)(2,1)} %tokens.3), dimensions={1,2} | broadcast | bytes 2359296 | tf_op jit(solution)/shard_map/broadcast_in_dim | solution.py:43
  3.2 6.1 %all-to-all-start = ((bf16[8,128,1024]{2,1,0:T(8,128)(2,1)}), bf16[8,128,1024]{2,1,0:T(8,128)(2,1)S(1)}, u32[]{:S(2)}, u32[]{:S(2)}) async-start(bf16[8,128,1024]{2,1,0:T(8,128)(2,1)} %broadcast_in_dim.28), calls=%async_computation | async-start | bytes 4194304 | tf_op jit(solution)/shard_map/all_to_all | solution.py:35
  15.8 24.7 %all-to-all-done.mine.tokens_mine = bf16[8,128,1024]{2,1,0:T(8,128)(2,1)S(1)} async-done(((bf16[8,128,1024]{2,1,0:T(8,128)(2,1)}), bf16[8,128,1024]{2,1,0:T(8,128)(2,1)S(1)}, u32[]{:S(2)}, u32[]{:S(2)}) %all-to-all-start) | async-done | bytes 2097184 | tf_op jit(solution)/shard_map/all_to_all | solution.py:35
  42.5 4.4 %all-to-all-start.1 = ((bf16[8,128,1024]{2,1,0:T(8,128)(2,1)}), bf16[8,128,1024]{2,1,0:T(8,128)(2,1)}, u32[]{:S(2)}, u32[]{:S(2)}) async-start(bf16[8,128,1024]{2,1,0:T(8,128)(2,1)} %broadcast_in_dim.24), calls=%async_computation.1 | async-start | bytes 4194304 | tf_op jit(solution)/shard_map/all_to_all | solution.py:35
  46.9 20.0 %forward.1 = (f32[2048,128]{1,0:T(8,128)}, bf16[2048,64]{1,0:T(8,128)(2,1)}, bf16[2048,64]{1,0:T(8,128)(2,1)}, bf16[2048,64]{1,0:T(8,128)(2,1)}, bf16[2048,256]{...) custom-call(bf16[8,128,1024]{2,1,0:T(8,128)(2,1)} %copy-done, ...), custom_call_target="tpu_custom_call" | custom-call | flops 1 | bytes 1 | tf_op jit(solution)/shard_map/forward/pallas_call | solution.py:600
  70.3 6.5 %mix.1 = bf16[8,128,1024]{2,1,0:T(8,128)(2,1)} custom-call(bf16[8,2,128,64]{3,2,1,0:T(8,128)(2,1)} %bitcast.34, bf16[8,2,128,256]{3,2,1,0:T(8,128)(2,1)} %bitcast.27, bf16[8,128,64]{2,1,0:T(8,128)(2,1)} %copy-done.16, bf16[8,128,256]{2,1,0:T(8,128)(2,1)} %copy-done.11, bf16[64,1024]{1,0:T(8,128)(2,1)} %bitcast.36, bf16[256,1024]{1,0:T(8,128)(2,1)} %w_down.3, ...), custom_call_target="tpu_custom_call" | custom-call | flops 1 | bytes 1 | tf_op jit(solution)/shard_map/mix/pallas_call | solution.py:627
  79.1 3.6 %all-to-all-start.2 = ((bf16[8,128,1024]{2,1,0:T(8,128)(2,1)}), bf16[8,128,1024]{2,1,0:T(8,128)(2,1)S(1)}, u32[]{:S(2)}, u32[]{:S(2)}) async-start(bf16[8,128,1024]{2,1,0:T(8,128)(2,1)} %mix.1), calls=%async_computation.2 | async-start | bytes 4194304 | tf_op jit(solution)/shard_map/all_to_all | solution.py:35
  83.6 13.7 %feed_back.1 = (bf16[2048,256]{1,0:T(8,128)(2,1)}, bf16[8,128,256]{2,1,0:T(8,128)(2,1)}, bf16[2048,64]{1,0:T(8,128)(2,1)}, bf16[528,256]{1,0:T(8,128)(2,1)}, bf1...) custom-call(bf16[8,128,1024]{2,1,0:T(8,128)(2,1)} %all-to-all-done.1.mine, ...), custom_call_target="tpu_custom_call" | custom-call | flops 1 | bytes 1 | tf_op jit(solution)/shard_map/feed_back/pallas_call | solution.py:642
  97.5 3.0 %collective-permute-start.10 = (bf16[528,256]{1,0:T(8,128)(2,1)}, bf16[528,256]{1,0:T(8,128)(2,1)S(1)}, u32[]{:S(2)}, u32[]{:S(2)}) collective-permute-start(bf16[528,256]{1,0:T(8,128)(2,1)} %get-tuple-element.103), channel_id=1, source_target_pairs={{0,64},{16,80},{32,96},{48,112},{64,0},{80,16},{96,32},{112,48},{1... | collective-permute-start | bytes 811016 | tf_op jit(solution)/shard_map/ppermute | solution.py:48
  102.6 21.4 %attend_back.1 = (bf16[2048,192]{1,0:T(8,128)(2,1)}, bf16[8,128,192]{2,1,0:T(8,128)(2,1)}, bf16[272,256]{1,0:T(8,128)(2,1)}, bf16[272,256]{1,0:T(8,128)(2,1)}, b...) custom-call(bf16[2048,64]{1,0:T(8,128)(2,1)} %get-tuple-element.80.queries, ...), custom_call_target="tpu_custom_call" | custom-call | flops 1 | bytes 1 | tf_op jit(solution)/shard_map/attend_back/pallas_call | solution.py:668
  124.9 3.2 %collective-permute-start.15 = (bf16[272,256]{1,0:T(8,128)(2,1)}, bf16[272,256]{1,0:T(8,128)(2,1)}, u32[]{:S(2)}, u32[]{:S(2)}) collective-permute-start(bf16[272,256]{1,0:T(8,128)(2,1)} %get-tuple-element.112), channel_id=1, source_target_pairs={{0,64},{16,80},{32,96},{48,112},{64,0},{80,16},{96,32},{112,48},{1... | collective-permute-start | bytes 417800 | tf_op jit(solution)/shard_map/ppermute | solution.py:48
  128.9 6.8 %input_back.1 = bf16[8,128,1024]{2,1,0:T(8,128)(2,1)} custom-call(bf16[8,2,128,192]{3,2,1,0:T(8,128)(2,1)} %bitcast.35, bf16[8,2,128,256]{3,2,1,0:T(8,128)(2,1)} %bitcast.25, bf16[8,128,192]{2,1,0:T(8,128)(2,1)} %copy-done.9, bf16[8,128,256]{2,1,0:T(8,128)(2,1)} %copy-done.8, f32[4,1024]{1,0:T(4,128)} %maximum_convert_fusion.vecs, ...), custom_call_target="tpu_custom_call" | custom-call | flops 1 | bytes 1 | tf_op jit(solution)/shard_map/input_back/pallas_call | solution.py:700
  135.7 4.1 %all-to-all-start.3 = ((bf16[4,256,1024]{2,1,0:T(8,128)(2,1)}), bf16[4,256,1024]{2,1,0:T(8,128)(2,1)S(1)}, u32[]{:S(2)}, u32[]{:S(2)}) async-start(bf16[4,256,1024]{2,1,0:T(8,128)(2,1)} %bitcast.24), calls=%async_computation.3 | async-start | bytes 4194304 | tf_op jit(solution)/shard_map/all_to_all | solution.py:39
  141.2 3.7 %collective-permute-start.17 = (bf16[800,256]{1,0:T(8,128)(2,1)S(1)}, bf16[800,256]{1,0:T(8,128)(2,1)S(1)}, u32[]{:S(2)}, u32[]{:S(2)}) collective-permute-start(bf16[800,256]{1,0:T(8,128)(2,1)S(1)} %pad_maximum_fusion), channel_id=1, source_target_pairs={{0,16},{16,0},{32,48},{48,32},{64,80},{80,64},{96,112},{112,96},{1... | collective-permute-start | bytes 1228808 | tf_op jit(solution)/shard_map/ppermute | solution.py:717
  146.9 2.7 %collective-permute-start.20 = (f32[5,1024]{1,0:T(8,128)S(1)}, f32[5,1024]{1,0:T(8,128)S(1)}, u32[]{:S(2)}, u32[]{:S(2)}) collective-permute-start(f32[5,1024]{1,0:T(8,128)S(1)} %add.57), channel_id=1, source_target_pairs={{0,18},{1,19},{2,16},{3,17},{4,22},{5,23},{6,20},{7,21},{8,26},{9,... | collective-permute-start | bytes 61448 | tf_op jit(solution)/shard_map/ppermute | solution.py:723
  149.6 6.7 %collective-permute-done.18 = f32[5,1024]{1,0:T(8,128)S(1)} collective-permute-done((f32[5,1024]{1,0:T(8,128)S(1)}, f32[5,1024]{1,0:T(8,128)S(1)}, u32[]{:S(2)}, u32[]{:S(2)}) %collective-permute-start.18) | collective-permute-done | bytes 20512 | tf_op jit(solution)/shard_map/ppermute | solution.py:720
  156.4 2.4 %collective-permute-start.21 = (f32[5,1024]{1,0:T(8,128)S(1)}, f32[5,1024]{1,0:T(8,128)S(1)}, u32[]{:S(2)}, u32[]{:S(2)}) collective-permute-start(f32[5,1024]{1,0:T(8,128)S(1)} %add_add_fusion.2), channel_id=1, source_target_pairs={{0,64},{16,80},{32,96},{48,112},{64,0},{80,16},{96,32},{112,48},{1... | collective-permute-start | bytes 61448 | tf_op jit(solution)/shard_map/ppermute | solution.py:48
  159.1 2.9 %collective-permute-start.23 = (f32[5,1024]{1,0:T(8,128)S(1)}, f32[5,1024]{1,0:T(8,128)S(1)}, u32[]{:S(2)}, u32[]{:S(2)}) collective-permute-start(f32[5,1024]{1,0:T(8,128)S(1)} %add_add_fusion.2), channel_id=1, source_target_pairs={{0,96},{16,112},{32,0},{48,16},{64,32},{80,48},{96,64},{112,80},{1... | collective-permute-start | bytes 61448 | tf_op jit(solution)/shard_map/ppermute | solution.py:48
  162.2 2.6 %collective-permute-start.29 = (bf16[800,256]{1,0:T(8,128)(2,1)S(1)}, bf16[800,256]{1,0:T(8,128)(2,1)S(1)}, u32[]{:S(2)}, u32[]{:S(2)}) collective-permute-start(bf16[800,256]{1,0:T(8,128)(2,1)S(1)} %add_convert_fusion.part_0), channel_id=1, source_target_pairs={{0,64},{16,80},{32,96},{48,112},{64,0},{80,16},{96,32},{112,48},{1... | collective-permute-start | bytes 1228808 | tf_op jit(solution)/shard_map/ppermute | solution.py:48
  165.5 3.3 %collective-permute-start.24 = (f32[5,1024]{1,0:T(8,128)S(1)}, f32[5,1024]{1,0:T(8,128)S(1)}, u32[]{:S(2)}, u32[]{:S(2)}) collective-permute-start(f32[5,1024]{1,0:T(8,128)S(1)} %add_add_fusion.1), channel_id=1, source_target_pairs={{0,8},{1,9},{2,10},{3,11},{4,12},{5,13},{6,14},{7,15},{8,0},{9,1},... | collective-permute-start | bytes 61448 | tf_op jit(solution)/shard_map/ppermute | solution.py:68
  171.0 3.1 %collective-permute-start.26 = (f32[5,1024]{1,0:T(8,128)S(1)}, f32[5,1024]{1,0:T(8,128)S(1)}, u32[]{:S(2)}, u32[]{:S(2)}) collective-permute-start(f32[5,1024]{1,0:T(8,128)S(1)} %add_add_fusion.1), channel_id=1, source_target_pairs={{0,12},{1,13},{2,14},{3,15},{4,0},{5,1},{6,2},{7,3},{8,4},{9,5},{1... | collective-permute-start | bytes 61448 | tf_op jit(solution)/shard_map/ppermute | solution.py:68
  174.7 2.7 %finish_out.1 = bf16[128,1024]{1,0:T(8,128)(2,1)} custom-call(bf16[8,128,1024]{2,1,0:T(8,128)(2,1)} %copy-done.1, bf16[128,1024]{1,0:T(8,128)(2,1)} %tokens.3, bf16[1,1024]{1,0:T(2,128)(2,1)} %broadcast_in_dim.29.out_bias), custom_call_target="tpu_custom_call" | custom-call | flops 1 | bytes 1 | tf_op jit(solution)/shard_map/finish_out/pallas_call | solution.py:729
  178.8 2.6 %fold.1 = (f32[128,1024]{1,0:T(8,128)}, bf16[128,1024]{1,0:T(8,128)(2,1)}) custom-call(bf16[4,256,1024]{2,1,0:T(8,128)(2,1)} %copy-done.2), custom_call_target="tpu_custom_call" | custom-call | flops 1 | bytes 1 | tf_op jit(solution)/shard_map/fold/pallas_call | solution.py:746
  183.4 3.2 %finish_grads.1 = (f32[192,1024]{1,0:T(8,128)}, f32[1,192]{1,0:T(1,128)}, f32[64,1024]{1,0:T(8,128)}, f32[1024,256]{1,0:T(8,128)}, f32[1,256]{1,0:T(1,128)}, /*index=5*/f32[256,1024]{1,0:T(8,128)}) custom-call(bf16[800,256]{1,0:T(8,128)(2,1)} %copy-done.6, bf16[800,256]{1,0:T(8,128)(2,1)} %copy-done.12, bf16[800,256]{1,0:T(8,128)(2,1)} %copy-done.13, ...), custom_call_target="tpu_custom_call" | custom-call | flops 1 | bytes 1 | tf_op jit(solution)/shard_map/finish_grads/pallas_call | solution.py:735
  (127 shorter events, 34.1 us)
Async XLA Ops:
  3.2 37.2 %all-to-all-start = ((bf16[8,128,1024]{2,1,0:T(8,128)(2,1)}), bf16[8,128,1024]{2,1,0:T(8,128)(2,1)S(1)}, u32[]{:S(2)}, u32[]{:S(2)}) async-start(bf16[8,128,1024]{2,1,0:T(8,128)(2,1)} %broadcast_in_dim.28), calls=%async_computation | async-start | bytes 4194304 | tf_op jit(solution)/shard_map/all_to_all | solution.py:35
  9.3 6.4 %collective-permute-start.3 = (bf16[1024,256]{1,0:T(8,128)(2,1)S(1)}, bf16[1024,256]{1,0:T(8,128)(2,1)}, u32[]{:S(2)}, u32[]{:S(2)}) collective-permute-start(bf16[1024,256]{1,0:T(8,128)(2,1)S(1)} %copy-done.3), channel_id=1, source_target_pairs={{0,1},{1,0},{2,3},{3,2},{4,5},{5,4},{6,7},{7,6},{8,9},{9,8},{10,11... | collective-permute-start | bytes 1572872 | tf_op jit(solution)/shard_map/ppermute | solution.py:31
  42.5 36.6 %all-to-all-start.1 = ((bf16[8,128,1024]{2,1,0:T(8,128)(2,1)}), bf16[8,128,1024]{2,1,0:T(8,128)(2,1)}, u32[]{:S(2)}, u32[]{:S(2)}) async-start(bf16[8,128,1024]{2,1,0:T(8,128)(2,1)} %broadcast_in_dim.24), calls=%async_computation.1 | async-start | bytes 4194304 | tf_op jit(solution)/shard_map/all_to_all | solution.py:35
  79.1 44.9 %all-to-all-start.2 = ((bf16[8,128,1024]{2,1,0:T(8,128)(2,1)}), bf16[8,128,1024]{2,1,0:T(8,128)(2,1)S(1)}, u32[]{:S(2)}, u32[]{:S(2)}) async-start(bf16[8,128,1024]{2,1,0:T(8,128)(2,1)} %mix.1), calls=%async_computation.2 | async-start | bytes 4194304 | tf_op jit(solution)/shard_map/all_to_all | solution.py:35
  97.3 26.7 %collective-permute-start.8 = (bf16[8,128,256]{2,1,0:T(8,128)(2,1)}, bf16[8,128,256]{2,1,0:T(8,128)(2,1)S(1)}, u32[]{:S(2)}, u32[]{:S(2)}) collective-permute-start(bf16[8,128,256]{2,1,0:T(8,128)(2,1)} %get-tuple-element.101), channel_id=1, source_target_pairs={{0,1},{1,0},{2,3},{3,2},{4,5},{5,4},{6,7},{7,6},{8,9},{9,8},{10,11... | collective-permute-start | bytes 1572872 | tf_op jit(solution)/shard_map/ppermute | solution.py:31
  97.5 26.5 %collective-permute-start.10 = (bf16[528,256]{1,0:T(8,128)(2,1)}, bf16[528,256]{1,0:T(8,128)(2,1)S(1)}, u32[]{:S(2)}, u32[]{:S(2)}) collective-permute-start(bf16[528,256]{1,0:T(8,128)(2,1)} %get-tuple-element.103), channel_id=1, source_target_pairs={{0,64},{16,80},{32,96},{48,112},{64,0},{80,16},{96,32},{112,48},{1... | collective-permute-start | bytes 811016 | tf_op jit(solution)/shard_map/ppermute | solution.py:48
  100.6 23.5 %collective-permute-start.11 = (bf16[528,256]{1,0:T(8,128)(2,1)}, bf16[528,256]{1,0:T(8,128)(2,1)S(1)}, u32[]{:S(2)}, u32[]{:S(2)}) collective-permute-start(bf16[528,256]{1,0:T(8,128)(2,1)} %get-tuple-element.104), channel_id=1, source_target_pairs={{0,96},{16,112},{32,0},{48,16},{64,32},{80,48},{96,64},{112,80},{1... | collective-permute-start | bytes 811016 | tf_op jit(solution)/shard_map/ppermute | solution.py:48
  101.7 22.4 %collective-permute-start.9 = (bf16[528,256]{1,0:T(8,128)(2,1)}, bf16[528,256]{1,0:T(8,128)(2,1)S(1)}, u32[]{:S(2)}, u32[]{:S(2)}) collective-permute-start(bf16[528,256]{1,0:T(8,128)(2,1)} %get-tuple-element.102), channel_id=1, source_target_pairs={{0,32},{16,48},{32,64},{48,80},{64,96},{80,112},{96,0},{112,16},{1... | collective-permute-start | bytes 811016 | tf_op jit(solution)/shard_map/ppermute | solution.py:48
  124.2 11.5 %collective-permute-start.14 = (bf16[272,256]{1,0:T(8,128)(2,1)}, bf16[272,256]{1,0:T(8,128)(2,1)}, u32[]{:S(2)}, u32[]{:S(2)}) collective-permute-start(bf16[272,256]{1,0:T(8,128)(2,1)} %get-tuple-element.111), channel_id=1, source_target_pairs={{0,32},{16,48},{32,64},{48,80},{64,96},{80,112},{96,0},{112,16},{1... | collective-permute-start | bytes 417800 | tf_op jit(solution)/shard_map/ppermute | solution.py:48
  124.9 10.8 %collective-permute-start.15 = (bf16[272,256]{1,0:T(8,128)(2,1)}, bf16[272,256]{1,0:T(8,128)(2,1)}, u32[]{:S(2)}, u32[]{:S(2)}) collective-permute-start(bf16[272,256]{1,0:T(8,128)(2,1)} %get-tuple-element.112), channel_id=1, source_target_pairs={{0,64},{16,80},{32,96},{48,112},{64,0},{80,16},{96,32},{112,48},{1... | collective-permute-start | bytes 417800 | tf_op jit(solution)/shard_map/ppermute | solution.py:48
  128.1 7.6 %collective-permute-start.16 = (bf16[272,256]{1,0:T(8,128)(2,1)}, bf16[272,256]{1,0:T(8,128)(2,1)}, u32[]{:S(2)}, u32[]{:S(2)}) collective-permute-start(bf16[272,256]{1,0:T(8,128)(2,1)} %get-tuple-element.113), channel_id=1, source_target_pairs={{0,96},{16,112},{32,0},{48,16},{64,32},{80,48},{96,64},{112,80},{1... | collective-permute-start | bytes 417800 | tf_op jit(solution)/shard_map/ppermute | solution.py:48
  128.1 7.6 %collective-permute-start.13 = (f32[5,1024]{1,0:T(8,128)}, f32[5,1024]{1,0:T(8,128)S(1)}, u32[]{:S(2)}, u32[]{:S(2)}) collective-permute-start(f32[5,1024]{1,0:T(8,128)} %get-tuple-element.124), channel_id=1, source_target_pairs={{0,1},{1,0},{2,3},{3,2},{4,5},{5,4},{6,7},{7,6},{8,9},{9,8},{10,11... | collective-permute-start | bytes 61448 | tf_op jit(solution)/shard_map/ppermute | solution.py:31
  135.7 41.7 %all-to-all-start.3 = ((bf16[4,256,1024]{2,1,0:T(8,128)(2,1)}), bf16[4,256,1024]{2,1,0:T(8,128)(2,1)S(1)}, u32[]{:S(2)}, u32[]{:S(2)}) async-start(bf16[4,256,1024]{2,1,0:T(8,128)(2,1)} %bitcast.24), calls=%async_computation.3 | async-start | bytes 4194304 | tf_op jit(solution)/shard_map/all_to_all | solution.py:39
  141.2 15.2 %collective-permute-start.17 = (bf16[800,256]{1,0:T(8,128)(2,1)S(1)}, bf16[800,256]{1,0:T(8,128)(2,1)S(1)}, u32[]{:S(2)}, u32[]{:S(2)}) collective-permute-start(bf16[800,256]{1,0:T(8,128)(2,1)S(1)} %pad_maximum_fusion), channel_id=1, source_target_pairs={{0,16},{16,0},{32,48},{48,32},{64,80},{80,64},{96,112},{112,96},{1... | collective-permute-start | bytes 1228808 | tf_op jit(solution)/shard_map/ppermute | solution.py:717
  144.8 11.5 %collective-permute-start.18 = (f32[5,1024]{1,0:T(8,128)S(1)}, f32[5,1024]{1,0:T(8,128)S(1)}, u32[]{:S(2)}, u32[]{:S(2)}) collective-permute-start(f32[5,1024]{1,0:T(8,128)S(1)} %add.57), channel_id=1, source_target_pairs={{0,2},{1,3},{2,0},{3,1},{4,6},{5,7},{6,4},{7,5},{8,10},{9,11},{10,... | collective-permute-start | bytes 61448 | tf_op jit(solution)/shard_map/ppermute | solution.py:720
  145.8 10.6 %collective-permute-start.19 = (f32[5,1024]{1,0:T(8,128)S(1)}, f32[5,1024]{1,0:T(8,128)S(1)}, u32[]{:S(2)}, u32[]{:S(2)}) collective-permute-start(f32[5,1024]{1,0:T(8,128)S(1)} %add.57), channel_id=1, source_target_pairs={{0,16},{16,0},{32,48},{48,32},{64,80},{80,64},{96,112},{112,96},{1... | collective-permute-start | bytes 61448 | tf_op jit(solution)/shard_map/ppermute | solution.py:721
  146.9 9.4 %collective-permute-start.20 = (f32[5,1024]{1,0:T(8,128)S(1)}, f32[5,1024]{1,0:T(8,128)S(1)}, u32[]{:S(2)}, u32[]{:S(2)}) collective-permute-start(f32[5,1024]{1,0:T(8,128)S(1)} %add.57), channel_id=1, source_target_pairs={{0,18},{1,19},{2,16},{3,17},{4,22},{5,23},{6,20},{7,21},{8,26},{9,... | collective-permute-start | bytes 61448 | tf_op jit(solution)/shard_map/ppermute | solution.py:723
  156.4 8.5 %collective-permute-start.21 = (f32[5,1024]{1,0:T(8,128)S(1)}, f32[5,1024]{1,0:T(8,128)S(1)}, u32[]{:S(2)}, u32[]{:S(2)}) collective-permute-start(f32[5,1024]{1,0:T(8,128)S(1)} %add_add_fusion.2), channel_id=1, source_target_pairs={{0,64},{16,80},{32,96},{48,112},{64,0},{80,16},{96,32},{112,48},{1... | collective-permute-start | bytes 61448 | tf_op jit(solution)/shard_map/ppermute | solution.py:48
  158.8 6.7 %collective-permute-start.22 = (f32[5,1024]{1,0:T(8,128)S(1)}, f32[5,1024]{1,0:T(8,128)S(1)}, u32[]{:S(2)}, u32[]{:S(2)}) collective-permute-start(f32[5,1024]{1,0:T(8,128)S(1)} %add_add_fusion.2), channel_id=1, source_target_pairs={{0,32},{16,48},{32,64},{48,80},{64,96},{80,112},{96,0},{112,16},{1... | collective-permute-start | bytes 61448 | tf_op jit(solution)/shard_map/ppermute | solution.py:48
  162.1 20.4 %collective-permute-start.28 = (bf16[800,256]{1,0:T(8,128)(2,1)S(1)}, bf16[800,256]{1,0:T(8,128)(2,1)S(1)}, u32[]{:S(2)}, u32[]{:S(2)}) collective-permute-start(bf16[800,256]{1,0:T(8,128)(2,1)S(1)} %add_convert_fusion.part_0), channel_id=1, source_target_pairs={{0,32},{16,48},{32,64},{48,80},{64,96},{80,112},{96,0},{112,16},{1... | collective-permute-start | bytes 1228808 | tf_op jit(solution)/shard_map/ppermute | solution.py:48
  162.2 20.3 %collective-permute-start.29 = (bf16[800,256]{1,0:T(8,128)(2,1)S(1)}, bf16[800,256]{1,0:T(8,128)(2,1)S(1)}, u32[]{:S(2)}, u32[]{:S(2)}) collective-permute-start(bf16[800,256]{1,0:T(8,128)(2,1)S(1)} %add_convert_fusion.part_0), channel_id=1, source_target_pairs={{0,64},{16,80},{32,96},{48,112},{64,0},{80,16},{96,32},{112,48},{1... | collective-permute-start | bytes 1228808 | tf_op jit(solution)/shard_map/ppermute | solution.py:48
  164.8 17.9 %collective-permute-start.30 = (bf16[800,256]{1,0:T(8,128)(2,1)S(1)}, bf16[800,256]{1,0:T(8,128)(2,1)}, u32[]{:S(2)}, u32[]{:S(2)}) collective-permute-start(bf16[800,256]{1,0:T(8,128)(2,1)S(1)} %add_convert_fusion.part_0), channel_id=1, source_target_pairs={{0,96},{16,112},{32,0},{48,16},{64,32},{80,48},{96,64},{112,80},{1... | collective-permute-start | bytes 1228808 | tf_op jit(solution)/shard_map/ppermute | solution.py:48
  168.8 8.6 %collective-permute-start.25 = (f32[5,1024]{1,0:T(8,128)S(1)}, f32[5,1024]{1,0:T(8,128)S(1)}, u32[]{:S(2)}, u32[]{:S(2)}) collective-permute-start(f32[5,1024]{1,0:T(8,128)S(1)} %add_add_fusion.1), channel_id=1, source_target_pairs={{0,4},{1,5},{2,6},{3,7},{4,8},{5,9},{6,10},{7,11},{8,12},{9,13},{1... | collective-permute-start | bytes 61448 | tf_op jit(solution)/shard_map/ppermute | solution.py:68
  181.4 6.6 %collective-permute-start.27 = (bf16[128,1024]{1,0:T(8,128)(2,1)}, bf16[128,1024]{1,0:T(8,128)(2,1)S(1)}, u32[]{:S(2)}, u32[]{:S(2)}) collective-permute-start(bf16[128,1024]{1,0:T(8,128)(2,1)} %get-tuple-element.130), channel_id=1, source_target_pairs={{0,2},{1,3},{2,0},{3,1},{4,6},{5,7},{6,4},{7,5},{8,10},{9,11},{10,... | collective-permute-start | bytes 786440 | tf_op jit(solution)/shard_map/ppermute | solution.py:754
  (37 other events, 252.8 us)

commit v5 on v4

--- a/solution.py
+++ b/solution.py
@@ -721,17 +721,19 @@
     far = lax.ppermute(small, "dp", Z_PAIR)
     both_z = [(d * 16 + t, (d ^ 1) * 16 + (t ^ 2)) for d in range(8) for t in range(16)]
     across = lax.ppermute(small, ("dp", "tensor"), both_z)
-    other_half, small = lax.optimization_barrier((other_half, (small + near) + (far + across)))
-    small = sum_four(small, move_x)
-    parts = spread_x(add_low(half, other_half))
-    small = sum_four(small, move_y)
-
     layer_out = pl.pallas_call(
         finish_out_kernel,
         name="finish_out",
         out_shape=shape(tokens.shape, LOW),
         cost_estimate=COST,
     )(branch, tokens, out_bias[None, :])
+    other_half, small, layer_out = lax.optimization_barrier(
+        (other_half, (small + near) + (far + across), layer_out)
+    )
+    small = sum_four(small, move_x)
+    parts = spread_x(add_low(half, other_half))
+
+
     grad_qkv, grad_qkv_bias, grad_out, grad_up, grad_up_bias, grad_down = pl.pallas_call(
         finish_grads_kernel,
         name="finish_grads",
@@ -742,7 +744,7 @@
         ],
         cost_estimate=COST,
     )(*parts)
-    scaled, layer_out, small = lax.optimization_barrier((scaled, layer_out, small))
+    scaled, small = lax.optimization_barrier((scaled, small))
     keep, send = pl.pallas_call(
         fold_kernel,
         name="fold",
@@ -752,6 +754,7 @@
         cost_estimate=COST,
     )(scaled)
     received = lax.ppermute(send, "tensor", Z_NEAR)
+    small = sum_four(small, move_y)
     input_grad = pl.pallas_call(
         finish_back_kernel,
         name="finish_back",

time: 192 us -> 207 us (1.078)
  waiting for transfers between devices: 39.3 us -> 54.8 us
    ppermute x12, waiting for transfers between devices: 0.22 us -> 16.6 us  [move_x(): return lax.ppermute(value, 'dp', pairs)]
    ppermute x1, waiting for transfers between devices: 0.71 us -> 4.8 us  [per_device(): received = lax.ppermute(send, 'tensor', Z_NEAR)]
    ppermute x1, waiting for transfers between devices: 6.73 us -> 3.42 us  [per_device(): near = lax.ppermute(small, 'tensor', Z_NEAR)]
    unnamed x52 -> x48, local copies, waits for them, and re-layouts: 6.2 us -> 4.21 us
  transfers between devices with their start and end apart: 35 -> 35, of which waited for: 8 -> 8; matrix products, arithmetic and copies ran while one was open for 3% -> 3% of each run, Pallas kernels for 40% -> 38%
where the time goes in v5:
time: 207 us; the launch traced here: 205 us
  Pallas kernels  79.3 us (38%)
  starting transfers between devices  54.8 us (26%)
  waiting for transfers between devices  54.8 us (26%)
  local copies, waits for them, and re-layouts  9.88 us (5%)
  other arithmetic  5.23 us (3%)
    all_to_all x3, waiting for transfers between devices, trade_chips(): lax.all_to_all(blocks, 'tensor', 0, 0, axis_index_groups=SAME_CORE, tiled...  27 us
    pallas_call x1, Pallas kernels, per_device(): launch(attend_back_kernel, 'attend_back', [whole((LEN, HEAD)), whole((LEN...  21.4 us
    pallas_call x1, Pallas kernels, per_device(): launch(forward_kernel, 'forward', [LEFT, LEFT, whole((4, model)), whole((...  20 us
    ppermute x12, starting transfers between devices, move_x(): return lax.ppermute(value, 'dp', pairs)  18.7 us
    ppermute x12, waiting for transfers between devices, move_x(): return lax.ppermute(value, 'dp', pairs)  16.6 us
    all_to_all x3, starting transfers between devices, trade_chips(): lax.all_to_all(blocks, 'tensor', 0, 0, axis_index_groups=SAME_CORE, tiled...  14 us
    pallas_call x1, Pallas kernels, per_device(): launch(feed_back_kernel, 'feed_back', [*[LEFT] * 7, whole((4, model)), by...  13.7 us
    pallas_call x1, Pallas kernels, per_device(): launch(input_back_kernel, 'input_back', [LEFT] * 4 + [whole((4, model))]...  6.78 us
  transfers between devices with their start and end apart: 35, of which 8 were waited for; matrix products, arithmetic and copies ran while one was open for 3% of the time, Pallas kernels for 38%

profile of v5, /device:TPU:0, one launch (start us, length us, event | category | flops | bytes accessed | tf_op | source)
XLA Modules:
  0.0 205.1 jit_solution(16692792368034599715)
XLA Ops:
  0.6 2.6 %broadcast_in_dim.28 = bf16[8,128,1024]{2,1,0:T(8,128)(2,1)} broadcast(bf16[128,1024]{1,0:T(8,128)(2,1)} %tokens.3), dimensions={1,2} | broadcast | bytes 2359296 | tf_op jit(solution)/shard_map/broadcast_in_dim | solution.py:43
  3.3 6.1 %all-to-all-start = ((bf16[8,128,1024]{2,1,0:T(8,128)(2,1)}), bf16[8,128,1024]{2,1,0:T(8,128)(2,1)S(1)}, u32[]{:S(2)}, u32[]{:S(2)}) async-start(bf16[8,128,1024]{2,1,0:T(8,128)(2,1)} %broadcast_in_dim.28), calls=%async_computation | async-start | bytes 4194304 | tf_op jit(solution)/shard_map/all_to_all | solution.py:35
  15.8 24.7 %all-to-all-done.mine.tokens_mine = bf16[8,128,1024]{2,1,0:T(8,128)(2,1)S(1)} async-done(((bf16[8,128,1024]{2,1,0:T(8,128)(2,1)}), bf16[8,128,1024]{2,1,0:T(8,128)(2,1)S(1)}, u32[]{:S(2)}, u32[]{:S(2)}) %all-to-all-start) | async-done | bytes 2097184 | tf_op jit(solution)/shard_map/all_to_all | solution.py:35
  42.5 4.3 %all-to-all-start.1 = ((bf16[8,128,1024]{2,1,0:T(8,128)(2,1)}), bf16[8,128,1024]{2,1,0:T(8,128)(2,1)}, u32[]{:S(2)}, u32[]{:S(2)}) async-start(bf16[8,128,1024]{2,1,0:T(8,128)(2,1)} %broadcast_in_dim.24), calls=%async_computation.1 | async-start | bytes 4194304 | tf_op jit(solution)/shard_map/all_to_all | solution.py:35
  46.9 20.0 %forward.1 = (f32[2048,128]{1,0:T(8,128)}, bf16[2048,64]{1,0:T(8,128)(2,1)}, bf16[2048,64]{1,0:T(8,128)(2,1)}, bf16[2048,64]{1,0:T(8,128)(2,1)}, bf16[2048,256]{...) custom-call(bf16[8,128,1024]{2,1,0:T(8,128)(2,1)} %copy-done, ...), custom_call_target="tpu_custom_call" | custom-call | flops 1 | bytes 1 | tf_op jit(solution)/shard_map/forward/pallas_call | solution.py:600
  70.3 6.5 %mix.1 = bf16[8,128,1024]{2,1,0:T(8,128)(2,1)} custom-call(bf16[8,2,128,64]{3,2,1,0:T(8,128)(2,1)} %bitcast.34, bf16[8,2,128,256]{3,2,1,0:T(8,128)(2,1)} %bitcast.27, bf16[8,128,64]{2,1,0:T(8,128)(2,1)} %copy-done.15, bf16[8,128,256]{2,1,0:T(8,128)(2,1)} %copy-done.11, bf16[64,1024]{1,0:T(8,128)(2,1)} %bitcast.36, bf16[256,1024]{1,0:T(8,128)(2,1)} %w_down.3, ...), custom_call_target="tpu_custom_call" | custom-call | flops 1 | bytes 1 | tf_op jit(solution)/shard_map/mix/pallas_call | solution.py:627
  79.1 3.6 %all-to-all-start.2 = ((bf16[8,128,1024]{2,1,0:T(8,128)(2,1)}), bf16[8,128,1024]{2,1,0:T(8,128)(2,1)S(1)}, u32[]{:S(2)}, u32[]{:S(2)}) async-start(bf16[8,128,1024]{2,1,0:T(8,128)(2,1)} %mix.1), calls=%async_computation.2 | async-start | bytes 4194304 | tf_op jit(solution)/shard_map/all_to_all | solution.py:35
  83.6 13.7 %feed_back.1 = (bf16[2048,256]{1,0:T(8,128)(2,1)}, bf16[8,128,256]{2,1,0:T(8,128)(2,1)}, bf16[2048,64]{1,0:T(8,128)(2,1)}, bf16[528,256]{1,0:T(8,128)(2,1)}, bf1...) custom-call(bf16[8,128,1024]{2,1,0:T(8,128)(2,1)} %all-to-all-done.1.mine, ...), custom_call_target="tpu_custom_call" | custom-call | flops 1 | bytes 1 | tf_op jit(solution)/shard_map/feed_back/pallas_call | solution.py:642
  97.5 3.0 %collective-permute-start.10 = (bf16[528,256]{1,0:T(8,128)(2,1)}, bf16[528,256]{1,0:T(8,128)(2,1)S(1)}, u32[]{:S(2)}, u32[]{:S(2)}) collective-permute-start(bf16[528,256]{1,0:T(8,128)(2,1)} %get-tuple-element.104), channel_id=1, source_target_pairs={{0,64},{16,80},{32,96},{48,112},{64,0},{80,16},{96,32},{112,48},{1... | collective-permute-start | bytes 811016 | tf_op jit(solution)/shard_map/ppermute | solution.py:48
  102.6 21.4 %attend_back.1 = (bf16[2048,192]{1,0:T(8,128)(2,1)}, bf16[8,128,192]{2,1,0:T(8,128)(2,1)}, bf16[272,256]{1,0:T(8,128)(2,1)}, bf16[272,256]{1,0:T(8,128)(2,1)}, b...) custom-call(bf16[2048,64]{1,0:T(8,128)(2,1)} %get-tuple-element.91.queries, ...), custom_call_target="tpu_custom_call" | custom-call | flops 1 | bytes 1 | tf_op jit(solution)/shard_map/attend_back/pallas_call | solution.py:668
  124.9 3.2 %collective-permute-start.15 = (bf16[272,256]{1,0:T(8,128)(2,1)}, bf16[272,256]{1,0:T(8,128)(2,1)}, u32[]{:S(2)}, u32[]{:S(2)}) collective-permute-start(bf16[272,256]{1,0:T(8,128)(2,1)} %get-tuple-element.117), channel_id=1, source_target_pairs={{0,64},{16,80},{32,96},{48,112},{64,0},{80,16},{96,32},{112,48},{1... | collective-permute-start | bytes 417800 | tf_op jit(solution)/shard_map/ppermute | solution.py:48
  128.9 6.8 %input_back.1 = bf16[8,128,1024]{2,1,0:T(8,128)(2,1)} custom-call(bf16[8,2,128,192]{3,2,1,0:T(8,128)(2,1)} %bitcast.35, bf16[8,2,128,256]{3,2,1,0:T(8,128)(2,1)} %bitcast.25, bf16[8,128,192]{2,1,0:T(8,128)(2,1)} %copy-done.9, bf16[8,128,256]{2,1,0:T(8,128)(2,1)} %copy-done.8, f32[4,1024]{1,0:T(4,128)} %maximum_convert_fusion.vecs, ...), custom_call_target="tpu_custom_call" | custom-call | flops 1 | bytes 1 | tf_op jit(solution)/shard_map/input_back/pallas_call | solution.py:700
  135.7 4.1 %all-to-all-start.3 = ((bf16[4,256,1024]{2,1,0:T(8,128)(2,1)}), bf16[4,256,1024]{2,1,0:T(8,128)(2,1)S(1)}, u32[]{:S(2)}, u32[]{:S(2)}) async-start(bf16[4,256,1024]{2,1,0:T(8,128)(2,1)} %bitcast.24), calls=%async_computation.3 | async-start | bytes 4194304 | tf_op jit(solution)/shard_map/all_to_all | solution.py:39
  141.2 3.7 %collective-permute-start.17 = (bf16[800,256]{1,0:T(8,128)(2,1)S(1)}, bf16[800,256]{1,0:T(8,128)(2,1)S(1)}, u32[]{:S(2)}, u32[]{:S(2)}) collective-permute-start(bf16[800,256]{1,0:T(8,128)(2,1)S(1)} %pad_maximum_fusion), channel_id=1, source_target_pairs={{0,16},{16,0},{32,48},{48,32},{64,80},{80,64},{96,112},{112,96},{1... | collective-permute-start | bytes 1228808 | tf_op jit(solution)/shard_map/ppermute | solution.py:717
  147.0 2.7 %collective-permute-start.20 = (f32[5,1024]{1,0:T(8,128)S(1)}, f32[5,1024]{1,0:T(8,128)S(1)}, u32[]{:S(2)}, u32[]{:S(2)}) collective-permute-start(f32[5,1024]{1,0:T(8,128)S(1)} %add.57), channel_id=1, source_target_pairs={{0,18},{1,19},{2,16},{3,17},{4,22},{5,23},{6,20},{7,21},{8,26},{9,... | collective-permute-start | bytes 61448 | tf_op jit(solution)/shard_map/ppermute | solution.py:723
  150.3 2.7 %finish_out.1 = bf16[128,1024]{1,0:T(8,128)(2,1)} custom-call(bf16[8,128,1024]{2,1,0:T(8,128)(2,1)} %copy-done.1, bf16[128,1024]{1,0:T(8,128)(2,1)} %tokens.3, bf16[1,1024]{1,0:T(2,128)(2,1)} %broadcast_in_dim.29.out_bias), custom_call_target="tpu_custom_call" | custom-call | flops 1 | bytes 1 | tf_op jit(solution)/shard_map/finish_out/pallas_call | solution.py:724
  153.0 3.4 %collective-permute-done.18 = f32[5,1024]{1,0:T(8,128)S(1)} collective-permute-done((f32[5,1024]{1,0:T(8,128)S(1)}, f32[5,1024]{1,0:T(8,128)S(1)}, u32[]{:S(2)}, u32[]{:S(2)}) %collective-permute-start.18) | collective-permute-done | bytes 20512 | tf_op jit(solution)/shard_map/ppermute | solution.py:720
  163.6 15.0 %collective-permute-done.21 = f32[5,1024]{1,0:T(8,128)S(1)} collective-permute-done((f32[5,1024]{1,0:T(8,128)S(1)}, f32[5,1024]{1,0:T(8,128)S(1)}, u32[]{:S(2)}, u32[]{:S(2)}) %collective-permute-start.21) | collective-permute-done | bytes 20512 | tf_op jit(solution)/shard_map/ppermute | solution.py:48
  178.6 2.7 %collective-permute-start.23 = (f32[5,1024]{1,0:T(8,128)S(1)}, f32[5,1024]{1,0:T(8,128)S(1)}, u32[]{:S(2)}, u32[]{:S(2)}) collective-permute-start(f32[5,1024]{1,0:T(8,128)S(1)} %add_add_fusion.2), channel_id=1, source_target_pairs={{0,96},{16,112},{32,0},{48,16},{64,32},{80,48},{96,64},{112,80},{1... | collective-permute-start | bytes 61448 | tf_op jit(solution)/shard_map/ppermute | solution.py:48
  182.9 3.4 %collective-permute-start.28 = (f32[5,1024]{1,0:T(8,128)S(1)}, f32[5,1024]{1,0:T(8,128)S(1)}, u32[]{:S(2)}, u32[]{:S(2)}) collective-permute-start(f32[5,1024]{1,0:T(8,128)S(1)} %add_add_fusion.1), channel_id=1, source_target_pairs={{0,8},{1,9},{2,10},{3,11},{4,12},{5,13},{6,14},{7,15},{8,0},{9,1},... | collective-permute-start | bytes 61448 | tf_op jit(solution)/shard_map/ppermute | solution.py:68
  186.9 2.7 %collective-permute-start.30 = (f32[5,1024]{1,0:T(8,128)S(1)}, f32[5,1024]{1,0:T(8,128)S(1)}, u32[]{:S(2)}, u32[]{:S(2)}) collective-permute-start(f32[5,1024]{1,0:T(8,128)S(1)} %add_add_fusion.1), channel_id=1, source_target_pairs={{0,12},{1,13},{2,14},{3,15},{4,0},{5,1},{6,2},{7,3},{8,4},{9,5},{1... | collective-permute-start | bytes 61448 | tf_op jit(solution)/shard_map/ppermute | solution.py:68
  189.6 3.2 %finish_grads.1 = (f32[192,1024]{1,0:T(8,128)}, f32[1,192]{1,0:T(1,128)}, f32[64,1024]{1,0:T(8,128)}, f32[1024,256]{1,0:T(8,128)}, f32[1,256]{1,0:T(1,128)}, /*index=5*/f32[256,1024]{1,0:T(8,128)}) custom-call(bf16[800,256]{1,0:T(8,128)(2,1)} %copy-done.6, bf16[800,256]{1,0:T(8,128)(2,1)} %copy-done.12, bf16[800,256]{1,0:T(8,128)(2,1)} %collective-permute-done.26.part_2, ...), custom_call_target="tpu_custom_call" | custom-call | flops 1 | bytes 1 | tf_op jit(solution)/shard_map/finish_grads/pallas_call | solution.py:737
  192.8 2.6 %fold.1 = (f32[128,1024]{1,0:T(8,128)}, bf16[128,1024]{1,0:T(8,128)(2,1)}) custom-call(bf16[4,256,1024]{2,1,0:T(8,128)(2,1)} %copy-done.2), custom_call_target="tpu_custom_call" | custom-call | flops 1 | bytes 1 | tf_op jit(solution)/shard_map/fold/pallas_call | solution.py:748
  197.2 4.8 %collective-permute-done.24.part = bf16[128,1024]{1,0:T(8,128)(2,1)S(1)} collective-permute-done((bf16[128,1024]{1,0:T(8,128)(2,1)}, bf16[128,1024]{1,0:T(8,128)(2,1)S(1)}, u32[]{:S(2)}, u32[]{:S(2)}) %collective-permute-start.24) | collective-permute-done | bytes 262176 | tf_op jit(solution)/shard_map/ppermute | solution.py:756
  (123 shorter events, 37.2 us)
Async XLA Ops:
  3.3 37.2 %all-to-all-start = ((bf16[8,128,1024]{2,1,0:T(8,128)(2,1)}), bf16[8,128,1024]{2,1,0:T(8,128)(2,1)S(1)}, u32[]{:S(2)}, u32[]{:S(2)}) async-start(bf16[8,128,1024]{2,1,0:T(8,128)(2,1)} %broadcast_in_dim.28), calls=%async_computation | async-start | bytes 4194304 | tf_op jit(solution)/shard_map/all_to_all | solution.py:35
  42.5 36.6 %all-to-all-start.1 = ((bf16[8,128,1024]{2,1,0:T(8,128)(2,1)}), bf16[8,128,1024]{2,1,0:T(8,128)(2,1)}, u32[]{:S(2)}, u32[]{:S(2)}) async-start(bf16[8,128,1024]{2,1,0:T(8,128)(2,1)} %broadcast_in_dim.24), calls=%async_computation.1 | async-start | bytes 4194304 | tf_op jit(solution)/shard_map/all_to_all | solution.py:35
  79.1 44.9 %all-to-all-start.2 = ((bf16[8,128,1024]{2,1,0:T(8,128)(2,1)}), bf16[8,128,1024]{2,1,0:T(8,128)(2,1)S(1)}, u32[]{:S(2)}, u32[]{:S(2)}) async-start(bf16[8,128,1024]{2,1,0:T(8,128)(2,1)} %mix.1), calls=%async_computation.2 | async-start | bytes 4194304 | tf_op jit(solution)/shard_map/all_to_all | solution.py:35
  97.4 26.7 %collective-permute-start.8 = (bf16[8,128,256]{2,1,0:T(8,128)(2,1)}, bf16[8,128,256]{2,1,0:T(8,128)(2,1)S(1)}, u32[]{:S(2)}, u32[]{:S(2)}) collective-permute-start(bf16[8,128,256]{2,1,0:T(8,128)(2,1)} %get-tuple-element.102), channel_id=1, source_target_pairs={{0,1},{1,0},{2,3},{3,2},{4,5},{5,4},{6,7},{7,6},{8,9},{9,8},{10,11... | collective-permute-start | bytes 1572872 | tf_op jit(solution)/shard_map/ppermute | solution.py:31
  97.5 26.5 %collective-permute-start.10 = (bf16[528,256]{1,0:T(8,128)(2,1)}, bf16[528,256]{1,0:T(8,128)(2,1)S(1)}, u32[]{:S(2)}, u32[]{:S(2)}) collective-permute-start(bf16[528,256]{1,0:T(8,128)(2,1)} %get-tuple-element.104), channel_id=1, source_target_pairs={{0,64},{16,80},{32,96},{48,112},{64,0},{80,16},{96,32},{112,48},{1... | collective-permute-start | bytes 811016 | tf_op jit(solution)/shard_map/ppermute | solution.py:48
  100.6 23.5 %collective-permute-start.11 = (bf16[528,256]{1,0:T(8,128)(2,1)}, bf16[528,256]{1,0:T(8,128)(2,1)S(1)}, u32[]{:S(2)}, u32[]{:S(2)}) collective-permute-start(bf16[528,256]{1,0:T(8,128)(2,1)} %get-tuple-element.105), channel_id=1, source_target_pairs={{0,96},{16,112},{32,0},{48,16},{64,32},{80,48},{96,64},{112,80},{1... | collective-permute-start | bytes 811016 | tf_op jit(solution)/shard_map/ppermute | solution.py:48
  101.7 22.4 %collective-permute-start.9 = (bf16[528,256]{1,0:T(8,128)(2,1)}, bf16[528,256]{1,0:T(8,128)(2,1)S(1)}, u32[]{:S(2)}, u32[]{:S(2)}) collective-permute-start(bf16[528,256]{1,0:T(8,128)(2,1)} %get-tuple-element.103), channel_id=1, source_target_pairs={{0,32},{16,48},{32,64},{48,80},{64,96},{80,112},{96,0},{112,16},{1... | collective-permute-start | bytes 811016 | tf_op jit(solution)/shard_map/ppermute | solution.py:48
  124.2 11.5 %collective-permute-start.14 = (bf16[272,256]{1,0:T(8,128)(2,1)}, bf16[272,256]{1,0:T(8,128)(2,1)}, u32[]{:S(2)}, u32[]{:S(2)}) collective-permute-start(bf16[272,256]{1,0:T(8,128)(2,1)} %get-tuple-element.116), channel_id=1, source_target_pairs={{0,32},{16,48},{32,64},{48,80},{64,96},{80,112},{96,0},{112,16},{1... | collective-permute-start | bytes 417800 | tf_op jit(solution)/shard_map/ppermute | solution.py:48
  124.9 10.9 %collective-permute-start.15 = (bf16[272,256]{1,0:T(8,128)(2,1)}, bf16[272,256]{1,0:T(8,128)(2,1)}, u32[]{:S(2)}, u32[]{:S(2)}) collective-permute-start(bf16[272,256]{1,0:T(8,128)(2,1)} %get-tuple-element.117), channel_id=1, source_target_pairs={{0,64},{16,80},{32,96},{48,112},{64,0},{80,16},{96,32},{112,48},{1... | collective-permute-start | bytes 417800 | tf_op jit(solution)/shard_map/ppermute | solution.py:48
  128.1 7.6 %collective-permute-start.16 = (bf16[272,256]{1,0:T(8,128)(2,1)}, bf16[272,256]{1,0:T(8,128)(2,1)}, u32[]{:S(2)}, u32[]{:S(2)}) collective-permute-start(bf16[272,256]{1,0:T(8,128)(2,1)} %get-tuple-element.118), channel_id=1, source_target_pairs={{0,96},{16,112},{32,0},{48,16},{64,32},{80,48},{96,64},{112,80},{1... | collective-permute-start | bytes 417800 | tf_op jit(solution)/shard_map/ppermute | solution.py:48
  128.1 7.6 %collective-permute-start.13 = (f32[5,1024]{1,0:T(8,128)}, f32[5,1024]{1,0:T(8,128)S(1)}, u32[]{:S(2)}, u32[]{:S(2)}) collective-permute-start(f32[5,1024]{1,0:T(8,128)} %get-tuple-element.122), channel_id=1, source_target_pairs={{0,1},{1,0},{2,3},{3,2},{4,5},{5,4},{6,7},{7,6},{8,9},{9,8},{10,11... | collective-permute-start | bytes 61448 | tf_op jit(solution)/shard_map/ppermute | solution.py:31
  135.7 47.1 %all-to-all-start.3 = ((bf16[4,256,1024]{2,1,0:T(8,128)(2,1)}), bf16[4,256,1024]{2,1,0:T(8,128)(2,1)S(1)}, u32[]{:S(2)}, u32[]{:S(2)}) async-start(bf16[4,256,1024]{2,1,0:T(8,128)(2,1)} %bitcast.24), calls=%async_computation.3 | async-start | bytes 4194304 | tf_op jit(solution)/shard_map/all_to_all | solution.py:39
  141.2 15.2 %collective-permute-start.17 = (bf16[800,256]{1,0:T(8,128)(2,1)S(1)}, bf16[800,256]{1,0:T(8,128)(2,1)S(1)}, u32[]{:S(2)}, u32[]{:S(2)}) collective-permute-start(bf16[800,256]{1,0:T(8,128)(2,1)S(1)} %pad_maximum_fusion), channel_id=1, source_target_pairs={{0,16},{16,0},{32,48},{48,32},{64,80},{80,64},{96,112},{112,96},{1... | collective-permute-start | bytes 1228808 | tf_op jit(solution)/shard_map/ppermute | solution.py:717
  144.9 11.5 %collective-permute-start.18 = (f32[5,1024]{1,0:T(8,128)S(1)}, f32[5,1024]{1,0:T(8,128)S(1)}, u32[]{:S(2)}, u32[]{:S(2)}) collective-permute-start(f32[5,1024]{1,0:T(8,128)S(1)} %add.57), channel_id=1, source_target_pairs={{0,2},{1,3},{2,0},{3,1},{4,6},{5,7},{6,4},{7,5},{8,10},{9,11},{10,... | collective-permute-start | bytes 61448 | tf_op jit(solution)/shard_map/ppermute | solution.py:720
  145.8 10.6 %collective-permute-start.19 = (f32[5,1024]{1,0:T(8,128)S(1)}, f32[5,1024]{1,0:T(8,128)S(1)}, u32[]{:S(2)}, u32[]{:S(2)}) collective-permute-start(f32[5,1024]{1,0:T(8,128)S(1)} %add.57), channel_id=1, source_target_pairs={{0,16},{16,0},{32,48},{48,32},{64,80},{80,64},{96,112},{112,96},{1... | collective-permute-start | bytes 61448 | tf_op jit(solution)/shard_map/ppermute | solution.py:721
  147.0 9.4 %collective-permute-start.20 = (f32[5,1024]{1,0:T(8,128)S(1)}, f32[5,1024]{1,0:T(8,128)S(1)}, u32[]{:S(2)}, u32[]{:S(2)}) collective-permute-start(f32[5,1024]{1,0:T(8,128)S(1)} %add.57), channel_id=1, source_target_pairs={{0,18},{1,19},{2,16},{3,17},{4,22},{5,23},{6,20},{7,21},{8,26},{9,... | collective-permute-start | bytes 61448 | tf_op jit(solution)/shard_map/ppermute | solution.py:723
  156.6 30.3 %collective-permute-start.25 = (bf16[800,256]{1,0:T(8,128)(2,1)S(1)}, bf16[800,256]{1,0:T(8,128)(2,1)S(1)}, u32[]{:S(2)}, u32[]{:S(2)}) collective-permute-start(bf16[800,256]{1,0:T(8,128)(2,1)S(1)} %add_convert_fusion.part_0), channel_id=1, source_target_pairs={{0,32},{16,48},{32,64},{48,80},{64,96},{80,112},{96,0},{112,16},{1... | collective-permute-start | bytes 1228808 | tf_op jit(solution)/shard_map/ppermute | solution.py:48
  158.6 30.9 %collective-permute-start.26 = (bf16[800,256]{1,0:T(8,128)(2,1)S(1)}, bf16[800,256]{1,0:T(8,128)(2,1)}, u32[]{:S(2)}, u32[]{:S(2)}) collective-permute-start(bf16[800,256]{1,0:T(8,128)(2,1)S(1)} %add_convert_fusion.part_0), channel_id=1, source_target_pairs={{0,64},{16,80},{32,96},{48,112},{64,0},{80,16},{96,32},{112,48},{1... | collective-permute-start | bytes 1228808 | tf_op jit(solution)/shard_map/ppermute | solution.py:48
  159.9 29.6 %collective-permute-start.27 = (bf16[800,256]{1,0:T(8,128)(2,1)S(1)}, bf16[800,256]{1,0:T(8,128)(2,1)}, u32[]{:S(2)}, u32[]{:S(2)}) collective-permute-start(bf16[800,256]{1,0:T(8,128)(2,1)S(1)} %add_convert_fusion.part_0), channel_id=1, source_target_pairs={{0,96},{16,112},{32,0},{48,16},{64,32},{80,48},{96,64},{112,80},{1... | collective-permute-start | bytes 1228808 | tf_op jit(solution)/shard_map/ppermute | solution.py:48
  161.6 17.0 %collective-permute-start.21 = (f32[5,1024]{1,0:T(8,128)S(1)}, f32[5,1024]{1,0:T(8,128)S(1)}, u32[]{:S(2)}, u32[]{:S(2)}) collective-permute-start(f32[5,1024]{1,0:T(8,128)S(1)} %add_add_fusion.2), channel_id=1, source_target_pairs={{0,64},{16,80},{32,96},{48,112},{64,0},{80,16},{96,32},{112,48},{1... | collective-permute-start | bytes 61448 | tf_op jit(solution)/shard_map/ppermute | solution.py:48
  162.8 18.5 %collective-permute-start.22 = (f32[5,1024]{1,0:T(8,128)S(1)}, f32[5,1024]{1,0:T(8,128)S(1)}, u32[]{:S(2)}, u32[]{:S(2)}) collective-permute-start(f32[5,1024]{1,0:T(8,128)S(1)} %add_add_fusion.2), channel_id=1, source_target_pairs={{0,32},{16,48},{32,64},{48,80},{64,96},{80,112},{96,0},{112,16},{1... | collective-permute-start | bytes 61448 | tf_op jit(solution)/shard_map/ppermute | solution.py:48
  182.9 13.7 %collective-permute-start.28 = (f32[5,1024]{1,0:T(8,128)S(1)}, f32[5,1024]{1,0:T(8,128)S(1)}, u32[]{:S(2)}, u32[]{:S(2)}) collective-permute-start(f32[5,1024]{1,0:T(8,128)S(1)} %add_add_fusion.1), channel_id=1, source_target_pairs={{0,8},{1,9},{2,10},{3,11},{4,12},{5,13},{6,14},{7,15},{8,0},{9,1},... | collective-permute-start | bytes 61448 | tf_op jit(solution)/shard_map/ppermute | solution.py:68
  186.3 10.3 %collective-permute-start.29 = (f32[5,1024]{1,0:T(8,128)S(1)}, f32[5,1024]{1,0:T(8,128)S(1)}, u32[]{:S(2)}, u32[]{:S(2)}) collective-permute-start(f32[5,1024]{1,0:T(8,128)S(1)} %add_add_fusion.1), channel_id=1, source_target_pairs={{0,4},{1,5},{2,6},{3,7},{4,8},{5,9},{6,10},{7,11},{8,12},{9,13},{1... | collective-permute-start | bytes 61448 | tf_op jit(solution)/shard_map/ppermute | solution.py:68
  186.9 9.7 %collective-permute-start.30 = (f32[5,1024]{1,0:T(8,128)S(1)}, f32[5,1024]{1,0:T(8,128)S(1)}, u32[]{:S(2)}, u32[]{:S(2)}) collective-permute-start(f32[5,1024]{1,0:T(8,128)S(1)} %add_add_fusion.1), channel_id=1, source_target_pairs={{0,12},{1,13},{2,14},{3,15},{4,0},{5,1},{6,2},{7,3},{8,4},{9,5},{1... | collective-permute-start | bytes 61448 | tf_op jit(solution)/shard_map/ppermute | solution.py:68
  (35 other events, 246.6 us)
